TPU v7x, 128 devices: a whole 4x4x4 slice. The times are simulated.
128 devices in a mesh: pair: 8 (over y_hi, x), virt: 8 (over y_lo, z), rep: 2 (over core).
Axes of the slice: x: 4, y: 4 (y_hi: 2, y_lo: 2; y = y_hi * 2 + y_lo), z: 4, core: 2. Of those that a mesh axis runs over, the one named last changes fastest.
Arguments:
- amplitudes: bfloat16 [8, 8, 1024, 1024], P('pair', None, None, 'virt'), may hold values from -6 to 6
- tile_mask: int32 [8, 8, 8, 8], replicated, may hold values from 0 to 1, as said below
- hole_integrals: bfloat16 [8, 1024, 8, 1024], P('pair', None, None, 'virt'), may hold values from -0.0625 to 0.0625
- virt_fock: bfloat16 [1024, 1024], P('virt'), may hold values from -0.1875 to 0.1875
- occ_energy: float32 [8], replicated, may hold values from -4 to -0.5
- virt_energy: float32 [1024], replicated, may hold values from 0.5 to 4
Outputs:
- new_amplitudes: float32 [8, 8, 1024, 1024], P('pair', None, 'rep', 'virt')
Inputs may be any that keep to these rules, and one draw needn't show every extreme that they name: `tile_mask`: entries are 0 or 1; tiles whose two virtual tile indices are equal are always 1; the share of kept tiles differs from one first occupied index to another.
All inputs are finite; a program needn't handle non-finite values.
Results may differ from a plain program's by a relative error of at most 0.0013.
Values may be sent and summed in bfloat16 or wider, within the bound.
No kernel may reach another device: no remote copies, remote signals or barrier semaphores. Data moves between devices by JAX's collectives and lax.ppermute only.
A program may use at most 128 MiB of HBM per device.

v0:
```python
import jax
import jax.numpy as jnp
from jax import lax
from jax.sharding import PartitionSpec as P

TILE = 128


def expand_tiles(flags, tile_width):
    lead_dim, second_dim, across_dim, down_dim = flags.shape
    spread = jnp.broadcast_to(
        flags[:, :, :, None, :, None],
        (lead_dim, second_dim, across_dim, tile_width, down_dim, tile_width),
    )
    return spread.reshape(lead_dim, second_dim, across_dim * tile_width, down_dim * tile_width)


def local(amplitudes, tile_mask, hole_integrals, virt_fock, occ_energy, virt_energy):
    own_rows = amplitudes.shape[0]
    occ_count = amplitudes.shape[1]
    virt_count = amplitudes.shape[2]
    virt_local = amplitudes.shape[3]
    rep_count = lax.axis_size("rep")
    half_rows = virt_count // rep_count
    pair_index = lax.axis_index("pair")
    virt_index = lax.axis_index("virt")
    rep_index = lax.axis_index("rep")
    local_tiles = virt_local // TILE
    own_flags = lax.dynamic_slice(
        tile_mask,
        (pair_index * own_rows, 0, 0, virt_index * local_tiles),
        (own_rows, occ_count, virt_count // TILE, local_tiles),
    )
    keep = expand_tiles(own_flags.astype(jnp.bfloat16), TILE)
    masked = amplitudes * keep
    row_start = rep_index * half_rows
    keep_half = lax.dynamic_slice_in_dim(keep, row_start, half_rows, 2)
    masked_half = lax.dynamic_slice_in_dim(masked, row_start, half_rows, 2)
    full_amps = lax.all_gather(masked_half, "virt", axis=3, tiled=True)
    hole_term = jnp.einsum(
        "ikac,kcjb->ijab",
        full_amps,
        lax.all_gather(hole_integrals, "pair", axis=0, tiled=True),
        preferred_element_type=jnp.float32,
    )
    fock_term = jnp.einsum(
        "ijad,bd->ijab", full_amps, virt_fock, preferred_element_type=jnp.float32
    )
    residual = keep_half.astype(jnp.float32) * (hole_term + fock_term)
    occ_own = lax.dynamic_slice_in_dim(occ_energy, pair_index * own_rows, own_rows, 0)
    virt_rows = lax.dynamic_slice_in_dim(virt_energy, row_start, half_rows, 0)
    virt_cols = lax.dynamic_slice_in_dim(virt_energy, virt_index * virt_local, virt_local, 0)
    denominator = (
        virt_rows[None, None, :, None]
        + virt_cols[None, None, None, :]
        - occ_own[:, None, None, None]
        - occ_energy[None, :, None, None]
    )
    return masked_half.astype(jnp.float32) + residual / denominator


def solution(mesh):
    return jax.shard_map(
        local,
        mesh=mesh,
        in_specs=(
            P("pair", None, None, "virt"),
            P(),
            P("pair", None, None, "virt"),
            P("virt", None),
            P(),
            P(),
        ),
        out_specs=P("pair", None, "rep", "virt"),
        check_vma=False,
    )
```

profile of v0, /device:TPU:1, one launch (start us, length us, event | category | flops | bytes accessed | tf_op | source)
XLA Modules:
  0.0 323.6 jit_solution(17220707840419048759)
XLA Ops:
  6.5 0.0 copy-start
  6.5 0.0 copy-start.2
  6.5 0.0 all-gather.3.cloned.1.call-start
  6.5 1.0 constant_dynamic-slice_fusion.1
  7.5 0.1 copy.11
  7.6 0.1 copy.8
  7.7 0.1 broadcast_bitcast_fusion
  7.8 2.6 dynamic-slice_multiply_fusion
  10.4 0.0 all-gather.3.cloned.1.call-update
  10.4 0.0 all-gather.5.cloned.1.call-start
  10.5 0.0 copy-done.2
  10.5 1.7 copy.9
  12.1 0.0 copy-start.4
  12.1 0.0 copy-start.3
  12.1 0.0 all-gather.5.cloned.1.call-update
  12.2 0.6 copy-done.4
  12.8 0.7 dynamic_slice.23
  13.5 0.0 copy-done.3
  13.5 0.1 dynamic_slice.21
  13.5 0.1 dynamic_slice.22
  13.6 1.5 add_subtract_fusion
  15.1 0.0 copy-start.1
  15.1 94.0 %all-gather.3.cloned.1.call-done = bf16[1,8,512,1024]{3,2,1,0:T(8,128)(2,1)} async-done(((bf16[1,8,512,128]{3,2,1,0:T(8,128)(2,1)}), bf16[1,8,512,1024]{3,2,1,0:T(8,128)(2,1)}) %all-gather.3.cloned.1.call-update) | async-done | bytes 8388624 | tf_op jit(solution)/shard_map/all_gather | solution.py:39
  109.2 0.0 copy-done
  109.2 5.7 %fusion.2 = f32[8,512,128]{2,1,0:T(8,128)S(1)} fusion(bf16[1,8,512,1024]{3,2,1,0:T(8,128)(2,1)} %all-gather.3.cloned.1.call-done, bf16[128,1024]{1,0:T(8,128)(2,1)S(1)} %copy-done), kind=kOutput, calls=%fused_computation.2 | convolution fusion | flops 1073741824 | bytes 10747904 | tf_op jit(solution)/shard_map/ijad,bd->ijab/dot_general | solution.py:46
  114.9 186.0 %all-gather.5.cloned.1.call-done = bf16[8,1024,8,128]{3,1,0,2:T(8,128)(2,1)} async-done(((bf16[1,1024,8,128]{3,1,0,2:T(8,128)(2,1)}), bf16[8,1024,8,128]{3,1,0,2:T(8,128)(2,1)}) %all-gather.5.cloned.1.call-update) | async-done | bytes 16777232 | tf_op jit(solution)/shard_map/all_gather | solution.py:43
  300.9 0.0 copy-done.1
  300.9 15.8 %fusion.6 = f32[1,8,512,128]{3,2,1,0:T(8,128)} fusion(f32[8,512,128]{2,1,0:T(8,128)S(1)} %fusion.2, bf16[1,8,512,128]{3,2,1,0:T(8,128)(2,1)S(1)} %copy-done.1, bf16[8,1024,8,128]{3,1,0,2:T(8,128)(2,1)} %all-gather.5.cloned.1.call-done, bf16[1,8,512,1024]{3,2,1,0:T(8,128)(2,1)} %all-gather.3.cloned.1.call-done, f32[8]{0:T(128)S(1)} %copy-done.4, ...), kind=kOutput, calls=%fused_computation.7 | convolution fusion | flops 8593080320 | bytes 30687264 | tf_op jit(solution)/shard_map/ikac,kcjb->ijab/dot_general | solution.py:40
  (2 shorter events, 0.0 us)
Async XLA Ops:
  6.5 102.6 %copy-start = (bf16[128,1024]{1,0:T(8,128)(2,1)S(1)}, bf16[128,1024]{1,0:T(8,128)(2,1)}, u32[]{:S(2)}) copy-start(bf16[128,1024]{1,0:T(8,128)(2,1)} %param.9) | copy-start | bytes 786436
  6.5 3.9 %copy-start.2 = (bf16[1,1024,8,128]{3,2,1,0:T(8,128)(2,1)S(1)}, bf16[1,1024,8,128]{3,2,1,0:T(8,128)(2,1)}, u32[]{:S(2)}) copy-start(bf16[1,1024,8,128]{3,2,1,0:T(8,128)(2,1)} %param.8) | copy-start | bytes 6291460
  6.5 102.6 %all-gather.3.cloned.1.call-start = ((), (), s32[]{:S(2)}) async-start(), calls=%async_computation | async-start | bytes 9437184 | tf_op jit(solution)/shard_map/all_gather | solution.py:39
  10.4 290.5 %all-gather.5.cloned.1.call-start = ((), (), s32[]{:S(2)}) async-start(), calls=%async_computation.1 | async-start | bytes 18874368 | tf_op jit(solution)/shard_map/all_gather | solution.py:43
  12.1 0.7 copy-start.4
  12.1 1.3 copy-start.3
  15.1 285.8 %copy-start.1 = (bf16[1,8,512,128]{3,2,1,0:T(8,128)(2,1)S(1)}, bf16[1,8,512,128]{3,2,1,0:T(8,128)(2,1)}, u32[]{:S(2)}) copy-start(bf16[1,8,512,128]{3,2,1,0:T(8,128)(2,1)} %dynamic-slice_multiply_fusion) | copy-start | bytes 3145732
Sparse Core Ops, SparseCore 0:
  10.5 98.5 all-gather.2
  111.5 189.3 all-gather.4
where the time goes:
time: 324 us
  waiting for transfers between devices  280 us (86%)
  matrix products  21.6 us (7%)
  between operations  13.4 us (4%)
  local copies, waits for them, and re-layouts  4.37 us (1%)
  other arithmetic  4.11 us (1%)
    all_gather x1, waiting for transfers between devices, local(): lax.all_gather(hole_integrals, 'pair', axis=0, tiled=True)  186 us
    all_gather x1, waiting for transfers between devices, local(): full_amps = lax.all_gather(masked_half, 'virt', axis=3, tiled=True)  94 us
    dot_general x1, matrix products, local(): jnp.einsum('ikac,kcjb->ijab', full_amps, lax.all_gather(hole_integrals, '...  15.8 us
  transfers between devices with their start and end apart: 2, of which 2 were waited for; matrix products, arithmetic and copies ran while one was open for 3% of the time, Pallas kernels for 0%

commit v1 on v0

v1 whole, which is shorter than its diff:
```python
import functools

import jax
import jax.numpy as jnp
from jax import lax
from jax.experimental import pallas as pl
from jax.experimental.pallas import tpu as pltpu
from jax.sharding import PartitionSpec as P

TILE = 128
AXES = ("pair", "virt", "rep")
X = Z = 4


def device_permutation(move):
    pairs = []
    for index in range(128):
        p, v, core = index // 16, (index // 2) % 8, index % 2
        y, x, z, core = move((p // 4) * 2 + v // 4, p % 4, v % 4, core)
        pairs.append((index, ((y // 2) * 4 + x % 4) * 16 + ((y % 2) * 4 + z % 4) * 2 + core))
    return pairs


def step_of(core):
    return 1 if core == 0 else -1


ALONG_X = device_permutation(lambda y, x, z, c: (y, x + step_of(c), z, c))
ALONG_Z = device_permutation(lambda y, x, z, c: (y, x, z + step_of(c), c))
Y_LOW = device_permutation(lambda y, x, z, c: (y ^ 1, x, z, c))
Y_HIGH = device_permutation(lambda y, x, z, c: (y ^ 2, x, z, c))
CORES = device_permutation(lambda y, x, z, c: (y, x, z, 1 - c))


def send(block, permutation):
    return lax.ppermute(block, AXES, permutation)


def partial_kernel(where, *refs):
    left, right = refs[0:8], refs[8:16]
    fock_ref, out_ref, a_all, b_all, sems = refs[16:]
    rows = out_ref.shape[1]
    core, row_start = where[0], pl.multiple_of(where[1], rows)
    copies = []
    for slot in range(8):
        copies.append(
            pltpu.make_async_copy(right[slot], b_all.at[where[10 + slot]], sems.at[slot])
        )
        copies.append(
            pltpu.make_async_copy(
                left[slot].at[:, pl.ds(row_start, rows), :],
                a_all.at[where[2 + slot]],
                sems.at[8 + slot],
            )
        )
    for copy in copies:
        copy.start()
    for copy in copies:
        copy.wait()
    block = 256

    def tile(step, carry):
        pair_j, row_block = step // (rows // block), step % (rows // block)
        row = pl.multiple_of(row_block * block, block)
        total = jnp.zeros((block, 2 * TILE), jnp.float32)
        for v in range(8):
            odd = (core + v) % 2
            lhs = jnp.concatenate([a_all[v, m, pl.ds(row, block), :] for m in range(4)], axis=1)
            rhs = jnp.concatenate(
                [
                    jnp.concatenate(
                        [b_all[2 * m + odd, v // 2, 2 * pair_j + h] for h in range(2)], axis=1
                    )
                    for m in range(4)
                ],
                axis=0,
            )
            total += jnp.dot(lhs, rhs, preferred_element_type=jnp.float32)
        for h in range(2):
            first = (core + h) % 2
            lhs = jnp.concatenate(
                [a_all[2 * t + first, pair_j, pl.ds(row, block), :] for t in range(4)], axis=1
            )
            rhs = jnp.concatenate(
                [
                    fock_ref[pl.ds(pl.multiple_of((2 * t + first) * TILE, TILE), TILE), :]
                    for t in range(4)
                ],
                axis=0,
            )
            fock = jnp.dot(lhs, rhs, preferred_element_type=jnp.float32)
            out_ref[2 * pair_j + h, pl.ds(row, block), :] = (
                total[:, h * TILE : (h + 1) * TILE] + fock
            )
        return carry

    lax.fori_loop(0, 4 * (rows // block), tile, 0)


def partial_sums(where, left, right, fock_columns, rows):
    anywhere = pl.BlockSpec(memory_space=pl.ANY)
    return pl.pallas_call(
        partial_kernel,
        out_shape=jax.ShapeDtypeStruct((8, rows, TILE), jnp.float32),
        in_specs=[pl.BlockSpec(memory_space=pltpu.SMEM)]
        + [anywhere] * 16
        + [pl.BlockSpec(memory_space=pltpu.VMEM)],
        out_specs=pl.BlockSpec(memory_space=pltpu.VMEM),
        scratch_shapes=[
            pltpu.VMEM((8, 4, rows, TILE), jnp.bfloat16),
            pltpu.VMEM((8, 4, 8, TILE, TILE), jnp.bfloat16),
            pltpu.SemaphoreType.DMA((16,)),
        ],
        compiler_params=pltpu.CompilerParams(vmem_limit_bytes=48 * 2**20),
        cost_estimate=pl.CostEstimate(
            flops=2 * rows * 1024 * 4608, bytes_accessed=24 * 2**20, transcendentals=0
        ),
        name="partial_sums",
    )(where, *left, *right, fock_columns)


def local(amplitudes, tile_mask, hole_integrals, virt_fock, occ_energy, virt_energy):
    p, v, r = (lax.axis_index(name) for name in AXES)
    rows = 512
    flags = lax.dynamic_slice(tile_mask, (p, 0, 0, v), (1, 8, 8, 1)).reshape(8, 8)
    odd = (r + v) % 2
    own_flags = lax.dynamic_index_in_dim(flags.reshape(4, 2, 8), odd, 1, keepdims=False)
    own_amps = lax.dynamic_index_in_dim(
        amplitudes.reshape(4, 2, 1024, TILE), odd, 1, keepdims=False
    )
    keep_rows = jnp.broadcast_to(own_flags[:, :, None], (4, 8, TILE)).reshape(4, 1024, 1)
    left_own = own_amps * keep_rows.astype(jnp.bfloat16)
    right_own = lax.dynamic_index_in_dim(
        hole_integrals.reshape(4, 2, TILE, 8, TILE), (r + p) % 2, 1, keepdims=False
    ).transpose(0, 2, 1, 3)

    left_far, right_far = send(left_own, Y_LOW), send(right_own, Y_HIGH)
    left, right = [left_own], [right_own]
    left_p, right_p = [left_far], [right_far]
    for _ in range(3):
        left.append(send(left[-1], ALONG_Z))
        right.append(send(right[-1], ALONG_X))
        left_p.append(send(left_p[-1], ALONG_Z))
        right_p.append(send(right_p[-1], ALONG_X))

    step = 1 - 2 * r
    near_z = [(v // 4) * 4 + (v - q * step) % 4 for q in range(4)]
    near_x = [(p // 4) * 4 + (p - q * step) % 4 for q in range(4)]
    places = near_z + [(t + 4) % 8 for t in near_z] + near_x + [(t + 4) % 8 for t in near_x]
    fock_columns = virt_fock.T

    def half(which):
        where = jnp.stack([r, which * rows] + places).astype(jnp.int32)
        return partial_sums(where, left + left_p, right + right_p, fock_columns, rows)

    other_part = half(1 - r)
    arrived = send(other_part, CORES)
    total = half(r) + arrived

    row_start = r * rows
    keep_half = jnp.broadcast_to(
        lax.dynamic_slice_in_dim(flags, r * 4, 4, 1)[:, :, None], (8, 4, TILE)
    ).reshape(1, 8, rows, 1)
    amps_half = lax.dynamic_slice_in_dim(amplitudes, row_start, rows, 2)
    masked_half = amps_half * keep_half.astype(jnp.bfloat16)
    residual = keep_half.astype(jnp.float32) * total[None]
    occ_own = lax.dynamic_slice_in_dim(occ_energy, p, 1, 0)
    virt_rows = lax.dynamic_slice_in_dim(virt_energy, row_start, rows, 0)
    virt_cols = lax.dynamic_slice_in_dim(virt_energy, v * TILE, TILE, 0)
    denominator = (
        virt_rows[None, None, :, None]
        + virt_cols[None, None, None, :]
        - occ_own[:, None, None, None]
        - occ_energy[None, :, None, None]
    )
    return masked_half.astype(jnp.float32) + residual / denominator


def solution(mesh):
    return jax.shard_map(
        local,
        mesh=mesh,
        in_specs=(
            P("pair", None, None, "virt"),
            P(),
            P("pair", None, None, "virt"),
            P("virt", None),
            P(),
            P(),
        ),
        out_specs=P("pair", None, "rep", "virt"),
        check_vma=False,
    )
```

time: 324 us -> 153 us (0.47)
  waiting for transfers between devices: 280 us -> 66.8 us
  starting transfers between devices: 0.04 us -> 43.1 us
  Pallas kernels: 0 us -> 26.4 us
  matrix products: 21.6 us -> 0 us
  between operations: 13.4 us -> 0.22 us
  local copies, waits for them, and re-layouts: 4.37 us -> 8.28 us
  other arithmetic: 4.11 us -> 7.48 us
    all_gather x2 -> x0, waiting for transfers between devices: 280 us -> none  [the longest x1 186 us: local(): lax.all_gather(hole_integrals, 'pair', axis=0, tiled=True)]
    ppermute x0 -> x15, waiting for transfers between devices: none -> 66.8 us  [send(): return lax.ppermute(block, AXES, permutation)]
    ppermute x0 -> x15, starting transfers between devices: none -> 43.1 us  [send(): return lax.ppermute(block, AXES, permutation)]
    pallas_call x0 -> x2, Pallas kernels: none -> 26.4 us  [partial_sums(): pl.pallas_call(partial_kernel, out_shape=jax.ShapeDtypeStruct((8, rows, T...]
    dot_general x2 -> x0, matrix products: 21.6 us -> none  [the longest x1 15.8 us: local(): jnp.einsum('ikac,kcjb->ijab', full_amps, lax.all_gather(hole_integrals, '...]
    add x0 -> x1, other arithmetic: none -> 4.94 us  [local(): return masked_half.astype(jnp.float32) + residual / denominator]
  transfers between devices with their start and end apart: 2 -> 15, of which waited for: 2 -> 10; matrix products, arithmetic and copies ran while one was open for 3% -> 3% of each run, Pallas kernels for 0% -> 9%
where the time goes in v1:
time: 153 us; the launch traced here: 152 us
  waiting for transfers between devices  66.8 us (44%)
  starting transfers between devices  43.1 us (28%)
  Pallas kernels  26.4 us (17%)
  local copies, waits for them, and re-layouts  8.28 us (5%)
  other arithmetic  7.48 us (5%)
    ppermute x15, waiting for transfers between devices, send(): return lax.ppermute(block, AXES, permutation)  66.8 us
    ppermute x15, starting transfers between devices, send(): return lax.ppermute(block, AXES, permutation)  43.1 us
    pallas_call x2, Pallas kernels, partial_sums(): pl.pallas_call(partial_kernel, out_shape=jax.ShapeDtypeStruct((8, rows, T...  26.4 us
    unnamed x31, local copies, waits for them, and re-layouts  5.14 us
    add x1, other arithmetic, local(): return masked_half.astype(jnp.float32) + residual / denominator  4.94 us
  transfers between devices with their start and end apart: 15, of which 10 were waited for; matrix products, arithmetic and copies ran while one was open for 3% of the time, Pallas kernels for 9%

profile of v1, /device:TPU:1, one launch (start us, length us, event | category | flops | bytes accessed | tf_op | source)
XLA Modules:
  0.0 152.2 jit_solution(7794586312713017314)
XLA Ops:
  0.0 1.0 constant_dynamic-slice_fusion.1
  1.2 1.8 %bitcast_multiply_fusion.refs_0_ = bf16[4,1024,128]{2,1,0:T(8,128)(2,1)S(1)} fusion(bf16[4,2,1024,128]{3,2,1,0:T(8,128)(2,1)} %bitcast.56, s32[]{:T(128)S(6)} %select_n.147, bf16[4,1024]{1,0:T(4,128)(2,1)S(1)} %bitcast.57), kind=kLoop, calls=%fused_computation.1 | loop fusion | flops 524288 | bytes 2105348 | tf_op jit(solution)/shard_map/mul | solution.py:132
  3.0 2.2 %collective-permute-start.3 = (bf16[4,1024,128]{2,1,0:T(8,128)(2,1)S(1)}, bf16[4,1024,128]{2,1,0:T(8,128)(2,1)}, u32[]{:S(2)}, u32[]{:S(2)}) collective-permute-start(bf16[4,1024,128]{2,1,0:T(8,128)(2,1)S(1)} %bitcast_multiply_fusion.refs_0_), channel_id=1, source_target_pairs={{0,8},{1,9},{2,10},{3,11},{4,12},{5,13},{6,14},{7,15},{8,0},{9,1},... | collective-permute-start | bytes 3145736 | tf_op jit(solution)/shard_map/ppermute | solution.py:36
  5.5 2.7 %collective-permute-start.10 = (bf16[4,8,128,128]{3,2,1,0:T(8,128)(2,1)S(1)}, bf16[4,8,128,128]{3,2,1,0:T(8,128)(2,1)S(1)}, u32[]{:S(2)}, u32[]{:S(2)}) collective-permute-start(bf16[4,8,128,128]{3,2,1,0:T(8,128)(2,1)S(1)} %bitcast.52), channel_id=1, source_target_pairs={{0,64},{1,65},{2,66},{3,67},{4,68},{5,69},{6,70},{7,71},{8,72},{9,... | collective-permute-start | bytes 3145736 | tf_op jit(solution)/shard_map/ppermute | solution.py:36
  8.2 3.8 %collective-permute-start = (bf16[4,1024,128]{2,1,0:T(8,128)(2,1)S(1)}, bf16[4,1024,128]{2,1,0:T(8,128)(2,1)S(1)}, u32[]{:S(2)}, u32[]{:S(2)}) collective-permute-start(bf16[4,1024,128]{2,1,0:T(8,128)(2,1)S(1)} %bitcast_multiply_fusion.refs_0_), channel_id=1, source_target_pairs={{0,2},{1,7},{2,4},{3,1},{4,6},{5,3},{6,0},{7,5},{8,10},{9,15},{10,... | collective-permute-start | bytes 3145736 | tf_op jit(solution)/shard_map/ppermute | solution.py:36
  12.0 2.5 %collective-permute-start.7 = (bf16[4,8,128,128]{3,2,1,0:T(8,128)(2,1)S(1)}, bf16[4,8,128,128]{3,2,1,0:T(8,128)(2,1)S(1)}, u32[]{:S(2)}, u32[]{:S(2)}) collective-permute-start(bf16[4,8,128,128]{3,2,1,0:T(8,128)(2,1)S(1)} %bitcast.53), channel_id=1, source_target_pairs={{0,16},{1,49},{2,18},{3,51},{4,20},{5,53},{6,22},{7,55},{8,24},{9,... | collective-permute-start | bytes 3145736 | tf_op jit(solution)/shard_map/ppermute | solution.py:36
  14.4 13.3 %collective-permute-done.3.refs_4_ = bf16[4,1024,128]{2,1,0:T(8,128)(2,1)} collective-permute-done((bf16[4,1024,128]{2,1,0:T(8,128)(2,1)S(1)}, bf16[4,1024,128]{2,1,0:T(8,128)(2,1)}, u32[]{:S(2)}, u32[]{:S(2)}) %collective-permute-start.3) | collective-permute-done | bytes 1048608 | tf_op jit(solution)/shard_map/ppermute | solution.py:36
  27.8 4.0 %collective-permute-start.4 = (bf16[4,1024,128]{2,1,0:T(8,128)(2,1)}, bf16[4,1024,128]{2,1,0:T(8,128)(2,1)S(1)}, u32[]{:S(2)}, u32[]{:S(2)}) collective-permute-start(bf16[4,1024,128]{2,1,0:T(8,128)(2,1)} %collective-permute-done.3.refs_4_), channel_id=1, source_target_pairs={{0,2},{1,7},{2,4},{3,1},{4,6},{5,3},{6,0},{7,5},{8,10},{9,15},{10,... | collective-permute-start | bytes 3145736 | tf_op jit(solution)/shard_map/ppermute | solution.py:36
  31.8 21.1 %collective-permute-done.10.refs_12_ = bf16[4,8,128,128]{3,2,1,0:T(8,128)(2,1)S(1)} collective-permute-done((bf16[4,8,128,128]{3,2,1,0:T(8,128)(2,1)S(1)}, bf16[4,8,128,128]{3,2,1,0:T(8,128)(2,1)S(1)}, u32[]{:S(2)}, u32[]{:S(2)}) %collective-permute-start.10) | collective-permute-done | bytes 1048608 | tf_op jit(solution)/shard_map/ppermute | solution.py:36
  52.8 2.5 %collective-permute-start.11 = (bf16[4,8,128,128]{3,2,1,0:T(8,128)(2,1)S(1)}, bf16[4,8,128,128]{3,2,1,0:T(8,128)(2,1)S(1)}, u32[]{:S(2)}, u32[]{:S(2)}) collective-permute-start(bf16[4,8,128,128]{3,2,1,0:T(8,128)(2,1)S(1)} %collective-permute-done.10.refs_12_), channel_id=1, source_target_pairs={{0,16},{1,49},{2,18},{3,51},{4,20},{5,53},{6,22},{7,55},{8,24},{9,... | collective-permute-start | bytes 3145736 | tf_op jit(solution)/shard_map/ppermute | solution.py:36
  55.3 3.8 %collective-permute-start.1 = (bf16[4,1024,128]{2,1,0:T(8,128)(2,1)S(1)}, bf16[4,1024,128]{2,1,0:T(8,128)(2,1)}, u32[]{:S(2)}, u32[]{:S(2)}) collective-permute-start(bf16[4,1024,128]{2,1,0:T(8,128)(2,1)S(1)} %collective-permute-done.refs_1_), channel_id=1, source_target_pairs={{0,2},{1,7},{2,4},{3,1},{4,6},{5,3},{6,0},{7,5},{8,10},{9,15},{10,... | collective-permute-start | bytes 3145736 | tf_op jit(solution)/shard_map/ppermute | solution.py:36
  59.1 1.0 copy-done.1
  60.7 6.3 %collective-permute-done.11.refs_13_ = bf16[4,8,128,128]{3,2,1,0:T(8,128)(2,1)S(1)} collective-permute-done((bf16[4,8,128,128]{3,2,1,0:T(8,128)(2,1)S(1)}, bf16[4,8,128,128]{3,2,1,0:T(8,128)(2,1)S(1)}, u32[]{:S(2)}, u32[]{:S(2)}) %collective-permute-start.11) | collective-permute-done | bytes 1048608 | tf_op jit(solution)/shard_map/ppermute | solution.py:36
  67.1 3.5 %collective-permute-start.12 = (bf16[4,8,128,128]{3,2,1,0:T(8,128)(2,1)S(1)}, bf16[4,8,128,128]{3,2,1,0:T(8,128)(2,1)}, u32[]{:S(2)}, u32[]{:S(2)}) collective-permute-start(bf16[4,8,128,128]{3,2,1,0:T(8,128)(2,1)S(1)} %collective-permute-done.11.refs_13_), channel_id=1, source_target_pairs={{0,16},{1,49},{2,18},{3,51},{4,20},{5,53},{6,22},{7,55},{8,24},{9,... | collective-permute-start | bytes 3145736 | tf_op jit(solution)/shard_map/ppermute | solution.py:36
  70.8 3.5 %collective-permute-start.2 = (bf16[4,1024,128]{2,1,0:T(8,128)(2,1)}, bf16[4,1024,128]{2,1,0:T(8,128)(2,1)}, u32[]{:S(2)}, u32[]{:S(2)}) collective-permute-start(bf16[4,1024,128]{2,1,0:T(8,128)(2,1)} %collective-permute-done.1.refs_2_), channel_id=1, source_target_pairs={{0,2},{1,7},{2,4},{3,1},{4,6},{5,3},{6,0},{7,5},{8,10},{9,15},{10,... | collective-permute-start | bytes 3145736 | tf_op jit(solution)/shard_map/ppermute | solution.py:36
  74.3 4.0 %collective-permute-done.8.refs_10_ = bf16[4,8,128,128]{3,2,1,0:T(8,128)(2,1)} collective-permute-done((bf16[4,8,128,128]{3,2,1,0:T(8,128)(2,1)S(1)}, bf16[4,8,128,128]{3,2,1,0:T(8,128)(2,1)}, u32[]{:S(2)}, u32[]{:S(2)}) %collective-permute-start.8) | collective-permute-done | bytes 1048608 | tf_op jit(solution)/shard_map/ppermute | solution.py:36
  78.3 3.5 %collective-permute-start.9 = (bf16[4,8,128,128]{3,2,1,0:T(8,128)(2,1)}, bf16[4,8,128,128]{3,2,1,0:T(8,128)(2,1)}, u32[]{:S(2)}, u32[]{:S(2)}) collective-permute-start(bf16[4,8,128,128]{3,2,1,0:T(8,128)(2,1)} %collective-permute-done.8.refs_10_), channel_id=1, source_target_pairs={{0,16},{1,49},{2,18},{3,51},{4,20},{5,53},{6,22},{7,55},{8,24},{9,... | collective-permute-start | bytes 3145736 | tf_op jit(solution)/shard_map/ppermute | solution.py:36
  82.1 3.5 %collective-permute-start.6 = (bf16[4,1024,128]{2,1,0:T(8,128)(2,1)}, bf16[4,1024,128]{2,1,0:T(8,128)(2,1)}, u32[]{:S(2)}, u32[]{:S(2)}) collective-permute-start(bf16[4,1024,128]{2,1,0:T(8,128)(2,1)} %collective-permute-done.5.refs_6_), channel_id=1, source_target_pairs={{0,2},{1,7},{2,4},{3,1},{4,6},{5,3},{6,0},{7,5},{8,10},{9,15},{10,... | collective-permute-start | bytes 3145736 | tf_op jit(solution)/shard_map/ppermute | solution.py:36
  85.6 4.0 %collective-permute-done.12.refs_14_ = bf16[4,8,128,128]{3,2,1,0:T(8,128)(2,1)} collective-permute-done((bf16[4,8,128,128]{3,2,1,0:T(8,128)(2,1)S(1)}, bf16[4,8,128,128]{3,2,1,0:T(8,128)(2,1)}, u32[]{:S(2)}, u32[]{:S(2)}) %collective-permute-start.12) | collective-permute-done | bytes 1048608 | tf_op jit(solution)/shard_map/ppermute | solution.py:36
  89.5 3.5 %collective-permute-start.13 = (bf16[4,8,128,128]{3,2,1,0:T(8,128)(2,1)}, bf16[4,8,128,128]{3,2,1,0:T(8,128)(2,1)}, u32[]{:S(2)}, u32[]{:S(2)}) collective-permute-start(bf16[4,8,128,128]{3,2,1,0:T(8,128)(2,1)} %collective-permute-done.12.refs_14_), channel_id=1, source_target_pairs={{0,16},{1,49},{2,18},{3,51},{4,20},{5,53},{6,22},{7,55},{8,24},{9,... | collective-permute-start | bytes 3145736 | tf_op jit(solution)/shard_map/ppermute | solution.py:36
  93.0 1.1 copy.25
  94.4 6.5 %collective-permute-done.9.refs_11_ = bf16[4,8,128,128]{3,2,1,0:T(8,128)(2,1)} collective-permute-done((bf16[4,8,128,128]{3,2,1,0:T(8,128)(2,1)}, bf16[4,8,128,128]{3,2,1,0:T(8,128)(2,1)}, u32[]{:S(2)}, u32[]{:S(2)}) %collective-permute-start.9) | collective-permute-done | bytes 1048608 | tf_op jit(solution)/shard_map/ppermute | solution.py:36
  100.9 3.8 %collective-permute-done.6.refs_7_ = bf16[4,1024,128]{2,1,0:T(8,128)(2,1)} collective-permute-done((bf16[4,1024,128]{2,1,0:T(8,128)(2,1)}, bf16[4,1024,128]{2,1,0:T(8,128)(2,1)}, u32[]{:S(2)}, u32[]{:S(2)}) %collective-permute-start.6) | collective-permute-done | bytes 1048608 | tf_op jit(solution)/shard_map/ppermute | solution.py:36
  104.6 7.5 %collective-permute-done.13.refs_15_ = bf16[4,8,128,128]{3,2,1,0:T(8,128)(2,1)} collective-permute-done((bf16[4,8,128,128]{3,2,1,0:T(8,128)(2,1)}, bf16[4,8,128,128]{3,2,1,0:T(8,128)(2,1)}, u32[]{:S(2)}, u32[]{:S(2)}) %collective-permute-start.13) | collective-permute-done | bytes 1048608 | tf_op jit(solution)/shard_map/ppermute | solution.py:36
  112.1 1.2 copy-done.2
  113.3 13.2 %partial_sums.3 = f32[8,512,128]{2,1,0:T(8,128)} custom-call(s32[18]{0:T(128)S(1)} %stack.100.where, bf16[4,1024,128]{2,1,0:T(8,128)(2,1)S(1)} %bitcast_multiply_fusion.refs_0_, bf16[4,1024,128]{2,1,0:T(8,128)(2,1)S(1)} %copy-done.2, bf16[4,1024,128]{2,1,0:T(8,128)(2,1)} %collective-permute-done.1.refs_2_, ...), custom_call_target="tpu_custom_call" | custom-call | flops 4831838208 | bytes 25165824 | tf_op jit(solution)/shard_map/partial_sums/pallas_call | solution.py:102
  126.5 3.4 %collective-permute-start.14 = (f32[8,512,128]{2,1,0:T(8,128)}, f32[8,512,128]{2,1,0:T(8,128)}, u32[]{:S(2)}, u32[]{:S(2)}) collective-permute-start(f32[8,512,128]{2,1,0:T(8,128)} %partial_sums.3), channel_id=1, source_target_pairs={{0,1},{1,0},{2,3},{3,2},{4,5},{5,4},{6,7},{7,6},{8,9},{9,8},{10,11... | collective-permute-start | bytes 6291464 | tf_op jit(solution)/shard_map/ppermute | solution.py:36
  130.8 0.8 constant_dynamic-slice_fusion.2
  132.1 0.8 add_subtract_fusion
  132.8 1.2 copy-done.3
  134.1 13.2 %partial_sums.2 = f32[8,512,128]{2,1,0:T(8,128)} custom-call(s32[18]{0:T(128)S(1)} %stack.98.where, bf16[4,1024,128]{2,1,0:T(8,128)(2,1)S(1)} %bitcast_multiply_fusion.refs_0_, bf16[4,1024,128]{2,1,0:T(8,128)(2,1)S(1)} %copy-done.3, bf16[4,1024,128]{2,1,0:T(8,128)(2,1)} %collective-permute-done.1.refs_2_, ...), custom_call_target="tpu_custom_call" | custom-call | flops 4831838208 | bytes 25165824 | tf_op jit(solution)/shard_map/partial_sums/pallas_call | solution.py:102
  147.3 4.9 %bitcast_add_fusion = f32[1,8,512,128]{3,2,1,0:T(8,128)} fusion(f32[8,512,128]{2,1,0:T(8,128)} %partial_sums.2, f32[8,512,128]{2,1,0:T(8,128)} %collective-permute-done.14, f32[8]{0:T(128)S(1)} %copy-done.11, f32[512,128]{1,0:T(8,128)S(1)} %add_subtract_fusion, f32[8,512]{1,0:T(8,128)S(1)} %broadcast_bitcast_fusion, bf16[1,8,1024,128]{3,2,1,0:T(8,128)(2,1)S(1)} %copy-done.9, ...), kind=kLoop, calls=%fused_computation | loop fusion | flops 4718592 | bytes 7626788 | tf_op jit(solution)/shard_map/add | solution.py:176
  (48 shorter events, 3.1 us)
Async XLA Ops:
  0.0 5.2 %copy-start = (bf16[1,1024,8,128]{3,2,1,0:T(8,128)(2,1)S(1)}, bf16[1,1024,8,128]{3,2,1,0:T(8,128)(2,1)}, u32[]{:S(2)}) copy-start(bf16[1,1024,8,128]{3,2,1,0:T(8,128)(2,1)} %param.8) | copy-start | bytes 6291460
  3.0 24.8 %collective-permute-start.3 = (bf16[4,1024,128]{2,1,0:T(8,128)(2,1)S(1)}, bf16[4,1024,128]{2,1,0:T(8,128)(2,1)}, u32[]{:S(2)}, u32[]{:S(2)}) collective-permute-start(bf16[4,1024,128]{2,1,0:T(8,128)(2,1)S(1)} %bitcast_multiply_fusion.refs_0_), channel_id=1, source_target_pairs={{0,8},{1,9},{2,10},{3,11},{4,12},{5,13},{6,14},{7,15},{8,0},{9,1},... | collective-permute-start | bytes 3145736 | tf_op jit(solution)/shard_map/ppermute | solution.py:36
  5.5 65.3 %copy-start.4 = (bf16[4,1,128,8,128]{4,2,3,0,1:T(8,128)(2,1)}, bf16[4,1,128,8,128]{4,2,3,0,1:T(8,128)(2,1)S(1)}, u32[]{:S(2)}) copy-start(bf16[4,1,128,8,128]{4,2,3,0,1:T(8,128)(2,1)S(1)} %copy.35) | copy-start | bytes 3145732
  5.5 47.3 %collective-permute-start.10 = (bf16[4,8,128,128]{3,2,1,0:T(8,128)(2,1)S(1)}, bf16[4,8,128,128]{3,2,1,0:T(8,128)(2,1)S(1)}, u32[]{:S(2)}, u32[]{:S(2)}) collective-permute-start(bf16[4,8,128,128]{3,2,1,0:T(8,128)(2,1)S(1)} %bitcast.52), channel_id=1, source_target_pairs={{0,64},{1,65},{2,66},{3,67},{4,68},{5,69},{6,70},{7,71},{8,72},{9,... | collective-permute-start | bytes 3145736 | tf_op jit(solution)/shard_map/ppermute | solution.py:36
  8.2 47.1 %collective-permute-start = (bf16[4,1024,128]{2,1,0:T(8,128)(2,1)S(1)}, bf16[4,1024,128]{2,1,0:T(8,128)(2,1)S(1)}, u32[]{:S(2)}, u32[]{:S(2)}) collective-permute-start(bf16[4,1024,128]{2,1,0:T(8,128)(2,1)S(1)} %bitcast_multiply_fusion.refs_0_), channel_id=1, source_target_pairs={{0,2},{1,7},{2,4},{3,1},{4,6},{5,3},{6,0},{7,5},{8,10},{9,15},{10,... | collective-permute-start | bytes 3145736 | tf_op jit(solution)/shard_map/ppermute | solution.py:36
  12.0 48.1 %collective-permute-start.7 = (bf16[4,8,128,128]{3,2,1,0:T(8,128)(2,1)S(1)}, bf16[4,8,128,128]{3,2,1,0:T(8,128)(2,1)S(1)}, u32[]{:S(2)}, u32[]{:S(2)}) collective-permute-start(bf16[4,8,128,128]{3,2,1,0:T(8,128)(2,1)S(1)} %bitcast.53), channel_id=1, source_target_pairs={{0,16},{1,49},{2,18},{3,51},{4,20},{5,53},{6,22},{7,55},{8,24},{9,... | collective-permute-start | bytes 3145736 | tf_op jit(solution)/shard_map/ppermute | solution.py:36
  27.8 32.8 %collective-permute-start.4 = (bf16[4,1024,128]{2,1,0:T(8,128)(2,1)}, bf16[4,1024,128]{2,1,0:T(8,128)(2,1)S(1)}, u32[]{:S(2)}, u32[]{:S(2)}) collective-permute-start(bf16[4,1024,128]{2,1,0:T(8,128)(2,1)} %collective-permute-done.3.refs_4_), channel_id=1, source_target_pairs={{0,2},{1,7},{2,4},{3,1},{4,6},{5,3},{6,0},{7,5},{8,10},{9,15},{10,... | collective-permute-start | bytes 3145736 | tf_op jit(solution)/shard_map/ppermute | solution.py:36
  52.8 21.5 %copy-start.5 = (bf16[4,8,128,128]{3,2,1,0:T(8,128)(2,1)}, bf16[4,8,128,128]{3,2,1,0:T(8,128)(2,1)S(1)}, u32[]{:S(2)}) copy-start(bf16[4,8,128,128]{3,2,1,0:T(8,128)(2,1)S(1)} %collective-permute-done.10.refs_12_) | copy-start | bytes 3145732
  52.8 14.2 %collective-permute-start.11 = (bf16[4,8,128,128]{3,2,1,0:T(8,128)(2,1)S(1)}, bf16[4,8,128,128]{3,2,1,0:T(8,128)(2,1)S(1)}, u32[]{:S(2)}, u32[]{:S(2)}) collective-permute-start(bf16[4,8,128,128]{3,2,1,0:T(8,128)(2,1)S(1)} %collective-permute-done.10.refs_12_), channel_id=1, source_target_pairs={{0,16},{1,49},{2,18},{3,51},{4,20},{5,53},{6,22},{7,55},{8,24},{9,... | collective-permute-start | bytes 3145736 | tf_op jit(solution)/shard_map/ppermute | solution.py:36
  55.3 15.5 %collective-permute-start.1 = (bf16[4,1024,128]{2,1,0:T(8,128)(2,1)S(1)}, bf16[4,1024,128]{2,1,0:T(8,128)(2,1)}, u32[]{:S(2)}, u32[]{:S(2)}) collective-permute-start(bf16[4,1024,128]{2,1,0:T(8,128)(2,1)S(1)} %collective-permute-done.refs_1_), channel_id=1, source_target_pairs={{0,2},{1,7},{2,4},{3,1},{4,6},{5,3},{6,0},{7,5},{8,10},{9,15},{10,... | collective-permute-start | bytes 3145736 | tf_op jit(solution)/shard_map/ppermute | solution.py:36
  59.1 1.0 copy-start.1
  60.1 18.2 %copy-start.6 = (bf16[4,8,128,128]{3,2,1,0:T(8,128)(2,1)}, bf16[4,8,128,128]{3,2,1,0:T(8,128)(2,1)S(1)}, u32[]{:S(2)}) copy-start(bf16[4,8,128,128]{3,2,1,0:T(8,128)(2,1)S(1)} %collective-permute-done.7.refs_9_) | copy-start | bytes 3145732
  60.1 18.2 %collective-permute-start.8 = (bf16[4,8,128,128]{3,2,1,0:T(8,128)(2,1)S(1)}, bf16[4,8,128,128]{3,2,1,0:T(8,128)(2,1)}, u32[]{:S(2)}, u32[]{:S(2)}) collective-permute-start(bf16[4,8,128,128]{3,2,1,0:T(8,128)(2,1)S(1)} %collective-permute-done.7.refs_9_), channel_id=1, source_target_pairs={{0,16},{1,49},{2,18},{3,51},{4,20},{5,53},{6,22},{7,55},{8,24},{9,... | collective-permute-start | bytes 3145736 | tf_op jit(solution)/shard_map/ppermute | solution.py:36
  60.6 21.2 %copy-start.7 = (bf16[4,1024,128]{2,1,0:T(8,128)(2,1)}, bf16[4,1024,128]{2,1,0:T(8,128)(2,1)S(1)}, u32[]{:S(2)}) copy-start(bf16[4,1024,128]{2,1,0:T(8,128)(2,1)S(1)} %collective-permute-done.4.refs_5_) | copy-start | bytes 3145732
  60.6 21.4 %collective-permute-start.5 = (bf16[4,1024,128]{2,1,0:T(8,128)(2,1)S(1)}, bf16[4,1024,128]{2,1,0:T(8,128)(2,1)}, u32[]{:S(2)}, u32[]{:S(2)}) collective-permute-start(bf16[4,1024,128]{2,1,0:T(8,128)(2,1)S(1)} %collective-permute-done.4.refs_5_), channel_id=1, source_target_pairs={{0,2},{1,7},{2,4},{3,1},{4,6},{5,3},{6,0},{7,5},{8,10},{9,15},{10,... | collective-permute-start | bytes 3145736 | tf_op jit(solution)/shard_map/ppermute | solution.py:36
  67.1 15.0 %copy-start.8 = (bf16[4,8,128,128]{3,2,1,0:T(8,128)(2,1)}, bf16[4,8,128,128]{3,2,1,0:T(8,128)(2,1)S(1)}, u32[]{:S(2)}) copy-start(bf16[4,8,128,128]{3,2,1,0:T(8,128)(2,1)S(1)} %collective-permute-done.11.refs_13_) | copy-start | bytes 3145732
  67.1 22.5 %collective-permute-start.12 = (bf16[4,8,128,128]{3,2,1,0:T(8,128)(2,1)S(1)}, bf16[4,8,128,128]{3,2,1,0:T(8,128)(2,1)}, u32[]{:S(2)}, u32[]{:S(2)}) collective-permute-start(bf16[4,8,128,128]{3,2,1,0:T(8,128)(2,1)S(1)} %collective-permute-done.11.refs_13_), channel_id=1, source_target_pairs={{0,16},{1,49},{2,18},{3,51},{4,20},{5,53},{6,22},{7,55},{8,24},{9,... | collective-permute-start | bytes 3145736 | tf_op jit(solution)/shard_map/ppermute | solution.py:36
  70.8 23.5 %collective-permute-start.2 = (bf16[4,1024,128]{2,1,0:T(8,128)(2,1)}, bf16[4,1024,128]{2,1,0:T(8,128)(2,1)}, u32[]{:S(2)}, u32[]{:S(2)}) collective-permute-start(bf16[4,1024,128]{2,1,0:T(8,128)(2,1)} %collective-permute-done.1.refs_2_), channel_id=1, source_target_pairs={{0,2},{1,7},{2,4},{3,1},{4,6},{5,3},{6,0},{7,5},{8,10},{9,15},{10,... | collective-permute-start | bytes 3145736 | tf_op jit(solution)/shard_map/ppermute | solution.py:36
  78.3 22.6 %collective-permute-start.9 = (bf16[4,8,128,128]{3,2,1,0:T(8,128)(2,1)}, bf16[4,8,128,128]{3,2,1,0:T(8,128)(2,1)}, u32[]{:S(2)}, u32[]{:S(2)}) collective-permute-start(bf16[4,8,128,128]{3,2,1,0:T(8,128)(2,1)} %collective-permute-done.8.refs_10_), channel_id=1, source_target_pairs={{0,16},{1,49},{2,18},{3,51},{4,20},{5,53},{6,22},{7,55},{8,24},{9,... | collective-permute-start | bytes 3145736 | tf_op jit(solution)/shard_map/ppermute | solution.py:36
  82.1 22.6 %collective-permute-start.6 = (bf16[4,1024,128]{2,1,0:T(8,128)(2,1)}, bf16[4,1024,128]{2,1,0:T(8,128)(2,1)}, u32[]{:S(2)}, u32[]{:S(2)}) collective-permute-start(bf16[4,1024,128]{2,1,0:T(8,128)(2,1)} %collective-permute-done.5.refs_6_), channel_id=1, source_target_pairs={{0,2},{1,7},{2,4},{3,1},{4,6},{5,3},{6,0},{7,5},{8,10},{9,15},{10,... | collective-permute-start | bytes 3145736 | tf_op jit(solution)/shard_map/ppermute | solution.py:36
  89.5 22.6 %collective-permute-start.13 = (bf16[4,8,128,128]{3,2,1,0:T(8,128)(2,1)}, bf16[4,8,128,128]{3,2,1,0:T(8,128)(2,1)}, u32[]{:S(2)}, u32[]{:S(2)}) collective-permute-start(bf16[4,8,128,128]{3,2,1,0:T(8,128)(2,1)} %collective-permute-done.12.refs_14_), channel_id=1, source_target_pairs={{0,16},{1,49},{2,18},{3,51},{4,20},{5,53},{6,22},{7,55},{8,24},{9,... | collective-permute-start | bytes 3145736 | tf_op jit(solution)/shard_map/ppermute | solution.py:36
  112.1 1.2 copy-start.2
  113.3 16.7 %copy-start.11 = (f32[8]{0:T(128)S(1)}, f32[8]{0:T(128)}, u32[]{:S(2)}) copy-start(f32[8]{0:T(128)} %param.10) | copy-start | bytes 100
  113.3 17.3 %copy-start.10 = (f32[1024]{0:T(1024)S(1)}, f32[1024]{0:T(1024)}, u32[]{:S(2)}) copy-start(f32[1024]{0:T(1024)} %param.11) | copy-start | bytes 12292
  126.5 20.8 %collective-permute-start.14 = (f32[8,512,128]{2,1,0:T(8,128)}, f32[8,512,128]{2,1,0:T(8,128)}, u32[]{:S(2)}, u32[]{:S(2)}) collective-permute-start(f32[8,512,128]{2,1,0:T(8,128)} %partial_sums.3), channel_id=1, source_target_pairs={{0,1},{1,0},{2,3},{3,2},{4,5},{5,4},{6,7},{7,6},{8,9},{9,8},{10,11... | collective-permute-start | bytes 6291464 | tf_op jit(solution)/shard_map/ppermute | solution.py:36
  132.8 1.2 copy-start.3
  134.1 13.2 %copy-start.9 = (bf16[1,8,1024,128]{3,2,1,0:T(8,128)(2,1)S(1)}, bf16[1,8,1024,128]{3,2,1,0:T(8,128)(2,1)}, u32[]{:S(2)}) copy-start(bf16[1,8,1024,128]{3,2,1,0:T(8,128)(2,1)} %param.6) | copy-start | bytes 6291460

commit v2 on v0

v2 whole, which is shorter than its diff:
```python
import functools

import jax
import jax.numpy as jnp
from jax import lax
from jax.experimental import pallas as pl
from jax.experimental.pallas import tpu as pltpu
from jax.sharding import PartitionSpec as P

TILE = 128
AXES = ("pair", "virt", "rep")


def device_permutation(move):
    pairs = []
    for index in range(128):
        p, v, core = index // 16, (index // 2) % 8, index % 2
        y, x, z, core = move((p // 4) * 2 + v // 4, p % 4, v % 4, core)
        pairs.append((index, ((y // 2) * 4 + x % 4) * 16 + ((y % 2) * 4 + z % 4) * 2 + core))
    return pairs


def step_of(core):
    return 1 if core == 0 else -1


ALONG_X = device_permutation(lambda y, x, z, c: (y, x + step_of(c), z, c))
ALONG_Z = device_permutation(lambda y, x, z, c: (y, x, z + step_of(c), c))
Y_LOW = device_permutation(lambda y, x, z, c: (y ^ 1, x, z, c))
Y_HIGH = device_permutation(lambda y, x, z, c: (y ^ 2, x, z, c))
CORES = device_permutation(lambda y, x, z, c: (y, x, z, 1 - c))


def send(block, permutation):
    return lax.ppermute(block, AXES, permutation)


def gate_kernel(*refs):
    pass


def gate(passed, after):
    anywhere = pl.BlockSpec(memory_space=pl.ANY)
    return pl.pallas_call(
        gate_kernel,
        out_shape=[jax.ShapeDtypeStruct(x.shape, x.dtype) for x in passed],
        in_specs=[anywhere] * (len(passed) + len(after)),
        out_specs=[anywhere] * len(passed),
        input_output_aliases={i: i for i in range(len(passed))},
        name="gate",
    )(*passed, *after)


def assemble(where, left, right, near, full, a_all, b_all, sems):
    p, v, core = where[0], where[1], where[2]
    step = 1 - 2 * core
    low = v // 4 if near[0] else 1 - v // 4
    high = p // 4 if near[1] else 1 - p // 4
    left_start = 2 * high if full[0] else 0
    right_start = pl.multiple_of(256 * low, 256) if full[1] else 0
    copies = []
    for q in range(4):
        x = (p + 4 - q * step) % 4
        copies.append(
            pltpu.make_async_copy(
                right[q].at[pl.ds(right_start, 256), :],
                b_all.at[pl.ds(pl.multiple_of(x * 256, 256), 256), :],
                sems.at[q],
            )
        )
        z = (v + 4 - q * step) % 4
        for m in range(2):
            x = 2 * m + (core + z) % 2
            copies.append(
                pltpu.make_async_copy(
                    left[q].at[left_start + m],
                    a_all.at[:, pl.ds(pl.multiple_of((2 * x + z // 2) * TILE, TILE), TILE)],
                    sems.at[4 + 2 * q + m],
                )
            )
    for copy in copies:
        copy.start()
    for copy in copies:
        copy.wait()


def multiply(where, near, fock_ref, acc_ref, out_ref, a_all, b_all, row_start):
    p, v, core = where[0], where[1], where[2]
    low = v // 4 if near[0] else 1 - v // 4
    high = p // 4 if near[1] else 1 - p // 4
    rows, width, block = out_ref.shape[0], 256, 512

    def columns_of(step, carry):
        columns = pl.ds(pl.multiple_of(step * width, width), width)
        for row in range(0, rows, block):
            part = pl.ds(row, block)
            source = pl.ds(row_start + row, block)
            total = jnp.dot(a_all[source, :], b_all[:, columns], preferred_element_type=jnp.float32)
            if acc_ref is not None:
                total += acc_ref[source, columns]
            out_ref[part, columns] = total
        return carry

    lax.fori_loop(0, 1024 // width, columns_of, 0)
    for x in range(4):
        fock = jnp.concatenate(
            [
                fock_ref[
                    pl.ds(pl.multiple_of((4 * low + 2 * t + (x + core) % 2) * TILE, TILE), TILE), :
                ]
                for t in range(2)
            ],
            axis=0,
        )
        columns = pl.ds(pl.multiple_of((4 * high + x) * TILE, TILE), TILE)
        for row in range(0, rows, block):
            out_ref[pl.ds(row, block), columns] += jnp.dot(
                a_all[pl.ds(row_start + row, block), x * 256 : (x + 1) * 256],
                fock,
                preferred_element_type=jnp.float32,
            )


def quarter_kernel(start_from, near, full, where, *refs):
    left, right, fock_ref = refs[0:4], refs[4:8], refs[8]
    refs = refs[9:]
    acc_ref = None
    if start_from:
        acc_ref, refs = refs[0], refs[1:]
    out_ref, a_all, b_all, sems = refs
    assemble(where, left, right, near, full, a_all, b_all, sems)
    multiply(where, near, fock_ref, acc_ref, out_ref, a_all, b_all, 0)


def last_kernel(near, full, where, *refs):
    left, right = refs[0:4], refs[4:8]
    fock_ref, acc_ref, out_ref, a_all, b_all, sems = refs[8:]
    assemble(where, left, right, near, full, a_all, b_all, sems)
    row_start = pl.multiple_of((1 - where[2]) * 512, 512)
    multiply(where, near, fock_ref, acc_ref, out_ref, a_all, b_all, row_start)


def rest_kernel(near, where, a_all, b_all, fock_ref, acc_ref, out_ref):
    row_start = pl.multiple_of(where[2] * 512, 512)
    multiply(where, near, fock_ref, acc_ref, out_ref, a_all, b_all, row_start)


ANYWHERE = pl.BlockSpec(memory_space=pl.ANY)
VMEM = pl.BlockSpec(memory_space=pltpu.VMEM)
SMEM = pl.BlockSpec(memory_space=pltpu.SMEM)
LIMIT = pltpu.CompilerParams(vmem_limit_bytes=32 * 2**20)


def cost(rows):
    return pl.CostEstimate(
        flops=2 * rows * 1024 * 1280, bytes_accessed=8 * 2**20, transcendentals=0
    )


def add_quarter(acc, where, left, right, fock_columns, near, full):
    start_from = acc is not None
    return pl.pallas_call(
        functools.partial(quarter_kernel, start_from, near, full),
        in_specs=[SMEM] + [ANYWHERE] * 8 + [VMEM] * (1 + start_from),
        out_specs=VMEM,
        scratch_shapes=[
            pltpu.VMEM((1024, 1024), jnp.bfloat16),
            pltpu.VMEM((1024, 1024), jnp.bfloat16),
            pltpu.SemaphoreType.DMA((12,)),
        ],
        out_shape=jax.ShapeDtypeStruct((1024, 1024), jnp.float32),
        input_output_aliases={10: 0} if start_from else {},
        compiler_params=LIMIT,
        cost_estimate=cost(1024),
        name="add_quarter",
    )(where, *left, *right, fock_columns, *([acc] * start_from))


def last_quarter(acc, where, left, right, fock_columns, near, full):
    return pl.pallas_call(
        functools.partial(last_kernel, near, full),
        in_specs=[SMEM] + [ANYWHERE] * 8 + [VMEM] * 2,
        out_specs=[VMEM] * 3,
        scratch_shapes=[pltpu.SemaphoreType.DMA((12,))],
        out_shape=[
            jax.ShapeDtypeStruct((512, 1024), jnp.float32),
            jax.ShapeDtypeStruct((1024, 1024), jnp.bfloat16),
            jax.ShapeDtypeStruct((1024, 1024), jnp.bfloat16),
        ],
        compiler_params=LIMIT,
        cost_estimate=cost(512),
        name="last_quarter",
    )(where, *left, *right, fock_columns, acc)


def rest_of_quarter(acc, where, a_all, b_all, fock_columns, near):
    return pl.pallas_call(
        functools.partial(rest_kernel, near),
        in_specs=[SMEM] + [VMEM] * 4,
        out_specs=VMEM,
        out_shape=jax.ShapeDtypeStruct((512, 1024), jnp.float32),
        compiler_params=LIMIT,
        cost_estimate=cost(512),
        name="rest_of_quarter",
    )(where, a_all, b_all, fock_columns, acc)


def update_kernel(where, flags_ref, occ_ref, virt_ref, own_ref, other_ref, amps_ref, out_ref, amps, new, sems):
    p, v, core = where[0], where[1], where[2]
    row_start = pl.multiple_of(core * 512, 512)
    load = pltpu.make_async_copy(amps_ref.at[0, :, pl.ds(row_start, 512), :], amps, sems.at[8])
    load.start()
    across = jnp.transpose(virt_ref[...])
    rows = [jnp.where(core == 0, across[:, t : t + 1], across[:, t + 4 : t + 5]) for t in range(4)]
    base = virt_ref[pl.ds(v, 1), :] - occ_ref[p]
    sums = [jnp.broadcast_to(row, (TILE, TILE)) + base for row in rows]
    load.wait()
    stores = []
    for j in range(8):
        for t in range(4):
            part = slice(t * TILE, (t + 1) * TILE)
            columns = slice(j * TILE, (j + 1) * TILE)
            keep = flags_ref[j, 4 * core + t].astype(jnp.float32)
            masked = amps[j, part, :].astype(jnp.float32) * keep
            residual = keep * (own_ref[part, columns] + other_ref[part, columns])
            new[j, part, :] = masked + residual / (sums[t] - occ_ref[j])
        store = pltpu.make_async_copy(new.at[j], out_ref.at[0, j], sems.at[j])
        store.start()
        stores.append(store)
    for store in stores:
        store.wait()


def update(where, flags, occ_energy, virt_energy, own_part, arrived, amplitudes):
    return pl.pallas_call(
        update_kernel,
        in_specs=[SMEM, SMEM, SMEM, VMEM, VMEM, VMEM, ANYWHERE],
        out_specs=ANYWHERE,
        out_shape=jax.ShapeDtypeStruct((1, 8, 512, TILE), jnp.float32),
        scratch_shapes=[
            pltpu.VMEM((8, 512, TILE), jnp.bfloat16),
            pltpu.VMEM((8, 512, TILE), jnp.float32),
            pltpu.SemaphoreType.DMA((9,)),
        ],
        compiler_params=LIMIT,
        name="update",
    )(where, flags, occ_energy, virt_energy, own_part, arrived, amplitudes)


def local(amplitudes, tile_mask, hole_integrals, virt_fock, occ_energy, virt_energy):
    p, v, r = (lax.axis_index(name) for name in AXES)
    rows = 512
    flags = lax.dynamic_slice(tile_mask, (p, 0, 0, v), (1, 8, 8, 1)).reshape(8, 8)
    odd = (r + v) % 2
    own_flags = lax.dynamic_index_in_dim(flags.reshape(4, 2, 8), odd, 1, keepdims=False)
    own_amps = lax.dynamic_index_in_dim(
        amplitudes.reshape(4, 2, 1024, TILE), odd, 1, keepdims=False
    )
    keep_rows = jnp.broadcast_to(own_flags[:, :, None], (4, 8, TILE)).reshape(4, 1024, 1)
    left_own = own_amps * keep_rows.astype(jnp.bfloat16)
    right_own = lax.dynamic_index_in_dim(
        hole_integrals.reshape(4, 2, TILE, 8, TILE), (r + p) % 2, 1, keepdims=False
    ).reshape(512, 1024)

    low, high = v // 4, p // 4

    def part_of(block, start, size):
        return lax.dynamic_slice_in_dim(block, start, size, 0)

    where = jnp.stack([p, v, r]).astype(jnp.int32)
    fock_columns = virt_fock.T

    left, right = [left_own], [right_own]
    right_a = [send(part_of(right_own, 256 * low, 256), Y_HIGH)]
    right.append(send(right[-1], ALONG_X))
    left.append(send(left[-1], ALONG_Z))
    right_a[0], left_a = gate([right_a[0], part_of(left_own, 2 * high, 2)], [left[1], right[1]])
    left_a = [send(left_a, Y_LOW)]
    for _ in range(2):
        right.append(send(right[-1], ALONG_X))
        left.append(send(left[-1], ALONG_Z))
    left_a[0], left_b = gate([left_a[0], part_of(left_own, 2 - 2 * high, 2)], [])
    left_b = [send(left_b, Y_LOW)]
    left_b[0], right_b = gate(
        [left_b[0], part_of(right_own, 256 - 256 * low, 256)], [left[2], right[2]]
    )
    right_b = [send(right_b, Y_HIGH)]
    for _ in range(3):
        for block in (left_a, left_b):
            block.append(send(block[-1], ALONG_Z))
        for block in (right_a, right_b):
            block.append(send(block[-1], ALONG_X))

    acc = add_quarter(None, where, left, right, fock_columns, (1, 1), (1, 1))
    acc = add_quarter(acc, where, left, right_a, fock_columns, (1, 0), (1, 0))
    acc = add_quarter(acc, where, left_a, right, fock_columns, (0, 1), (0, 1))
    far, small = (0, 0), (0, 0)
    other_part, a_all, b_all = last_quarter(acc, where, left_b, right_b, fock_columns, far, small)
    arrived = send(other_part, CORES)
    own_part = rest_of_quarter(acc, where, a_all, b_all, fock_columns, far)
    return update(where, flags, occ_energy, virt_energy.reshape(8, TILE), own_part, arrived, amplitudes)


def solution(mesh):
    return jax.shard_map(
        local,
        mesh=mesh,
        in_specs=(
            P("pair", None, None, "virt"),
            P(),
            P("pair", None, None, "virt"),
            P("virt", None),
            P(),
            P(),
        ),
        out_specs=P("pair", None, "rep", "virt"),
        check_vma=False,
    )
```

time: 324 us -> 133 us (0.41)
  waiting for transfers between devices: 280 us -> 59.6 us
  Pallas kernels: 0 us -> 29.6 us
  starting transfers between devices: 0.04 us -> 28.6 us
  matrix products: 21.6 us -> 0 us
  between operations: 13.4 us -> 0.37 us
  local copies, waits for them, and re-layouts: 4.37 us -> 11.3 us
    all_gather x2 -> x0, waiting for transfers between devices: 280 us -> none  [the longest x1 186 us: local(): lax.all_gather(hole_integrals, 'pair', axis=0, tiled=True)]
    ppermute x0 -> x23, waiting for transfers between devices: none -> 59.6 us  [send(): return lax.ppermute(block, AXES, permutation)]
    pallas_call x0 -> x9, Pallas kernels: none -> 29.6 us  [the longest x3 19.5 us: add_quarter(): pl.pallas_call(functools.partial(quarter_kernel, start_from, near, full),...]
    ppermute x0 -> x23, starting transfers between devices: none -> 28.6 us  [send(): return lax.ppermute(block, AXES, permutation)]
    dot_general x2 -> x0, matrix products: 21.6 us -> none  [the longest x1 15.8 us: local(): jnp.einsum('ikac,kcjb->ijab', full_amps, lax.all_gather(hole_integrals, '...]
    unnamed x12 -> x28, local copies, waits for them, and re-layouts: 2.41 us -> 7.06 us
  transfers between devices with their start and end apart: 2 -> 23, of which waited for: 2 -> 10; matrix products, arithmetic and copies ran while one was open for 3% -> 6% of each run, Pallas kernels for 0% -> 17%
where the time goes in v2:
time: 133 us; the launch traced here: 132 us
  waiting for transfers between devices  59.6 us (45%)
  Pallas kernels  29.6 us (22%)
  starting transfers between devices  28.6 us (22%)
  local copies, waits for them, and re-layouts  11.3 us (8%)
  other arithmetic  2.63 us (2%)
    ppermute x23, waiting for transfers between devices, send(): return lax.ppermute(block, AXES, permutation)  59.6 us
    ppermute x23, starting transfers between devices, send(): return lax.ppermute(block, AXES, permutation)  28.6 us
    pallas_call x3, Pallas kernels, add_quarter(): pl.pallas_call(functools.partial(quarter_kernel, start_from, near, full),...  19.5 us
    unnamed x28, local copies, waits for them, and re-layouts  7.06 us
    pallas_call x1, Pallas kernels, last_quarter(): pl.pallas_call(functools.partial(last_kernel, near, full), in_specs=[SMEM...  4.77 us
    dynamic_slice x2, local copies, waits for them, and re-layouts, part_of(): return lax.dynamic_slice_in_dim(block, start, size, 0)  3.35 us
    pallas_call x1, Pallas kernels, rest_of_quarter(): pl.pallas_call(functools.partial(rest_kernel, near), in_specs=[SMEM] + [V...  2.91 us
  transfers between devices with their start and end apart: 23, of which 10 were waited for; matrix products, arithmetic and copies ran while one was open for 6% of the time, Pallas kernels for 17%

profile of v2, /device:TPU:1, one launch (start us, length us, event | category | flops | bytes accessed | tf_op | source)
XLA Modules:
  0.0 132.1 jit_solution(9254735800442309623)
XLA Ops:
  0.0 1.6 %copy-done = bf16[1,1024,8,128]{3,2,1,0:T(8,128)(2,1)S(1)} copy-done((bf16[1,1024,8,128]{3,2,1,0:T(8,128)(2,1)S(1)}, bf16[1,1024,8,128]{3,2,1,0:T(8,128)(2,1)}, u32[]{:S(2)}) %copy-start) | copy-done | bytes 2097176
  1.9 3.4 %collective-permute-start.2 = (bf16[512,1024]{1,0:T(8,128)(2,1)S(1)}, bf16[512,1024]{1,0:T(8,128)(2,1)}, u32[]{:S(2)}, u32[]{:S(2)}) collective-permute-start(bf16[512,1024]{1,0:T(8,128)(2,1)S(1)} %bitcast.29), channel_id=1, source_target_pairs={{0,16},{1,49},{2,18},{3,51},{4,20},{5,53},{6,22},{7,55},{8,24},{9,... | collective-permute-start | bytes 3145736 | tf_op jit(solution)/shard_map/ppermute | solution.py:35
  6.4 2.5 %bitcast_multiply_fusion.refs_0_ = bf16[4,1024,128]{2,1,0:T(8,128)(2,1)} fusion(bf16[4,2,1024,128]{3,2,1,0:T(8,128)(2,1)} %bitcast.38, s32[]{:T(128)S(6)} %select_n.53, bf16[4,1024]{1,0:T(4,128)(2,1)S(1)} %bitcast.43), kind=kLoop, calls=%fused_computation.1 | loop fusion | flops 524288 | bytes 2105348 | tf_op jit(solution)/shard_map/mul | solution.py:260
  8.9 3.8 %collective-permute-start.1 = (bf16[4,1024,128]{2,1,0:T(8,128)(2,1)}, bf16[4,1024,128]{2,1,0:T(8,128)(2,1)}, u32[]{:S(2)}, u32[]{:S(2)}) collective-permute-start(bf16[4,1024,128]{2,1,0:T(8,128)(2,1)} %bitcast_multiply_fusion.refs_0_), channel_id=1, source_target_pairs={{0,2},{1,7},{2,4},{3,1},{4,6},{5,3},{6,0},{7,5},{8,10},{9,15},{10,... | collective-permute-start | bytes 3145736 | tf_op jit(solution)/shard_map/ppermute | solution.py:35
  12.7 1.1 constant_dynamic-slice_fusion
  13.7 2.9 %collective-permute-start = (bf16[256,1024]{1,0:T(8,128)(2,1)}, bf16[256,1024]{1,0:T(8,128)(2,1)}, u32[]{:S(2)}, u32[]{:S(2)}) collective-permute-start(bf16[256,1024]{1,0:T(8,128)(2,1)} %get-tuple-element.24), channel_id=1, source_target_pairs={{0,64},{1,65},{2,66},{3,67},{4,68},{5,69},{6,70},{7,71},{8,72},{9,... | collective-permute-start | bytes 1572872 | tf_op jit(solution)/shard_map/ppermute | solution.py:35
  16.7 2.3 %constant_dynamic-slice_fusion.1 = (bf16[2,1024,128]{2,1,0:T(8,128)(2,1)}, bf16[2,1024,128]{2,1,0:T(8,128)(2,1)}) fusion(bf16[4,1024,128]{2,1,0:T(8,128)(2,1)} %bitcast_multiply_fusion.refs_0_, s32[]{:T(128)S(6)} %select_n.56, s32[]{:T(128)S(6)} %select_n.55), kind=kLoop, calls=%fused_computation.6 | loop fusion | bytes 2097160 | tf_op jit(solution)/shard_map/dynamic_slice | solution.py:268
  18.9 8.6 %collective-permute-done.refs_0_ = bf16[256,1024]{1,0:T(8,128)(2,1)} collective-permute-done((bf16[256,1024]{1,0:T(8,128)(2,1)}, bf16[256,1024]{1,0:T(8,128)(2,1)}, u32[]{:S(2)}, u32[]{:S(2)}) %collective-permute-start) | collective-permute-done | bytes 524320 | tf_op jit(solution)/shard_map/ppermute | solution.py:35
  27.5 1.4 %collective-permute-start.3 = (bf16[2,1024,128]{2,1,0:T(8,128)(2,1)}, bf16[2,1024,128]{2,1,0:T(8,128)(2,1)}, u32[]{:S(2)}, u32[]{:S(2)}) collective-permute-start(bf16[2,1024,128]{2,1,0:T(8,128)(2,1)} %get-tuple-element.14), channel_id=1, source_target_pairs={{0,8},{1,9},{2,10},{3,11},{4,12},{5,13},{6,14},{7,15},{8,0},{9,1},... | collective-permute-start | bytes 1572872 | tf_op jit(solution)/shard_map/ppermute | solution.py:35
  28.9 1.5 %collective-permute-start.6 = (bf16[512,1024]{1,0:T(8,128)(2,1)}, bf16[512,1024]{1,0:T(8,128)(2,1)}, u32[]{:S(2)}, u32[]{:S(2)}) collective-permute-start(bf16[512,1024]{1,0:T(8,128)(2,1)} %collective-permute-done.2.refs_3_.refs_5_), channel_id=1, source_target_pairs={{0,16},{1,49},{2,18},{3,51},{4,20},{5,53},{6,22},{7,55},{8,24},{9,... | collective-permute-start | bytes 3145736 | tf_op jit(solution)/shard_map/ppermute | solution.py:35
  31.0 10.3 %collective-permute-done.3.refs_0_ = bf16[2,1024,128]{2,1,0:T(8,128)(2,1)} collective-permute-done((bf16[2,1024,128]{2,1,0:T(8,128)(2,1)}, bf16[2,1024,128]{2,1,0:T(8,128)(2,1)}, u32[]{:S(2)}, u32[]{:S(2)}) %collective-permute-start.3) | collective-permute-done | bytes 524320 | tf_op jit(solution)/shard_map/ppermute | solution.py:35
  41.2 1.3 collective-permute-start.4
  42.5 1.8 %collective-permute-start.19 = (bf16[256,1024]{1,0:T(8,128)(2,1)}, bf16[256,1024]{1,0:T(8,128)(2,1)}, u32[]{:S(2)}, u32[]{:S(2)}) collective-permute-start(bf16[256,1024]{1,0:T(8,128)(2,1)} %get-tuple-element.19.refs_4_), channel_id=1, source_target_pairs={{0,16},{1,49},{2,18},{3,51},{4,20},{5,53},{6,22},{7,55},{8,24},{9,... | collective-permute-start | bytes 1572872 | tf_op jit(solution)/shard_map/ppermute | solution.py:35
  44.6 10.6 %collective-permute-done.4.refs_0_ = bf16[2,1024,128]{2,1,0:T(8,128)(2,1)} collective-permute-done((bf16[2,1024,128]{2,1,0:T(8,128)(2,1)}, bf16[2,1024,128]{2,1,0:T(8,128)(2,1)}, u32[]{:S(2)}, u32[]{:S(2)}) %collective-permute-start.4) | collective-permute-done | bytes 524320 | tf_op jit(solution)/shard_map/ppermute | solution.py:35
  55.2 2.9 %collective-permute-start.10 = (bf16[256,1024]{1,0:T(8,128)(2,1)}, bf16[256,1024]{1,0:T(8,128)(2,1)S(1)}, u32[]{:S(2)}, u32[]{:S(2)}) collective-permute-start(bf16[256,1024]{1,0:T(8,128)(2,1)} %get-tuple-element.17), channel_id=1, source_target_pairs={{0,64},{1,65},{2,66},{3,67},{4,68},{5,69},{6,70},{7,71},{8,72},{9,... | collective-permute-start | bytes 1572872 | tf_op jit(solution)/shard_map/ppermute | solution.py:35
  59.1 10.6 %collective-permute-done.10.refs_4_ = bf16[256,1024]{1,0:T(8,128)(2,1)S(1)} collective-permute-done((bf16[256,1024]{1,0:T(8,128)(2,1)}, bf16[256,1024]{1,0:T(8,128)(2,1)S(1)}, u32[]{:S(2)}, u32[]{:S(2)}) %collective-permute-start.10) | collective-permute-done | bytes 524320 | tf_op jit(solution)/shard_map/ppermute | solution.py:35
  71.4 1.8 %collective-permute-done.7.refs_1_ = bf16[2,1024,128]{2,1,0:T(8,128)(2,1)} collective-permute-done((bf16[2,1024,128]{2,1,0:T(8,128)(2,1)}, bf16[2,1024,128]{2,1,0:T(8,128)(2,1)}, u32[]{:S(2)}, u32[]{:S(2)}) %collective-permute-start.7) | collective-permute-done | bytes 524320 | tf_op jit(solution)/shard_map/ppermute | solution.py:35
  73.3 1.1 collective-permute-start.8
  74.4 9.3 %collective-permute-done.11.refs_5_ = bf16[256,1024]{1,0:T(8,128)(2,1)} collective-permute-done((bf16[256,1024]{1,0:T(8,128)(2,1)S(1)}, bf16[256,1024]{1,0:T(8,128)(2,1)}, u32[]{:S(2)}, u32[]{:S(2)}) %collective-permute-start.11) | collective-permute-done | bytes 524320 | tf_op jit(solution)/shard_map/ppermute | solution.py:35
  83.6 2.1 %collective-permute-start.12 = (bf16[256,1024]{1,0:T(8,128)(2,1)}, bf16[256,1024]{1,0:T(8,128)(2,1)}, u32[]{:S(2)}, u32[]{:S(2)}) collective-permute-start(bf16[256,1024]{1,0:T(8,128)(2,1)} %collective-permute-done.11.refs_5_), channel_id=1, source_target_pairs={{0,16},{1,49},{2,18},{3,51},{4,20},{5,53},{6,22},{7,55},{8,24},{9,... | collective-permute-start | bytes 1572872 | tf_op jit(solution)/shard_map/ppermute | solution.py:35
  85.7 4.7 %collective-permute-done.15.refs_2_ = bf16[2,1024,128]{2,1,0:T(8,128)(2,1)} collective-permute-done((bf16[2,1024,128]{2,1,0:T(8,128)(2,1)S(1)}, bf16[2,1024,128]{2,1,0:T(8,128)(2,1)}, u32[]{:S(2)}, u32[]{:S(2)}) %collective-permute-start.15) | collective-permute-done | bytes 524320 | tf_op jit(solution)/shard_map/ppermute | solution.py:35
  92.4 1.1 copy.22
  93.6 2.5 %collective-permute-done.8.refs_2_ = bf16[2,1024,128]{2,1,0:T(8,128)(2,1)} collective-permute-done((bf16[2,1024,128]{2,1,0:T(8,128)(2,1)}, bf16[2,1024,128]{2,1,0:T(8,128)(2,1)}, u32[]{:S(2)}, u32[]{:S(2)}) %collective-permute-start.8) | collective-permute-done | bytes 524320 | tf_op jit(solution)/shard_map/ppermute | solution.py:35
  96.0 1.2 collective-permute-start.9
  97.3 1.2 copy-done.3
  98.5 6.2 %add_quarter.3.refs_9_ = f32[1024,1024]{1,0:T(8,128)S(1)} custom-call(s32[3]{0:T(128)S(1)} %pad_add_fusion.where, bf16[4,1024,128]{2,1,0:T(8,128)(2,1)} %bitcast_multiply_fusion.refs_0_, bf16[4,1024,128]{2,1,0:T(8,128)(2,1)} %collective-permute-done.1.refs_2_.refs_1_, bf16[4,1024,128]{2,1,0:T(8,128)(2,1)} %collective-permute-done.5.refs_2_, ...), custom_call_target="tpu_custom_call" | custom-call | flops 2684354560 | bytes 8388608 | tf_op jit(solution)/shard_map/add_quarter/pallas_call | solution.py:162
  104.7 6.8 %add_quarter.4.refs_9_ = f32[1024,1024]{1,0:T(8,128)S(1)} custom-call(s32[3]{0:T(128)S(1)} %pad_add_fusion.where, bf16[4,1024,128]{2,1,0:T(8,128)(2,1)} %bitcast_multiply_fusion.refs_0_, bf16[4,1024,128]{2,1,0:T(8,128)(2,1)} %collective-permute-done.1.refs_2_.refs_1_, ...), custom_call_target="tpu_custom_call", output_to_operand_aliasing={{}: (10, {})} | custom-call | flops 2684354560 | bytes 8388608 | tf_op jit(solution)/shard_map/add_quarter/pallas_call | solution.py:162
  111.6 6.5 %add_quarter.5.refs_9_.acc_ref = f32[1024,1024]{1,0:T(8,128)S(1)} custom-call(s32[3]{0:T(128)S(1)} %pad_add_fusion.where, bf16[2,1024,128]{2,1,0:T(8,128)(2,1)} %get-tuple-element.18.refs_0_, bf16[2,1024,128]{2,1,0:T(8,128)(2,1)S(1)} %copy-done.8, bf16[2,1024,128]{2,1,0:T(8,128)(2,1)} %collective-permute-done.15.refs_2_, ...), custom_call_target="tpu_custom_call", output_to_operand_aliasing={{}: (10, {})} | custom-call | flops 2684354560 | bytes 8388608 | tf_op jit(solution)/shard_map/add_quarter/pallas_call | solution.py:162
  118.1 4.8 %last_quarter.1 = (f32[512,1024]{1,0:T(8,128)S(1)}, bf16[1024,1024]{1,0:T(8,128)(2,1)S(1)}, bf16[1024,1024]{1,0:T(8,128)(2,1)S(1)}) custom-call(s32[3]{0:T(128)S(1)} %pad_add_fusion.where, bf16[2,1024,128]{2,1,0:T(8,128)(2,1)} %get-tuple-element.16.refs_0_, bf16[2,1024,128]{2,1,0:T(8,128)(2,1)} %collective-permute-done.7.refs_1_, ...), custom_call_target="tpu_custom_call" | custom-call | flops 1342177280 | bytes 8388608 | tf_op jit(solution)/shard_map/last_quarter/pallas_call | solution.py:180
  122.9 2.8 %collective-permute-start.22 = (f32[512,1024]{1,0:T(8,128)S(1)}, f32[512,1024]{1,0:T(8,128)S(1)}, u32[]{:S(2)}, u32[]{:S(2)}) collective-permute-start(f32[512,1024]{1,0:T(8,128)S(1)} %get-tuple-element.22), channel_id=1, source_target_pairs={{0,1},{1,0},{2,3},{3,2},{4,5},{5,4},{6,7},{7,6},{8,9},{9,8},{10,11... | collective-permute-start | bytes 6291464 | tf_op jit(solution)/shard_map/ppermute | solution.py:35
  125.6 2.9 %rest_of_quarter.1.own_ref = f32[512,1024]{1,0:T(8,128)S(1)} custom-call(s32[3]{0:T(128)S(1)} %pad_add_fusion.where, bf16[1024,1024]{1,0:T(8,128)(2,1)S(1)} %get-tuple-element.20.a_all, bf16[1024,1024]{1,0:T(8,128)(2,1)S(1)} %get-tuple-element.21.b_all, bf16[1024,128]{1,0:T(8,128)(2,1)S(1)} %bitcast.37, f32[1024,1024]{1,0:T(8,128)S(1)} %add_quarter.5.refs_9_.acc_ref), custom_call_target="tpu_custom_call" | custom-call | flops 1342177280 | bytes 8388608 | tf_op jit(solution)/shard_map/rest_of_quarter/pallas_call | solution.py:197
  129.4 2.5 %update.1 = f32[1,8,512,128]{3,2,1,0:T(8,128)} custom-call(s32[3]{0:T(128)S(1)} %pad_add_fusion.where, s32[8,8]{1,0:T(8,128)S(1)} %bitcast.40, f32[8]{0:T(128)S(1)} %copy-done.10, f32[8,128]{1,0:T(8,128)S(1)} %bitcast.41, f32[512,1024]{1,0:T(8,128)S(1)} %rest_of_quarter.1.own_ref, f32[512,1024]{1,0:T(8,128)S(1)} %collective-permute-done.22.other_ref, ...), custom_call_target="tpu_custom_call" | custom-call | tf_op jit(solution)/shard_map/update/pallas_call | solution.py:235
  (58 shorter events, 7.9 us)
Async XLA Ops:
  0.0 1.6 %copy-start = (bf16[1,1024,8,128]{3,2,1,0:T(8,128)(2,1)S(1)}, bf16[1,1024,8,128]{3,2,1,0:T(8,128)(2,1)}, u32[]{:S(2)}) copy-start(bf16[1,1024,8,128]{3,2,1,0:T(8,128)(2,1)} %param.8) | copy-start | bytes 6291460
  1.9 25.6 %collective-permute-start.2 = (bf16[512,1024]{1,0:T(8,128)(2,1)S(1)}, bf16[512,1024]{1,0:T(8,128)(2,1)}, u32[]{:S(2)}, u32[]{:S(2)}) collective-permute-start(bf16[512,1024]{1,0:T(8,128)(2,1)S(1)} %bitcast.29), channel_id=1, source_target_pairs={{0,16},{1,49},{2,18},{3,51},{4,20},{5,53},{6,22},{7,55},{8,24},{9,... | collective-permute-start | bytes 3145736 | tf_op jit(solution)/shard_map/ppermute | solution.py:35
  8.9 18.6 %collective-permute-start.1 = (bf16[4,1024,128]{2,1,0:T(8,128)(2,1)}, bf16[4,1024,128]{2,1,0:T(8,128)(2,1)}, u32[]{:S(2)}, u32[]{:S(2)}) collective-permute-start(bf16[4,1024,128]{2,1,0:T(8,128)(2,1)} %bitcast_multiply_fusion.refs_0_), channel_id=1, source_target_pairs={{0,2},{1,7},{2,4},{3,1},{4,6},{5,3},{6,0},{7,5},{8,10},{9,15},{10,... | collective-permute-start | bytes 3145736 | tf_op jit(solution)/shard_map/ppermute | solution.py:35
  13.7 13.8 %collective-permute-start = (bf16[256,1024]{1,0:T(8,128)(2,1)}, bf16[256,1024]{1,0:T(8,128)(2,1)}, u32[]{:S(2)}, u32[]{:S(2)}) collective-permute-start(bf16[256,1024]{1,0:T(8,128)(2,1)} %get-tuple-element.24), channel_id=1, source_target_pairs={{0,64},{1,65},{2,66},{3,67},{4,68},{5,69},{6,70},{7,71},{8,72},{9,... | collective-permute-start | bytes 1572872 | tf_op jit(solution)/shard_map/ppermute | solution.py:35
  27.5 13.7 %collective-permute-start.3 = (bf16[2,1024,128]{2,1,0:T(8,128)(2,1)}, bf16[2,1024,128]{2,1,0:T(8,128)(2,1)}, u32[]{:S(2)}, u32[]{:S(2)}) collective-permute-start(bf16[2,1024,128]{2,1,0:T(8,128)(2,1)} %get-tuple-element.14), channel_id=1, source_target_pairs={{0,8},{1,9},{2,10},{3,11},{4,12},{5,13},{6,14},{7,15},{8,0},{9,1},... | collective-permute-start | bytes 1572872 | tf_op jit(solution)/shard_map/ppermute | solution.py:35
  28.9 15.4 %collective-permute-start.6 = (bf16[512,1024]{1,0:T(8,128)(2,1)}, bf16[512,1024]{1,0:T(8,128)(2,1)}, u32[]{:S(2)}, u32[]{:S(2)}) collective-permute-start(bf16[512,1024]{1,0:T(8,128)(2,1)} %collective-permute-done.2.refs_3_.refs_5_), channel_id=1, source_target_pairs={{0,16},{1,49},{2,18},{3,51},{4,20},{5,53},{6,22},{7,55},{8,24},{9,... | collective-permute-start | bytes 3145736 | tf_op jit(solution)/shard_map/ppermute | solution.py:35
  30.4 14.3 %collective-permute-start.5 = (bf16[4,1024,128]{2,1,0:T(8,128)(2,1)}, bf16[4,1024,128]{2,1,0:T(8,128)(2,1)}, u32[]{:S(2)}, u32[]{:S(2)}) collective-permute-start(bf16[4,1024,128]{2,1,0:T(8,128)(2,1)} %collective-permute-done.1.refs_2_.refs_1_), channel_id=1, source_target_pairs={{0,2},{1,7},{2,4},{3,1},{4,6},{5,3},{6,0},{7,5},{8,10},{9,15},{10,... | collective-permute-start | bytes 3145736 | tf_op jit(solution)/shard_map/ppermute | solution.py:35
  41.2 14.0 %collective-permute-start.4 = (bf16[2,1024,128]{2,1,0:T(8,128)(2,1)}, bf16[2,1024,128]{2,1,0:T(8,128)(2,1)}, u32[]{:S(2)}, u32[]{:S(2)}) collective-permute-start(bf16[2,1024,128]{2,1,0:T(8,128)(2,1)} %get-tuple-element.15), channel_id=1, source_target_pairs={{0,8},{1,9},{2,10},{3,11},{4,12},{5,13},{6,14},{7,15},{8,0},{9,1},... | collective-permute-start | bytes 1572872 | tf_op jit(solution)/shard_map/ppermute | solution.py:35
  42.5 15.6 %collective-permute-start.19 = (bf16[256,1024]{1,0:T(8,128)(2,1)}, bf16[256,1024]{1,0:T(8,128)(2,1)}, u32[]{:S(2)}, u32[]{:S(2)}) collective-permute-start(bf16[256,1024]{1,0:T(8,128)(2,1)} %get-tuple-element.19.refs_4_), channel_id=1, source_target_pairs={{0,16},{1,49},{2,18},{3,51},{4,20},{5,53},{6,22},{7,55},{8,24},{9,... | collective-permute-start | bytes 1572872 | tf_op jit(solution)/shard_map/ppermute | solution.py:35
  55.2 14.5 %collective-permute-start.10 = (bf16[256,1024]{1,0:T(8,128)(2,1)}, bf16[256,1024]{1,0:T(8,128)(2,1)S(1)}, u32[]{:S(2)}, u32[]{:S(2)}) collective-permute-start(bf16[256,1024]{1,0:T(8,128)(2,1)} %get-tuple-element.17), channel_id=1, source_target_pairs={{0,64},{1,65},{2,66},{3,67},{4,68},{5,69},{6,70},{7,71},{8,72},{9,... | collective-permute-start | bytes 1572872 | tf_op jit(solution)/shard_map/ppermute | solution.py:35
  58.1 12.4 %collective-permute-start.20 = (bf16[256,1024]{1,0:T(8,128)(2,1)}, bf16[256,1024]{1,0:T(8,128)(2,1)}, u32[]{:S(2)}, u32[]{:S(2)}) collective-permute-start(bf16[256,1024]{1,0:T(8,128)(2,1)} %collective-permute-done.19.refs_5_), channel_id=1, source_target_pairs={{0,16},{1,49},{2,18},{3,51},{4,20},{5,53},{6,22},{7,55},{8,24},{9,... | collective-permute-start | bytes 1572872 | tf_op jit(solution)/shard_map/ppermute | solution.py:35
  59.0 11.6 %collective-permute-start.14 = (bf16[2,1024,128]{2,1,0:T(8,128)(2,1)}, bf16[2,1024,128]{2,1,0:T(8,128)(2,1)S(1)}, u32[]{:S(2)}, u32[]{:S(2)}) collective-permute-start(bf16[2,1024,128]{2,1,0:T(8,128)(2,1)} %get-tuple-element.18.refs_0_), channel_id=1, source_target_pairs={{0,2},{1,7},{2,4},{3,1},{4,6},{5,3},{6,0},{7,5},{8,10},{9,15},{10,... | collective-permute-start | bytes 1572872 | tf_op jit(solution)/shard_map/ppermute | solution.py:35
  59.0 31.4 %collective-permute-start.17 = (bf16[512,1024]{1,0:T(8,128)(2,1)}, bf16[512,1024]{1,0:T(8,128)(2,1)S(1)}, u32[]{:S(2)}, u32[]{:S(2)}) collective-permute-start(bf16[512,1024]{1,0:T(8,128)(2,1)} %collective-permute-done.6.refs_3_.refs_6_), channel_id=1, source_target_pairs={{0,16},{1,49},{2,18},{3,51},{4,20},{5,53},{6,22},{7,55},{8,24},{9,... | collective-permute-start | bytes 3145736 | tf_op jit(solution)/shard_map/ppermute | solution.py:35
  59.1 14.2 %collective-permute-start.7 = (bf16[2,1024,128]{2,1,0:T(8,128)(2,1)}, bf16[2,1024,128]{2,1,0:T(8,128)(2,1)}, u32[]{:S(2)}, u32[]{:S(2)}) collective-permute-start(bf16[2,1024,128]{2,1,0:T(8,128)(2,1)} %get-tuple-element.16.refs_0_), channel_id=1, source_target_pairs={{0,2},{1,7},{2,4},{3,1},{4,6},{5,3},{6,0},{7,5},{8,10},{9,15},{10,... | collective-permute-start | bytes 1572872 | tf_op jit(solution)/shard_map/ppermute | solution.py:35
  69.7 13.9 %collective-permute-start.11 = (bf16[256,1024]{1,0:T(8,128)(2,1)S(1)}, bf16[256,1024]{1,0:T(8,128)(2,1)}, u32[]{:S(2)}, u32[]{:S(2)}) collective-permute-start(bf16[256,1024]{1,0:T(8,128)(2,1)S(1)} %collective-permute-done.10.refs_4_), channel_id=1, source_target_pairs={{0,16},{1,49},{2,18},{3,51},{4,20},{5,53},{6,22},{7,55},{8,24},{9,... | collective-permute-start | bytes 1572872 | tf_op jit(solution)/shard_map/ppermute | solution.py:35
  70.5 26.7 %collective-permute-start.18 = (bf16[4,1024,128]{2,1,0:T(8,128)(2,1)}, bf16[4,1024,128]{2,1,0:T(8,128)(2,1)}, u32[]{:S(2)}, u32[]{:S(2)}) collective-permute-start(bf16[4,1024,128]{2,1,0:T(8,128)(2,1)} %collective-permute-done.5.refs_2_), channel_id=1, source_target_pairs={{0,2},{1,7},{2,4},{3,1},{4,6},{5,3},{6,0},{7,5},{8,10},{9,15},{10,... | collective-permute-start | bytes 3145736 | tf_op jit(solution)/shard_map/ppermute | solution.py:35
  70.6 19.9 %collective-permute-start.15 = (bf16[2,1024,128]{2,1,0:T(8,128)(2,1)S(1)}, bf16[2,1024,128]{2,1,0:T(8,128)(2,1)}, u32[]{:S(2)}, u32[]{:S(2)}) collective-permute-start(bf16[2,1024,128]{2,1,0:T(8,128)(2,1)S(1)} %collective-permute-done.14.refs_1_), channel_id=1, source_target_pairs={{0,2},{1,7},{2,4},{3,1},{4,6},{5,3},{6,0},{7,5},{8,10},{9,15},{10,... | collective-permute-start | bytes 1572872 | tf_op jit(solution)/shard_map/ppermute | solution.py:35
  73.3 22.8 %collective-permute-start.8 = (bf16[2,1024,128]{2,1,0:T(8,128)(2,1)}, bf16[2,1024,128]{2,1,0:T(8,128)(2,1)}, u32[]{:S(2)}, u32[]{:S(2)}) collective-permute-start(bf16[2,1024,128]{2,1,0:T(8,128)(2,1)} %collective-permute-done.7.refs_1_), channel_id=1, source_target_pairs={{0,2},{1,7},{2,4},{3,1},{4,6},{5,3},{6,0},{7,5},{8,10},{9,15},{10,... | collective-permute-start | bytes 1572872 | tf_op jit(solution)/shard_map/ppermute | solution.py:35
  83.6 13.6 %collective-permute-start.12 = (bf16[256,1024]{1,0:T(8,128)(2,1)}, bf16[256,1024]{1,0:T(8,128)(2,1)}, u32[]{:S(2)}, u32[]{:S(2)}) collective-permute-start(bf16[256,1024]{1,0:T(8,128)(2,1)} %collective-permute-done.11.refs_5_), channel_id=1, source_target_pairs={{0,16},{1,49},{2,18},{3,51},{4,20},{5,53},{6,22},{7,55},{8,24},{9,... | collective-permute-start | bytes 1572872 | tf_op jit(solution)/shard_map/ppermute | solution.py:35
  90.4 14.3 %collective-permute-start.21 = (bf16[256,1024]{1,0:T(8,128)(2,1)}, bf16[256,1024]{1,0:T(8,128)(2,1)}, u32[]{:S(2)}, u32[]{:S(2)}) collective-permute-start(bf16[256,1024]{1,0:T(8,128)(2,1)} %collective-permute-done.20.refs_6_), channel_id=1, source_target_pairs={{0,16},{1,49},{2,18},{3,51},{4,20},{5,53},{6,22},{7,55},{8,24},{9,... | collective-permute-start | bytes 1572872 | tf_op jit(solution)/shard_map/ppermute | solution.py:35
  90.4 1.0 copy-start.2
  91.4 20.1 %collective-permute-start.16 = (bf16[2,1024,128]{2,1,0:T(8,128)(2,1)}, bf16[2,1024,128]{2,1,0:T(8,128)(2,1)}, u32[]{:S(2)}, u32[]{:S(2)}) collective-permute-start(bf16[2,1024,128]{2,1,0:T(8,128)(2,1)} %collective-permute-done.15.refs_2_), channel_id=1, source_target_pairs={{0,2},{1,7},{2,4},{3,1},{4,6},{5,3},{6,0},{7,5},{8,10},{9,15},{10,... | collective-permute-start | bytes 1572872 | tf_op jit(solution)/shard_map/ppermute | solution.py:35
  96.0 22.0 %collective-permute-start.9 = (bf16[2,1024,128]{2,1,0:T(8,128)(2,1)}, bf16[2,1024,128]{2,1,0:T(8,128)(2,1)S(1)}, u32[]{:S(2)}, u32[]{:S(2)}) collective-permute-start(bf16[2,1024,128]{2,1,0:T(8,128)(2,1)} %collective-permute-done.8.refs_2_), channel_id=1, source_target_pairs={{0,2},{1,7},{2,4},{3,1},{4,6},{5,3},{6,0},{7,5},{8,10},{9,15},{10,... | collective-permute-start | bytes 1572872 | tf_op jit(solution)/shard_map/ppermute | solution.py:35
  97.3 20.8 %collective-permute-start.13 = (bf16[256,1024]{1,0:T(8,128)(2,1)}, bf16[256,1024]{1,0:T(8,128)(2,1)S(1)}, u32[]{:S(2)}, u32[]{:S(2)}) collective-permute-start(bf16[256,1024]{1,0:T(8,128)(2,1)} %collective-permute-done.12.refs_6_), channel_id=1, source_target_pairs={{0,16},{1,49},{2,18},{3,51},{4,20},{5,53},{6,22},{7,55},{8,24},{9,... | collective-permute-start | bytes 1572872 | tf_op jit(solution)/shard_map/ppermute | solution.py:35
  97.3 1.2 copy-start.3
  104.7 6.9 %copy-start.4 = (bf16[512,1024]{1,0:T(8,128)(2,1)S(1)}, bf16[512,1024]{1,0:T(8,128)(2,1)}, u32[]{:S(2)}) copy-start(bf16[512,1024]{1,0:T(8,128)(2,1)} %copy-done.2) | copy-start | bytes 3145732
  104.7 6.9 %copy-start.8 = (bf16[2,1024,128]{2,1,0:T(8,128)(2,1)S(1)}, bf16[2,1024,128]{2,1,0:T(8,128)(2,1)}, u32[]{:S(2)}) copy-start(bf16[2,1024,128]{2,1,0:T(8,128)(2,1)} %copy-done.7) | copy-start | bytes 1572868
  111.5 6.5 %copy-start.6 = (bf16[256,1024]{1,0:T(8,128)(2,1)S(1)}, bf16[256,1024]{1,0:T(8,128)(2,1)}, u32[]{:S(2)}) copy-start(bf16[256,1024]{1,0:T(8,128)(2,1)} %copy-done.5) | copy-start | bytes 1572868
  122.9 6.5 %collective-permute-start.22 = (f32[512,1024]{1,0:T(8,128)S(1)}, f32[512,1024]{1,0:T(8,128)S(1)}, u32[]{:S(2)}, u32[]{:S(2)}) collective-permute-start(f32[512,1024]{1,0:T(8,128)S(1)} %get-tuple-element.22), channel_id=1, source_target_pairs={{0,1},{1,0},{2,3},{3,2},{4,5},{5,4},{6,7},{7,6},{8,9},{9,8},{10,11... | collective-permute-start | bytes 6291464 | tf_op jit(solution)/shard_map/ppermute | solution.py:35
  125.6 3.8 %copy-start.1 = (bf16[1,8,1024,128]{3,2,1,0:T(8,128)(2,1)S(1)}, bf16[1,8,1024,128]{3,2,1,0:T(8,128)(2,1)}, u32[]{:S(2)}) copy-start(bf16[1,8,1024,128]{3,2,1,0:T(8,128)(2,1)} %amps_ref.1) | copy-start | bytes 6291460
  125.6 3.8 %copy-start.9 = (f32[1024]{0:T(1024)S(1)}, f32[1024]{0:T(1024)}, u32[]{:S(2)}) copy-start(f32[1024]{0:T(1024)} %param.11) | copy-start | bytes 12292
  125.6 3.8 %copy-start.10 = (f32[8]{0:T(128)S(1)}, f32[8]{0:T(128)}, u32[]{:S(2)}) copy-start(f32[8]{0:T(128)} %occ_ref.1) | copy-start | bytes 100
  (2 other events, 1.6 us)

commit v3 on v0

v3 whole, which is shorter than its diff:
```python
import functools

import jax
import jax.numpy as jnp
from jax import lax
from jax.experimental import pallas as pl
from jax.experimental.pallas import tpu as pltpu
from jax.sharding import PartitionSpec as P

TILE = 128
GATE, STAY = 7, 6
AXES = ("pair", "virt", "rep")


def device_permutation(move):
    pairs = []
    for index in range(128):
        p, v, core = index // 16, (index // 2) % 8, index % 2
        y, x, z, core = move((p // 4) * 2 + v // 4, p % 4, v % 4, core)
        pairs.append((index, ((y // 2) * 4 + x % 4) * 16 + ((y % 2) * 4 + z % 4) * 2 + core))
    return pairs


def ring_next(plane, place, cross):
    if plane == 0:
        return (1, place) if place == cross else (0, (place + 1) % 4)
    return (0, place) if place == (cross + 1) % 4 else (1, (place + 3) % 4)


def ring_move(plane, place, cross, core):
    if core == 0:
        return ring_next(plane, place, cross)
    return next(
        (a, b) for a in range(2) for b in range(4) if ring_next(a, b, cross) == (plane, place)
    )


def along_virt(y, x, z, core):
    low, z = ring_move(y % 2, z, 0 if x < 2 else 2, core)
    return (y // 2) * 2 + low, x, z, core


def along_pair(y, x, z, core):
    high, x = ring_move(y // 2, x, 2 if z < 2 else 0, core)
    return high * 2 + y % 2, x, z, core


ALONG_VIRT = device_permutation(along_virt)
ALONG_PAIR = device_permutation(along_pair)
CORES = device_permutation(lambda y, x, z, c: (y, x, z, 1 - c))


def send(block, permutation):
    return lax.ppermute(block, AXES, permutation)


def bit_of(index):
    return (index + index // 4) % 2


def on_ring(index, cross, core, step):
    plane, place = index // 4, index % 4
    spot = jnp.where(plane == 0, (place - cross + 3) % 4, 4 + (cross - place + 4) % 4)
    spot = (spot + 8 - (1 - 2 * core) * step) % 8
    return jnp.where(spot < 4, (spot + cross + 1) % 4, 4 + (cross - spot + 8) % 4)


class Tiles:
    def __init__(self, where, items):
        p, v, core = where[0], where[1], where[2]
        self.items = items
        self.odd = (core + bit_of(p) + bit_of(v)) % 2
        cross = jnp.where(p % 4 < 2, 0, 2)
        self.v = [on_ring(v, cross, core, q) for q in range(8)]
        cross = jnp.where(v % 4 < 2, 2, 0)
        self.k = [on_ring(p, cross, core, q) for q in range(8)]

    def pairs(self, item):
        i, j = self.items[item]
        for t in range(2):
            second = (self.odd + t) % 2
            k = jnp.where(second == 0, self.k[2 * j], self.k[2 * j + 1])
            yield t, 2 * i + t, self.v[2 * i + t], second, k


def start_left(tiles, left, a_all, sems, row_start, rows):
    part = pl.ds(row_start, rows)
    for item in range(len(tiles.items)):
        for t, q, _, _, k in tiles.pairs(item):
            for half in range(2):

                @pl.when(k // 4 == half)
                def _():
                    pltpu.make_async_copy(
                        left[q][half].at[(k % 4) // 2, part, :],
                        a_all.at[part, (2 * item + t) * TILE : (2 * item + t + 1) * TILE],
                        sems.at[item, t],
                    ).start()

    def wait(item):
        i = tiles.items[item][0]
        for t in range(2):
            pltpu.make_async_copy(
                left[2 * i + t][0].at[0, part, :],
                a_all.at[part, (2 * item + t) * TILE : (2 * item + t + 1) * TILE],
                sems.at[item, t],
            ).wait()

    return wait


def start_right(tiles, right, b_all, sems):
    for item in range(len(tiles.items)):
        j = tiles.items[item][1]
        for t, _, v, second, _ in tiles.pairs(item):
            for which in range(2):
                for half in range(2):

                    @pl.when((second == which) & (v // 4 == half))
                    def _():
                        rows = pl.ds(pl.multiple_of(((v % 4) // 2) * TILE, TILE), TILE)
                        pltpu.make_async_copy(
                            right[2 * j + which][half].at[rows, :],
                            b_all.at[(2 * item + t) * TILE : (2 * item + t + 1) * TILE, :],
                            sems.at[item, t],
                        ).start()

    def wait(item):
        j = tiles.items[item][1]
        for t in range(2):
            pltpu.make_async_copy(
                right[2 * j][0].at[pl.ds(0, TILE), :],
                b_all.at[(2 * item + t) * TILE : (2 * item + t + 1) * TILE, :],
                sems.at[item, t],
            ).wait()

    return wait


def multiply(tiles, fock_ref, acc_ref, out_ref, a_all, b_all, row_start):
    rows, width, block = out_ref.shape[0], 256, 512

    def columns_of(step, carry):
        columns = pl.ds(pl.multiple_of(step * width, width), width)
        for row in range(0, rows, block):
            source = pl.ds(row_start + row, block)
            total = jnp.dot(a_all[source, :], b_all[:, columns], preferred_element_type=jnp.float32)
            if acc_ref is not None:
                total += acc_ref[source, columns]
            out_ref[pl.ds(row, block), columns] = total
        return carry

    lax.fori_loop(0, 1024 // width, columns_of, 0)
    blank = jnp.zeros((TILE, TILE), jnp.bfloat16)
    for item in range(len(tiles.items)):
        fock, places = [], []
        for t, _, v, _, k in tiles.pairs(item):
            own = fock_ref[pl.ds(pl.multiple_of(v * TILE, TILE), TILE), :]
            fock.append(jnp.concatenate([own, blank] if t == 0 else [blank, own], axis=1))
            places.append(pl.ds(pl.multiple_of(k * TILE, TILE), TILE))
        fock = jnp.concatenate(fock, axis=0)
        for row in range(0, rows, block):
            part = pl.ds(row, block)
            left = a_all[pl.ds(row_start + row, block), item * 256 : (item + 1) * 256]
            total = jnp.dot(left, fock, preferred_element_type=jnp.float32)
            for t in range(2):
                out_ref[part, places[t]] += total[:, t * TILE : (t + 1) * TILE]


def gate_kernel(*refs):
    pass


def gate(passed, after):
    return pl.pallas_call(
        gate_kernel,
        out_shape=[jax.ShapeDtypeStruct(x.shape, x.dtype) for x in passed],
        in_specs=[ANYWHERE] * (len(passed) + len(after)),
        out_specs=[ANYWHERE] * len(passed),
        input_output_aliases={i: i for i in range(len(passed))},
        name="gate",
    )(*passed, *after)


def paired(refs):
    return [refs[n : n + 2] for n in range(0, len(refs), 2)]


def part_kernel(start_from, items, count, where, *refs):
    left, right = paired(refs[: 2 * count]), paired(refs[2 * count : 4 * count])
    fock_ref, refs = refs[4 * count], refs[4 * count + 1 :]
    acc_ref = None
    if start_from:
        acc_ref, refs = refs[0], refs[1:]
    out_ref, a_all, b_all, left_sems, right_sems = refs
    tiles = Tiles(where, items)
    wait_right = start_right(tiles, right, b_all, right_sems)
    wait_left = start_left(tiles, left, a_all, left_sems, 0, 1024)
    for item in range(len(items)):
        wait_right(item)
        wait_left(item)
    multiply(tiles, fock_ref, acc_ref, out_ref, a_all, b_all, 0)


def last_kernel(items, count, where, *refs):
    left, right = paired(refs[: 2 * count]), paired(refs[2 * count : 4 * count])
    fock_ref, acc_ref, out_ref, a_all, b_all, left_sems, right_sems = refs[4 * count :]
    tiles = Tiles(where, items)
    wait_right = start_right(tiles, right, b_all, right_sems)
    row_start = pl.multiple_of((1 - where[2]) * 512, 512)
    wait_left = start_left(tiles, left, a_all, left_sems.at[0], row_start, 512)
    kept = pl.multiple_of(where[2] * 512, 512)
    wait_kept = start_left(tiles, left, a_all, left_sems.at[1], kept, 512)
    for item in range(len(items)):
        wait_right(item)
        wait_left(item)
    multiply(tiles, fock_ref, acc_ref, out_ref, a_all, b_all, row_start)
    for item in range(len(items)):
        wait_kept(item)


def rest_kernel(items, where, a_all, b_all, fock_ref, acc_ref, out_ref):
    tiles = Tiles(where, items)
    row_start = pl.multiple_of(where[2] * 512, 512)
    multiply(tiles, fock_ref, acc_ref, out_ref, a_all, b_all, row_start)


ANYWHERE = pl.BlockSpec(memory_space=pl.ANY)
HBM = pl.BlockSpec(memory_space=pltpu.HBM)
VMEM = pl.BlockSpec(memory_space=pltpu.VMEM)
SMEM = pl.BlockSpec(memory_space=pltpu.SMEM)
LIMIT = pltpu.CompilerParams(vmem_limit_bytes=16 * 2**20)
FIRST = ((0, 0), (0, 1), (1, 0), (1, 1))
SECOND = ((0, 2), (2, 0), (1, 2), (2, 1), (2, 2))
THIRD = ((0, 3), (3, 0), (1, 3), (3, 1), (2, 3), (3, 2), (3, 3))


def cost(rows, items):
    return pl.CostEstimate(
        flops=2 * rows * 1280 * 256 * len(items),
        bytes_accessed=len(items) * 2**20,
        transcendentals=0,
    )


def flat(blocks, stay=8):
    halves = [half for block in blocks for half in block]
    return [
        pltpu.with_memory_space_constraint(half, pltpu.HBM) if n < 2 * stay else half
        for n, half in enumerate(halves)
    ]


def add_part(acc, where, left, right, fock_columns, items):
    start_from = acc is not None
    count = len(left)
    return pl.pallas_call(
        functools.partial(part_kernel, start_from, items, count),
        in_specs=[SMEM] + [HBM] * 4 * count + [VMEM] * (1 + start_from),
        out_specs=VMEM,
        scratch_shapes=[
            pltpu.VMEM((1024, 256 * len(items)), jnp.bfloat16),
            pltpu.VMEM((256 * len(items), 1024), jnp.bfloat16),
            pltpu.SemaphoreType.DMA((len(items), 2)),
            pltpu.SemaphoreType.DMA((len(items), 2)),
        ],
        out_shape=jax.ShapeDtypeStruct((1024, 1024), jnp.float32),
        input_output_aliases={4 * count + 2: 0} if start_from else {},
        compiler_params=LIMIT,
        cost_estimate=cost(1024, items),
        name="add_part",
    )(where, *flat(left), *flat(right), fock_columns, *([acc] * start_from))


def last_part(acc, where, left, right, fock_columns, items):
    count = len(left)
    return pl.pallas_call(
        functools.partial(last_kernel, items, count),
        in_specs=[SMEM] + [HBM] * 4 * count + [VMEM] * 2,
        out_specs=[VMEM] * 3,
        scratch_shapes=[
            pltpu.SemaphoreType.DMA((2, len(items), 2)),
            pltpu.SemaphoreType.DMA((len(items), 2)),
        ],
        out_shape=[
            jax.ShapeDtypeStruct((512, 1024), jnp.float32),
            jax.ShapeDtypeStruct((1024, 256 * len(items)), jnp.bfloat16),
            jax.ShapeDtypeStruct((256 * len(items), 1024), jnp.bfloat16),
        ],
        compiler_params=LIMIT,
        cost_estimate=cost(512, items),
        name="last_part",
    )(where, *flat(left, STAY), *flat(right, STAY), fock_columns, acc)


def rest_of_part(acc, where, a_all, b_all, fock_columns, items):
    return pl.pallas_call(
        functools.partial(rest_kernel, items),
        in_specs=[SMEM] + [VMEM] * 4,
        out_specs=VMEM,
        out_shape=jax.ShapeDtypeStruct((512, 1024), jnp.float32),
        compiler_params=LIMIT,
        cost_estimate=cost(512, items),
        name="rest_of_part",
    )(where, a_all, b_all, fock_columns, acc)


def update_kernel(where, flags_ref, occ_ref, virt_ref, own_ref, other_ref, amps_ref, out_ref, amps, new, sems):
    p, v, core = where[0], where[1], where[2]
    row_start = pl.multiple_of(core * 512, 512)
    load = pltpu.make_async_copy(amps_ref.at[0, :, pl.ds(row_start, 512), :], amps, sems.at[8])
    load.start()
    across = jnp.transpose(virt_ref[...])
    rows = [jnp.where(core == 0, across[:, t : t + 1], across[:, t + 4 : t + 5]) for t in range(4)]
    base = virt_ref[pl.ds(v, 1), :] - occ_ref[p]
    sums = [jnp.broadcast_to(row, (TILE, TILE)) + base for row in rows]
    load.wait()
    stores = []
    for j in range(8):
        for t in range(4):
            part = slice(t * TILE, (t + 1) * TILE)
            columns = slice(j * TILE, (j + 1) * TILE)
            keep = flags_ref[j, 4 * core + t].astype(jnp.float32)
            masked = amps[j, part, :].astype(jnp.float32) * keep
            residual = keep * (own_ref[part, columns] + other_ref[part, columns])
            new[j, part, :] = masked + residual / (sums[t] - occ_ref[j])
        store = pltpu.make_async_copy(new.at[j], out_ref.at[0, j], sems.at[j])
        store.start()
        stores.append(store)
    for store in stores:
        store.wait()


def update(where, flags, occ_energy, virt_energy, own_part, arrived, amplitudes):
    return pl.pallas_call(
        update_kernel,
        in_specs=[SMEM, SMEM, SMEM, VMEM, VMEM, VMEM, ANYWHERE],
        out_specs=ANYWHERE,
        out_shape=jax.ShapeDtypeStruct((1, 8, 512, TILE), jnp.float32),
        scratch_shapes=[
            pltpu.VMEM((8, 512, TILE), jnp.bfloat16),
            pltpu.VMEM((8, 512, TILE), jnp.float32),
            pltpu.SemaphoreType.DMA((9,)),
        ],
        compiler_params=LIMIT,
        name="update",
    )(where, flags, occ_energy, virt_energy, own_part, arrived, amplitudes)


def local(amplitudes, tile_mask, hole_integrals, virt_fock, occ_energy, virt_energy):
    p, v, r = (lax.axis_index(name) for name in AXES)
    flags = lax.dynamic_slice(tile_mask, (p, 0, 0, v), (1, 8, 8, 1)).reshape(8, 8)

    def half_of(block, half, pick):
        sizes = (1, 2, 1) + block.shape[3:]
        starts = (half, 0, pick) + (0,) * (block.ndim - 3)
        return lax.dynamic_slice(block, starts, sizes).reshape((2,) + block.shape[3:])

    def left_half(half):
        pick = (r + bit_of(v) + half) % 2
        kept = half_of(flags.reshape(2, 2, 2, 8), half, pick).astype(jnp.bfloat16)
        amps = half_of(amplitudes.reshape(2, 2, 2, 1024, TILE), half, pick)
        return amps * jnp.broadcast_to(kept[:, :, None], (2, 8, TILE)).reshape(2, 1024, 1)

    def right_half(half):
        pick = (r + bit_of(p) + half) % 2
        return half_of(hole_integrals.reshape(2, 2, 2, TILE, 8, TILE), half, pick).reshape(256, 1024)

    left = [[left_half(0), left_half(1)]]
    right = [[right_half(0), right_half(1)]]
    where = jnp.stack([p, v, r]).astype(jnp.int32)
    fock_columns = virt_fock.T
    for step in range(1, 8):
        passing = left[-1]
        if step == GATE:
            acc = add_part(None, where, left[:4], right[:4], fock_columns, FIRST)
            passing = [gate([passing[0]], [acc])[0], passing[1]]
            left[-1] = passing
        left.append([send(half, ALONG_VIRT) for half in passing])
        right.append([send(half, ALONG_PAIR) for half in right[-1]])
    acc = add_part(acc, where, left[:6], right[:6], fock_columns, SECOND)
    other_part, a_all, b_all = last_part(acc, where, left, right, fock_columns, THIRD)
    arrived = send(other_part, CORES)
    own_part = rest_of_part(acc, where, a_all, b_all, fock_columns, THIRD)
    return update(where, flags, occ_energy, virt_energy.reshape(8, TILE), own_part, arrived, amplitudes)


def solution(mesh):
    return jax.shard_map(
        local,
        mesh=mesh,
        in_specs=(
            P("pair", None, None, "virt"),
            P(),
            P("pair", None, None, "virt"),
            P("virt", None),
            P(),
            P(),
        ),
        out_specs=P("pair", None, "rep", "virt"),
        check_vma=False,
    )
```

time: 324 us -> 118 us (0.36)
  waiting for transfers between devices: 280 us -> 13.9 us
  starting transfers between devices: 0.04 us -> 63.3 us
  Pallas kernels: 0 us -> 30.3 us
  matrix products: 21.6 us -> 0 us
  between operations: 13.4 us -> 0.55 us
  local copies, waits for them, and re-layouts: 4.37 us -> 8.09 us
    all_gather x2 -> x0, waiting for transfers between devices: 280 us -> none  [the longest x1 186 us: local(): lax.all_gather(hole_integrals, 'pair', axis=0, tiled=True)]
    ppermute x0 -> x29, starting transfers between devices: none -> 63.3 us  [send(): return lax.ppermute(block, AXES, permutation)]
    pallas_call x0 -> x6, Pallas kernels: none -> 30.3 us  [the longest x2 16.2 us: add_part(): pl.pallas_call(functools.partial(part_kernel, start_from, items, count),...]
    dot_general x2 -> x0, matrix products: 21.6 us -> none  [the longest x1 15.8 us: local(): jnp.einsum('ikac,kcjb->ijab', full_amps, lax.all_gather(hole_integrals, '...]
    ppermute x0 -> x29, waiting for transfers between devices: none -> 13.9 us  [send(): return lax.ppermute(block, AXES, permutation)]
    unnamed x12 -> x67, local copies, waits for them, and re-layouts: 2.41 us -> 6.7 us
  transfers between devices with their start and end apart: 2 -> 29, of which waited for: 2 -> 10; matrix products, arithmetic and copies ran while one was open for 3% -> 1% of each run, Pallas kernels for 0% -> 18%
where the time goes in v3:
time: 118 us
  starting transfers between devices  63.3 us (54%)
  Pallas kernels  30.3 us (26%)
  waiting for transfers between devices  13.9 us (12%)
  local copies, waits for them, and re-layouts  8.09 us (7%)
  other arithmetic  1.85 us (2%)
    ppermute x29, starting transfers between devices, send(): return lax.ppermute(block, AXES, permutation)  63.3 us
    pallas_call x2, Pallas kernels, add_part(): pl.pallas_call(functools.partial(part_kernel, start_from, items, count),...  16.2 us
    ppermute x29, waiting for transfers between devices, send(): return lax.ppermute(block, AXES, permutation)  13.9 us
    pallas_call x1, Pallas kernels, last_part(): pl.pallas_call(functools.partial(last_kernel, items, count), in_specs=[SM...  7.12 us
    unnamed x67, local copies, waits for them, and re-layouts  6.7 us
    pallas_call x1, Pallas kernels, rest_of_part(): pl.pallas_call(functools.partial(rest_kernel, items), in_specs=[SMEM] + [...  4.58 us
    pallas_call x1, Pallas kernels, update(): pl.pallas_call(update_kernel, in_specs=[SMEM, SMEM, SMEM, VMEM, VMEM, VME...  2.46 us
  transfers between devices with their start and end apart: 29, of which 10 were waited for; matrix products, arithmetic and copies ran while one was open for 1% of the time, Pallas kernels for 18%

profile of v3, /device:TPU:1, one launch (start us, length us, event | category | flops | bytes accessed | tf_op | source)
XLA Modules:
  0.0 118.1 jit_solution(15055557984124566494)
XLA Ops:
  1.3 1.8 %bitcast_multiply_fusion = (bf16[2,1024,128]{2,1,0:T(8,128)(2,1)S(1)}, bf16[2,1024,128]{2,1,0:T(8,128)(2,1)S(1)}) fusion(bf16[2,2,2,1024,128]{4,3,2,1,0:T(8,128)(2,1)} %bitcast.49, s32[]{:T(128)S(6)} %select_n.67, bf16[2,1024]{1,0:T(2,128)(2,1)S(1)} %bitcast.64, bf16[2,1024]{1,0:T(2,128)(2,1)S(1)} %bitcast.65, s32[]{:T(128)S(6)} %select_n.65), kind=kLoop, calls=%fused_computation.2 | loop fusion | flops 524288 | bytes 2105352 | tf_op jit(solution)/shard_map/mul | solution.py:363
  3.1 4.7 %collective-permute-start.1 = (bf16[2,1024,128]{2,1,0:T(8,128)(2,1)S(1)}, bf16[2,1024,128]{2,1,0:T(8,128)(2,1)S(1)}, u32[]{:S(2)}, u32[]{:S(2)}) collective-permute-start(bf16[2,1024,128]{2,1,0:T(8,128)(2,1)S(1)} %get-tuple-element.13.refs_1_), channel_id=1, source_target_pairs={{0,8},{1,7},{2,4},{3,11},{4,6},{5,3},{6,0},{7,5},{8,14},{9,1},{10,... | collective-permute-start | bytes 1572872 | tf_op jit(solution)/shard_map/ppermute | solution.py:54
  9.2 2.5 %collective-permute-start.11 = (bf16[256,1024]{1,0:T(8,128)(2,1)S(1)}, bf16[256,1024]{1,0:T(8,128)(2,1)S(1)}, u32[]{:S(2)}, u32[]{:S(2)}) collective-permute-start(bf16[256,1024]{1,0:T(8,128)(2,1)S(1)} %bitcast.53), channel_id=1, source_target_pairs={{0,16},{1,49},{2,18},{3,51},{4,68},{5,53},{6,70},{7,55},{8,24},{9,... | collective-permute-start | bytes 1572872 | tf_op jit(solution)/shard_map/ppermute | solution.py:54
  11.9 3.0 %collective-permute-start.12 = (bf16[256,1024]{1,0:T(8,128)(2,1)S(1)}, bf16[256,1024]{1,0:T(8,128)(2,1)S(1)}, u32[]{:S(2)}, u32[]{:S(2)}) collective-permute-start(bf16[256,1024]{1,0:T(8,128)(2,1)S(1)} %bitcast.57), channel_id=1, source_target_pairs={{0,16},{1,49},{2,18},{3,51},{4,68},{5,53},{6,70},{7,55},{8,24},{9,... | collective-permute-start | bytes 1572872 | tf_op jit(solution)/shard_map/ppermute | solution.py:54
  14.9 2.4 %collective-permute-start.3 = (bf16[2,1024,128]{2,1,0:T(8,128)(2,1)S(1)}, bf16[2,1024,128]{2,1,0:T(8,128)(2,1)S(1)}, u32[]{:S(2)}, u32[]{:S(2)}) collective-permute-start(bf16[2,1024,128]{2,1,0:T(8,128)(2,1)S(1)} %collective-permute-done.1.refs_3_), channel_id=1, source_target_pairs={{0,8},{1,7},{2,4},{3,11},{4,6},{5,3},{6,0},{7,5},{8,14},{9,1},{10,... | collective-permute-start | bytes 1572872 | tf_op jit(solution)/shard_map/ppermute | solution.py:54
  17.9 3.4 %collective-permute-start.13 = (bf16[256,1024]{1,0:T(8,128)(2,1)S(1)}, bf16[256,1024]{1,0:T(8,128)(2,1)S(1)}, u32[]{:S(2)}, u32[]{:S(2)}) collective-permute-start(bf16[256,1024]{1,0:T(8,128)(2,1)S(1)} %collective-permute-done.11.refs_10_.refs_14_.refs_18_), channel_id=1, source_target_pairs={{0,16},{1,49},{2,18},{3,51},{4,68},{5,53},{6,70},{7,55},{8,24},{9,... | collective-permute-start | bytes 1572872 | tf_op jit(solution)/shard_map/ppermute | solution.py:54
  21.3 2.2 %collective-permute-done.12.refs_11_.refs_15_.refs_19_ = bf16[256,1024]{1,0:T(8,128)(2,1)S(1)} collective-permute-done((bf16[256,1024]{1,0:T(8,128)(2,1)S(1)}, bf16[256,1024]{1,0:T(8,128)(2,1)S(1)}, u32[]{:S(2)}, u32[]{:S(2)}) %collective-permute-start.12) | collective-permute-done | bytes 524320 | tf_op jit(solution)/shard_map/ppermute | solution.py:54
  23.5 3.4 %collective-permute-start.14 = (bf16[256,1024]{1,0:T(8,128)(2,1)S(1)}, bf16[256,1024]{1,0:T(8,128)(2,1)S(1)}, u32[]{:S(2)}, u32[]{:S(2)}) collective-permute-start(bf16[256,1024]{1,0:T(8,128)(2,1)S(1)} %collective-permute-done.12.refs_11_.refs_15_.refs_19_), channel_id=1, source_target_pairs={{0,16},{1,49},{2,18},{3,51},{4,68},{5,53},{6,70},{7,55},{8,24},{9,... | collective-permute-start | bytes 1572872 | tf_op jit(solution)/shard_map/ppermute | solution.py:54
  30.0 2.5 %collective-permute-start.15 = (bf16[256,1024]{1,0:T(8,128)(2,1)S(1)}, bf16[256,1024]{1,0:T(8,128)(2,1)S(1)}, u32[]{:S(2)}, u32[]{:S(2)}) collective-permute-start(bf16[256,1024]{1,0:T(8,128)(2,1)S(1)} %collective-permute-done.13.refs_12_.refs_16_.refs_20_), channel_id=1, source_target_pairs={{0,16},{1,49},{2,18},{3,51},{4,68},{5,53},{6,70},{7,55},{8,24},{9,... | collective-permute-start | bytes 1572872 | tf_op jit(solution)/shard_map/ppermute | solution.py:54
  32.5 2.2 %collective-permute-done.14.refs_13_.refs_17_.refs_21_ = bf16[256,1024]{1,0:T(8,128)(2,1)S(1)} collective-permute-done((bf16[256,1024]{1,0:T(8,128)(2,1)S(1)}, bf16[256,1024]{1,0:T(8,128)(2,1)S(1)}, u32[]{:S(2)}, u32[]{:S(2)}) %collective-permute-start.14) | collective-permute-done | bytes 524320 | tf_op jit(solution)/shard_map/ppermute | solution.py:54
  34.8 3.4 %collective-permute-start.16 = (bf16[256,1024]{1,0:T(8,128)(2,1)S(1)}, bf16[256,1024]{1,0:T(8,128)(2,1)S(1)}, u32[]{:S(2)}, u32[]{:S(2)}) collective-permute-start(bf16[256,1024]{1,0:T(8,128)(2,1)S(1)} %collective-permute-done.14.refs_13_.refs_17_.refs_21_), channel_id=1, source_target_pairs={{0,16},{1,49},{2,18},{3,51},{4,68},{5,53},{6,70},{7,55},{8,24},{9,... | collective-permute-start | bytes 1572872 | tf_op jit(solution)/shard_map/ppermute | solution.py:54
  39.2 1.7 %collective-permute-done.5.refs_7_ = bf16[2,1024,128]{2,1,0:T(8,128)(2,1)S(1)} collective-permute-done((bf16[2,1024,128]{2,1,0:T(8,128)(2,1)S(1)}, bf16[2,1024,128]{2,1,0:T(8,128)(2,1)S(1)}, u32[]{:S(2)}, u32[]{:S(2)}) %collective-permute-start.5) | collective-permute-done | bytes 524320 | tf_op jit(solution)/shard_map/ppermute | solution.py:54
  40.9 2.2 %collective-permute-start.7 = (bf16[2,1024,128]{2,1,0:T(8,128)(2,1)S(1)}, bf16[2,1024,128]{2,1,0:T(8,128)(2,1)S(1)}, u32[]{:S(2)}, u32[]{:S(2)}) collective-permute-start(bf16[2,1024,128]{2,1,0:T(8,128)(2,1)S(1)} %collective-permute-done.5.refs_7_), channel_id=1, source_target_pairs={{0,8},{1,7},{2,4},{3,11},{4,6},{5,3},{6,0},{7,5},{8,14},{9,1},{10,... | collective-permute-start | bytes 1572872 | tf_op jit(solution)/shard_map/ppermute | solution.py:54
  43.1 1.9 %collective-permute-start.20 = (bf16[256,1024]{1,0:T(8,128)(2,1)S(1)}, bf16[256,1024]{1,0:T(8,128)(2,1)S(1)}, u32[]{:S(2)}, u32[]{:S(2)}) collective-permute-start(bf16[256,1024]{1,0:T(8,128)(2,1)S(1)} %collective-permute-done.15.refs_14_.refs_18_.refs_22_), channel_id=1, source_target_pairs={{0,16},{1,49},{2,18},{3,51},{4,68},{5,53},{6,70},{7,55},{8,24},{9,... | collective-permute-start | bytes 1572872 | tf_op jit(solution)/shard_map/ppermute | solution.py:54
  46.0 3.4 %collective-permute-start.21 = (bf16[256,1024]{1,0:T(8,128)(2,1)S(1)}, bf16[256,1024]{1,0:T(8,128)(2,1)S(1)}, u32[]{:S(2)}, u32[]{:S(2)}) collective-permute-start(bf16[256,1024]{1,0:T(8,128)(2,1)S(1)} %collective-permute-done.16.refs_15_.refs_19_.refs_23_), channel_id=1, source_target_pairs={{0,16},{1,49},{2,18},{3,51},{4,68},{5,53},{6,70},{7,55},{8,24},{9,... | collective-permute-start | bytes 1572872 | tf_op jit(solution)/shard_map/ppermute | solution.py:54
  50.4 1.7 %collective-permute-done.7.refs_9_ = bf16[2,1024,128]{2,1,0:T(8,128)(2,1)S(1)} collective-permute-done((bf16[2,1024,128]{2,1,0:T(8,128)(2,1)S(1)}, bf16[2,1024,128]{2,1,0:T(8,128)(2,1)S(1)}, u32[]{:S(2)}, u32[]{:S(2)}) %collective-permute-start.7) | collective-permute-done | bytes 524320 | tf_op jit(solution)/shard_map/ppermute | solution.py:54
  52.1 2.2 %collective-permute-start.9 = (bf16[2,1024,128]{2,1,0:T(8,128)(2,1)S(1)}, bf16[2,1024,128]{2,1,0:T(8,128)(2,1)}, u32[]{:S(2)}, u32[]{:S(2)}) collective-permute-start(bf16[2,1024,128]{2,1,0:T(8,128)(2,1)S(1)} %collective-permute-done.7.refs_9_), channel_id=1, source_target_pairs={{0,8},{1,7},{2,4},{3,11},{4,6},{5,3},{6,0},{7,5},{8,14},{9,1},{10,... | collective-permute-start | bytes 1572872 | tf_op jit(solution)/shard_map/ppermute | solution.py:54
  54.3 1.9 %collective-permute-start.22 = (bf16[256,1024]{1,0:T(8,128)(2,1)S(1)}, bf16[256,1024]{1,0:T(8,128)(2,1)}, u32[]{:S(2)}, u32[]{:S(2)}) collective-permute-start(bf16[256,1024]{1,0:T(8,128)(2,1)S(1)} %collective-permute-done.20.refs_20_.refs_24_), channel_id=1, source_target_pairs={{0,16},{1,49},{2,18},{3,51},{4,68},{5,53},{6,70},{7,55},{8,24},{9,... | collective-permute-start | bytes 1572872 | tf_op jit(solution)/shard_map/ppermute | solution.py:54
  57.2 3.5 %collective-permute-start.23 = (bf16[256,1024]{1,0:T(8,128)(2,1)S(1)}, bf16[256,1024]{1,0:T(8,128)(2,1)}, u32[]{:S(2)}, u32[]{:S(2)}) collective-permute-start(bf16[256,1024]{1,0:T(8,128)(2,1)S(1)} %collective-permute-done.21.refs_21_.refs_25_), channel_id=1, source_target_pairs={{0,16},{1,49},{2,18},{3,51},{4,68},{5,53},{6,70},{7,55},{8,24},{9,... | collective-permute-start | bytes 1572872 | tf_op jit(solution)/shard_map/ppermute | solution.py:54
  61.6 1.8 %collective-permute-done.9.refs_11_ = bf16[2,1024,128]{2,1,0:T(8,128)(2,1)} collective-permute-done((bf16[2,1024,128]{2,1,0:T(8,128)(2,1)S(1)}, bf16[2,1024,128]{2,1,0:T(8,128)(2,1)}, u32[]{:S(2)}, u32[]{:S(2)}) %collective-permute-start.9) | collective-permute-done | bytes 524320 | tf_op jit(solution)/shard_map/ppermute | solution.py:54
  63.5 2.2 %collective-permute-start.17 = (bf16[2,1024,128]{2,1,0:T(8,128)(2,1)}, bf16[2,1024,128]{2,1,0:T(8,128)(2,1)S(1)}, u32[]{:S(2)}, u32[]{:S(2)}) collective-permute-start(bf16[2,1024,128]{2,1,0:T(8,128)(2,1)} %collective-permute-done.9.refs_11_), channel_id=1, source_target_pairs={{0,8},{1,7},{2,4},{3,11},{4,6},{5,3},{6,0},{7,5},{8,14},{9,1},{10,... | collective-permute-start | bytes 1572872 | tf_op jit(solution)/shard_map/ppermute | solution.py:54
  65.7 1.9 %collective-permute-start.24 = (bf16[256,1024]{1,0:T(8,128)(2,1)}, bf16[256,1024]{1,0:T(8,128)(2,1)S(1)}, u32[]{:S(2)}, u32[]{:S(2)}) collective-permute-start(bf16[256,1024]{1,0:T(8,128)(2,1)} %collective-permute-done.22.refs_22_.refs_26_), channel_id=1, source_target_pairs={{0,16},{1,49},{2,18},{3,51},{4,68},{5,53},{6,70},{7,55},{8,24},{9,... | collective-permute-start | bytes 1572872 | tf_op jit(solution)/shard_map/ppermute | solution.py:54
  68.5 3.5 %collective-permute-start.25 = (bf16[256,1024]{1,0:T(8,128)(2,1)}, bf16[256,1024]{1,0:T(8,128)(2,1)S(1)}, u32[]{:S(2)}, u32[]{:S(2)}) collective-permute-start(bf16[256,1024]{1,0:T(8,128)(2,1)} %collective-permute-done.23.refs_23_.refs_27_), channel_id=1, source_target_pairs={{0,16},{1,49},{2,18},{3,51},{4,68},{5,53},{6,70},{7,55},{8,24},{9,... | collective-permute-start | bytes 1572872 | tf_op jit(solution)/shard_map/ppermute | solution.py:54
  73.6 7.2 %add_part.2.refs_1_.refs_25_ = f32[1024,1024]{1,0:T(8,128)S(1)} custom-call(s32[3]{0:T(128)S(1)} %pad_add_fusion.where, bf16[2,1024,128]{2,1,0:T(8,128)(2,1)} %copy-done.11, bf16[2,1024,128]{2,1,0:T(8,128)(2,1)} %copy-done.10, bf16[2,1024,128]{2,1,0:T(8,128)(2,1)} %copy-done.15, bf16[2,1024,128]{2,1,0:T(8,128)(2,1)} %copy-done.12, ...), custom_call_target="tpu_custom_call" | custom-call | flops 2684354560 | bytes 4194304 | tf_op jit(solution)/shard_map/add_part/pallas_call | solution.py:257
  80.9 2.0 %copy-done.1 = f32[1024,1024]{1,0:T(8,128)} copy-done((f32[1024,1024]{1,0:T(8,128)}, f32[1024,1024]{1,0:T(8,128)S(1)}, u32[]{:S(2)}) %copy-start.1) | copy-done | bytes 4194328
  82.9 2.2 %collective-permute-start.26 = (bf16[256,1024]{1,0:T(8,128)(2,1)S(1)}, bf16[256,1024]{1,0:T(8,128)(2,1)}, u32[]{:S(2)}, u32[]{:S(2)}) collective-permute-start(bf16[256,1024]{1,0:T(8,128)(2,1)S(1)} %collective-permute-done.24.refs_28_), channel_id=1, source_target_pairs={{0,16},{1,49},{2,18},{3,51},{4,68},{5,53},{6,70},{7,55},{8,24},{9,... | collective-permute-start | bytes 1572872 | tf_op jit(solution)/shard_map/ppermute | solution.py:54
  87.1 2.2 %copy-done.2 = f32[1024,1024]{1,0:T(8,128)S(1)} copy-done((f32[1024,1024]{1,0:T(8,128)S(1)}, f32[1024,1024]{1,0:T(8,128)}, u32[]{:S(2)}) %copy-start.2) | copy-done | bytes 4194328
  89.3 9.0 %add_part.3.refs_33_.acc_ref = f32[1024,1024]{1,0:T(8,128)S(1)} custom-call(s32[3]{0:T(128)S(1)} %pad_add_fusion.where, bf16[2,1024,128]{2,1,0:T(8,128)(2,1)} %copy-done.11, bf16[2,1024,128]{2,1,0:T(8,128)(2,1)} %copy-done.10, bf16[2,1024,128]{2,1,0:T(8,128)(2,1)} %copy-done.15, bf16[2,1024,128]{2,1,0:T(8,128)(2,1)} %copy-done.12, ...), custom_call_target="tpu_custom_call", output_to_operand_aliasing={{}: (26, {})} | custom-call | flops 3355443200 | bytes 5242880 | tf_op jit(solution)/shard_map/add_part/pallas_call | solution.py:257
  98.3 7.1 %last_part.1 = (f32[512,1024]{1,0:T(8,128)S(1)}, bf16[1024,1792]{1,0:T(8,128)(2,1)S(1)}, bf16[1792,1024]{1,0:T(8,128)(2,1)S(1)}) custom-call(s32[3]{0:T(128)S(1)} %pad_add_fusion.where, bf16[2,1024,128]{2,1,0:T(8,128)(2,1)} %copy-done.11, bf16[2,1024,128]{2,1,0:T(8,128)(2,1)} %copy-done.10, bf16[2,1024,128]{2,1,0:T(8,128)(2,1)} %copy-done.15, ...), custom_call_target="tpu_custom_call" | custom-call | flops 2348810240 | bytes 7340032 | tf_op jit(solution)/shard_map/last_part/pallas_call | solution.py:277
  105.4 5.4 %collective-permute-start.28 = (f32[512,1024]{1,0:T(8,128)S(1)}, f32[512,1024]{1,0:T(8,128)S(1)}, u32[]{:S(2)}, u32[]{:S(2)}) collective-permute-start(f32[512,1024]{1,0:T(8,128)S(1)} %get-tuple-element.10), channel_id=1, source_target_pairs={{0,1},{1,0},{2,3},{3,2},{4,5},{5,4},{6,7},{7,6},{8,9},{9,8},{10,11... | collective-permute-start | bytes 6291464 | tf_op jit(solution)/shard_map/ppermute | solution.py:54
  110.8 4.6 %rest_of_part.1.own_ref = f32[512,1024]{1,0:T(8,128)S(1)} custom-call(s32[3]{0:T(128)S(1)} %pad_add_fusion.where, bf16[1024,1792]{1,0:T(8,128)(2,1)S(1)} %get-tuple-element.8.a_all, bf16[1792,1024]{1,0:T(8,128)(2,1)S(1)} %get-tuple-element.9.b_all, bf16[1024,128]{1,0:T(8,128)(2,1)S(1)} %bitcast.48, f32[1024,1024]{1,0:T(8,128)S(1)} %add_part.3.refs_33_.acc_ref), custom_call_target="tpu_custom_call" | custom-call | flops 2348810240 | bytes 7340032 | tf_op jit(solution)/shard_map/rest_of_part/pallas_call | solution.py:297
  115.4 2.5 %update.1 = f32[1,8,512,128]{3,2,1,0:T(8,128)} custom-call(s32[3]{0:T(128)S(1)} %pad_add_fusion.where, s32[8,8]{1,0:T(8,128)S(1)} %bitcast.51, f32[8]{0:T(128)S(1)} %copy-done.7, f32[8,128]{1,0:T(8,128)S(1)} %bitcast.52, f32[512,1024]{1,0:T(8,128)S(1)} %rest_of_part.1.own_ref, f32[512,1024]{1,0:T(8,128)S(1)} %collective-permute-done.28.other_ref, ...), custom_call_target="tpu_custom_call" | custom-call | tf_op jit(solution)/shard_map/update/pallas_call | solution.py:335
  (104 shorter events, 15.9 us)
Async XLA Ops:
  3.1 11.8 %collective-permute-start.1 = (bf16[2,1024,128]{2,1,0:T(8,128)(2,1)S(1)}, bf16[2,1024,128]{2,1,0:T(8,128)(2,1)S(1)}, u32[]{:S(2)}, u32[]{:S(2)}) collective-permute-start(bf16[2,1024,128]{2,1,0:T(8,128)(2,1)S(1)} %get-tuple-element.13.refs_1_), channel_id=1, source_target_pairs={{0,8},{1,7},{2,4},{3,11},{4,6},{5,3},{6,0},{7,5},{8,14},{9,1},{10,... | collective-permute-start | bytes 1572872 | tf_op jit(solution)/shard_map/ppermute | solution.py:54
  7.8 65.6 %copy-start.28 = (bf16[128,1024]{1,0:T(8,128)(2,1)S(1)}, bf16[128,1024]{1,0:T(8,128)(2,1)}, u32[]{:S(2)}) copy-start(bf16[128,1024]{1,0:T(8,128)(2,1)} %param.9) | copy-start | bytes 786436
  9.2 64.4 %copy-start.8 = (bf16[32,8,8,128]{3,1,2,0:T(8,128)(2,1)}, bf16[32,8,8,128]{3,1,2,0:T(8,128)(2,1)S(1)}, u32[]{:S(2)}) copy-start(bf16[32,8,8,128]{3,1,2,0:T(8,128)(2,1)S(1)} %copy.39) | copy-start | bytes 1572868
  9.2 8.7 %collective-permute-start.11 = (bf16[256,1024]{1,0:T(8,128)(2,1)S(1)}, bf16[256,1024]{1,0:T(8,128)(2,1)S(1)}, u32[]{:S(2)}, u32[]{:S(2)}) collective-permute-start(bf16[256,1024]{1,0:T(8,128)(2,1)S(1)} %bitcast.53), channel_id=1, source_target_pairs={{0,16},{1,49},{2,18},{3,51},{4,68},{5,53},{6,70},{7,55},{8,24},{9,... | collective-permute-start | bytes 1572872 | tf_op jit(solution)/shard_map/ppermute | solution.py:54
  11.9 60.1 %copy-start.9 = (bf16[32,8,8,128]{3,1,2,0:T(8,128)(2,1)}, bf16[32,8,8,128]{3,1,2,0:T(8,128)(2,1)S(1)}, u32[]{:S(2)}) copy-start(bf16[32,8,8,128]{3,1,2,0:T(8,128)(2,1)S(1)} %copy.38) | copy-start | bytes 1572868
  11.9 11.6 %collective-permute-start.12 = (bf16[256,1024]{1,0:T(8,128)(2,1)S(1)}, bf16[256,1024]{1,0:T(8,128)(2,1)S(1)}, u32[]{:S(2)}, u32[]{:S(2)}) collective-permute-start(bf16[256,1024]{1,0:T(8,128)(2,1)S(1)} %bitcast.57), channel_id=1, source_target_pairs={{0,16},{1,49},{2,18},{3,51},{4,68},{5,53},{6,70},{7,55},{8,24},{9,... | collective-permute-start | bytes 1572872 | tf_op jit(solution)/shard_map/ppermute | solution.py:54
  14.9 12.1 %collective-permute-start = (bf16[2,1024,128]{2,1,0:T(8,128)(2,1)S(1)}, bf16[2,1024,128]{2,1,0:T(8,128)(2,1)S(1)}, u32[]{:S(2)}, u32[]{:S(2)}) collective-permute-start(bf16[2,1024,128]{2,1,0:T(8,128)(2,1)S(1)} %get-tuple-element.14.refs_0_), channel_id=1, source_target_pairs={{0,8},{1,7},{2,4},{3,11},{4,6},{5,3},{6,0},{7,5},{8,14},{9,1},{10,... | collective-permute-start | bytes 1572872 | tf_op jit(solution)/shard_map/ppermute | solution.py:54
  14.9 13.9 %collective-permute-start.3 = (bf16[2,1024,128]{2,1,0:T(8,128)(2,1)S(1)}, bf16[2,1024,128]{2,1,0:T(8,128)(2,1)S(1)}, u32[]{:S(2)}, u32[]{:S(2)}) collective-permute-start(bf16[2,1024,128]{2,1,0:T(8,128)(2,1)S(1)} %collective-permute-done.1.refs_3_), channel_id=1, source_target_pairs={{0,8},{1,7},{2,4},{3,11},{4,6},{5,3},{6,0},{7,5},{8,14},{9,1},{10,... | collective-permute-start | bytes 1572872 | tf_op jit(solution)/shard_map/ppermute | solution.py:54
  17.9 12.1 %collective-permute-start.13 = (bf16[256,1024]{1,0:T(8,128)(2,1)S(1)}, bf16[256,1024]{1,0:T(8,128)(2,1)S(1)}, u32[]{:S(2)}, u32[]{:S(2)}) collective-permute-start(bf16[256,1024]{1,0:T(8,128)(2,1)S(1)} %collective-permute-done.11.refs_10_.refs_14_.refs_18_), channel_id=1, source_target_pairs={{0,16},{1,49},{2,18},{3,51},{4,68},{5,53},{6,70},{7,55},{8,24},{9,... | collective-permute-start | bytes 1572872 | tf_op jit(solution)/shard_map/ppermute | solution.py:54
  23.5 11.2 %collective-permute-start.14 = (bf16[256,1024]{1,0:T(8,128)(2,1)S(1)}, bf16[256,1024]{1,0:T(8,128)(2,1)S(1)}, u32[]{:S(2)}, u32[]{:S(2)}) collective-permute-start(bf16[256,1024]{1,0:T(8,128)(2,1)S(1)} %collective-permute-done.12.refs_11_.refs_15_.refs_19_), channel_id=1, source_target_pairs={{0,16},{1,49},{2,18},{3,51},{4,68},{5,53},{6,70},{7,55},{8,24},{9,... | collective-permute-start | bytes 1572872 | tf_op jit(solution)/shard_map/ppermute | solution.py:54
  26.9 11.2 %collective-permute-start.2 = (bf16[2,1024,128]{2,1,0:T(8,128)(2,1)S(1)}, bf16[2,1024,128]{2,1,0:T(8,128)(2,1)S(1)}, u32[]{:S(2)}, u32[]{:S(2)}) collective-permute-start(bf16[2,1024,128]{2,1,0:T(8,128)(2,1)S(1)} %collective-permute-done.refs_2_), channel_id=1, source_target_pairs={{0,8},{1,7},{2,4},{3,11},{4,6},{5,3},{6,0},{7,5},{8,14},{9,1},{10,... | collective-permute-start | bytes 1572872 | tf_op jit(solution)/shard_map/ppermute | solution.py:54
  28.8 12.1 %collective-permute-start.5 = (bf16[2,1024,128]{2,1,0:T(8,128)(2,1)S(1)}, bf16[2,1024,128]{2,1,0:T(8,128)(2,1)S(1)}, u32[]{:S(2)}, u32[]{:S(2)}) collective-permute-start(bf16[2,1024,128]{2,1,0:T(8,128)(2,1)S(1)} %collective-permute-done.3.refs_5_), channel_id=1, source_target_pairs={{0,8},{1,7},{2,4},{3,11},{4,6},{5,3},{6,0},{7,5},{8,14},{9,1},{10,... | collective-permute-start | bytes 1572872 | tf_op jit(solution)/shard_map/ppermute | solution.py:54
  30.0 13.1 %collective-permute-start.15 = (bf16[256,1024]{1,0:T(8,128)(2,1)S(1)}, bf16[256,1024]{1,0:T(8,128)(2,1)S(1)}, u32[]{:S(2)}, u32[]{:S(2)}) collective-permute-start(bf16[256,1024]{1,0:T(8,128)(2,1)S(1)} %collective-permute-done.13.refs_12_.refs_16_.refs_20_), channel_id=1, source_target_pairs={{0,16},{1,49},{2,18},{3,51},{4,68},{5,53},{6,70},{7,55},{8,24},{9,... | collective-permute-start | bytes 1572872 | tf_op jit(solution)/shard_map/ppermute | solution.py:54
  34.8 11.2 %collective-permute-start.16 = (bf16[256,1024]{1,0:T(8,128)(2,1)S(1)}, bf16[256,1024]{1,0:T(8,128)(2,1)S(1)}, u32[]{:S(2)}, u32[]{:S(2)}) collective-permute-start(bf16[256,1024]{1,0:T(8,128)(2,1)S(1)} %collective-permute-done.14.refs_13_.refs_17_.refs_21_), channel_id=1, source_target_pairs={{0,16},{1,49},{2,18},{3,51},{4,68},{5,53},{6,70},{7,55},{8,24},{9,... | collective-permute-start | bytes 1572872 | tf_op jit(solution)/shard_map/ppermute | solution.py:54
  38.2 11.2 %collective-permute-start.4 = (bf16[2,1024,128]{2,1,0:T(8,128)(2,1)S(1)}, bf16[2,1024,128]{2,1,0:T(8,128)(2,1)S(1)}, u32[]{:S(2)}, u32[]{:S(2)}) collective-permute-start(bf16[2,1024,128]{2,1,0:T(8,128)(2,1)S(1)} %collective-permute-done.2.refs_4_), channel_id=1, source_target_pairs={{0,8},{1,7},{2,4},{3,11},{4,6},{5,3},{6,0},{7,5},{8,14},{9,1},{10,... | collective-permute-start | bytes 1572872 | tf_op jit(solution)/shard_map/ppermute | solution.py:54
  40.9 11.2 %collective-permute-start.7 = (bf16[2,1024,128]{2,1,0:T(8,128)(2,1)S(1)}, bf16[2,1024,128]{2,1,0:T(8,128)(2,1)S(1)}, u32[]{:S(2)}, u32[]{:S(2)}) collective-permute-start(bf16[2,1024,128]{2,1,0:T(8,128)(2,1)S(1)} %collective-permute-done.5.refs_7_), channel_id=1, source_target_pairs={{0,8},{1,7},{2,4},{3,11},{4,6},{5,3},{6,0},{7,5},{8,14},{9,1},{10,... | collective-permute-start | bytes 1572872 | tf_op jit(solution)/shard_map/ppermute | solution.py:54
  43.1 11.2 %collective-permute-start.20 = (bf16[256,1024]{1,0:T(8,128)(2,1)S(1)}, bf16[256,1024]{1,0:T(8,128)(2,1)S(1)}, u32[]{:S(2)}, u32[]{:S(2)}) collective-permute-start(bf16[256,1024]{1,0:T(8,128)(2,1)S(1)} %collective-permute-done.15.refs_14_.refs_18_.refs_22_), channel_id=1, source_target_pairs={{0,16},{1,49},{2,18},{3,51},{4,68},{5,53},{6,70},{7,55},{8,24},{9,... | collective-permute-start | bytes 1572872 | tf_op jit(solution)/shard_map/ppermute | solution.py:54
  46.0 11.2 %collective-permute-start.21 = (bf16[256,1024]{1,0:T(8,128)(2,1)S(1)}, bf16[256,1024]{1,0:T(8,128)(2,1)S(1)}, u32[]{:S(2)}, u32[]{:S(2)}) collective-permute-start(bf16[256,1024]{1,0:T(8,128)(2,1)S(1)} %collective-permute-done.16.refs_15_.refs_19_.refs_23_), channel_id=1, source_target_pairs={{0,16},{1,49},{2,18},{3,51},{4,68},{5,53},{6,70},{7,55},{8,24},{9,... | collective-permute-start | bytes 1572872 | tf_op jit(solution)/shard_map/ppermute | solution.py:54
  49.4 11.3 %collective-permute-start.6 = (bf16[2,1024,128]{2,1,0:T(8,128)(2,1)S(1)}, bf16[2,1024,128]{2,1,0:T(8,128)(2,1)S(1)}, u32[]{:S(2)}, u32[]{:S(2)}) collective-permute-start(bf16[2,1024,128]{2,1,0:T(8,128)(2,1)S(1)} %collective-permute-done.4.refs_6_), channel_id=1, source_target_pairs={{0,8},{1,7},{2,4},{3,11},{4,6},{5,3},{6,0},{7,5},{8,14},{9,1},{10,... | collective-permute-start | bytes 1572872 | tf_op jit(solution)/shard_map/ppermute | solution.py:54
  52.1 11.3 %collective-permute-start.9 = (bf16[2,1024,128]{2,1,0:T(8,128)(2,1)S(1)}, bf16[2,1024,128]{2,1,0:T(8,128)(2,1)}, u32[]{:S(2)}, u32[]{:S(2)}) collective-permute-start(bf16[2,1024,128]{2,1,0:T(8,128)(2,1)S(1)} %collective-permute-done.7.refs_9_), channel_id=1, source_target_pairs={{0,8},{1,7},{2,4},{3,11},{4,6},{5,3},{6,0},{7,5},{8,14},{9,1},{10,... | collective-permute-start | bytes 1572872 | tf_op jit(solution)/shard_map/ppermute | solution.py:54
  54.3 11.3 %collective-permute-start.22 = (bf16[256,1024]{1,0:T(8,128)(2,1)S(1)}, bf16[256,1024]{1,0:T(8,128)(2,1)}, u32[]{:S(2)}, u32[]{:S(2)}) collective-permute-start(bf16[256,1024]{1,0:T(8,128)(2,1)S(1)} %collective-permute-done.20.refs_20_.refs_24_), channel_id=1, source_target_pairs={{0,16},{1,49},{2,18},{3,51},{4,68},{5,53},{6,70},{7,55},{8,24},{9,... | collective-permute-start | bytes 1572872 | tf_op jit(solution)/shard_map/ppermute | solution.py:54
  57.2 11.2 %collective-permute-start.23 = (bf16[256,1024]{1,0:T(8,128)(2,1)S(1)}, bf16[256,1024]{1,0:T(8,128)(2,1)}, u32[]{:S(2)}, u32[]{:S(2)}) collective-permute-start(bf16[256,1024]{1,0:T(8,128)(2,1)S(1)} %collective-permute-done.21.refs_21_.refs_25_), channel_id=1, source_target_pairs={{0,16},{1,49},{2,18},{3,51},{4,68},{5,53},{6,70},{7,55},{8,24},{9,... | collective-permute-start | bytes 1572872 | tf_op jit(solution)/shard_map/ppermute | solution.py:54
  60.7 11.2 %collective-permute-start.8 = (bf16[2,1024,128]{2,1,0:T(8,128)(2,1)S(1)}, bf16[2,1024,128]{2,1,0:T(8,128)(2,1)}, u32[]{:S(2)}, u32[]{:S(2)}) collective-permute-start(bf16[2,1024,128]{2,1,0:T(8,128)(2,1)S(1)} %collective-permute-done.6.refs_8_), channel_id=1, source_target_pairs={{0,8},{1,7},{2,4},{3,11},{4,6},{5,3},{6,0},{7,5},{8,14},{9,1},{10,... | collective-permute-start | bytes 1572872 | tf_op jit(solution)/shard_map/ppermute | solution.py:54
  63.5 19.4 %collective-permute-start.17 = (bf16[2,1024,128]{2,1,0:T(8,128)(2,1)}, bf16[2,1024,128]{2,1,0:T(8,128)(2,1)S(1)}, u32[]{:S(2)}, u32[]{:S(2)}) collective-permute-start(bf16[2,1024,128]{2,1,0:T(8,128)(2,1)} %collective-permute-done.9.refs_11_), channel_id=1, source_target_pairs={{0,8},{1,7},{2,4},{3,11},{4,6},{5,3},{6,0},{7,5},{8,14},{9,1},{10,... | collective-permute-start | bytes 1572872 | tf_op jit(solution)/shard_map/ppermute | solution.py:54
  65.7 17.2 %collective-permute-start.24 = (bf16[256,1024]{1,0:T(8,128)(2,1)}, bf16[256,1024]{1,0:T(8,128)(2,1)S(1)}, u32[]{:S(2)}, u32[]{:S(2)}) collective-permute-start(bf16[256,1024]{1,0:T(8,128)(2,1)} %collective-permute-done.22.refs_22_.refs_26_), channel_id=1, source_target_pairs={{0,16},{1,49},{2,18},{3,51},{4,68},{5,53},{6,70},{7,55},{8,24},{9,... | collective-permute-start | bytes 1572872 | tf_op jit(solution)/shard_map/ppermute | solution.py:54
  68.5 16.6 %collective-permute-start.25 = (bf16[256,1024]{1,0:T(8,128)(2,1)}, bf16[256,1024]{1,0:T(8,128)(2,1)S(1)}, u32[]{:S(2)}, u32[]{:S(2)}) collective-permute-start(bf16[256,1024]{1,0:T(8,128)(2,1)} %collective-permute-done.23.refs_23_.refs_27_), channel_id=1, source_target_pairs={{0,16},{1,49},{2,18},{3,51},{4,68},{5,53},{6,70},{7,55},{8,24},{9,... | collective-permute-start | bytes 1572872 | tf_op jit(solution)/shard_map/ppermute | solution.py:54
  72.1 14.1 %collective-permute-start.10 = (bf16[2,1024,128]{2,1,0:T(8,128)(2,1)}, bf16[2,1024,128]{2,1,0:T(8,128)(2,1)S(1)}, u32[]{:S(2)}, u32[]{:S(2)}) collective-permute-start(bf16[2,1024,128]{2,1,0:T(8,128)(2,1)} %collective-permute-done.8.refs_10_), channel_id=1, source_target_pairs={{0,8},{1,7},{2,4},{3,11},{4,6},{5,3},{6,0},{7,5},{8,14},{9,1},{10,... | collective-permute-start | bytes 1572872 | tf_op jit(solution)/shard_map/ppermute | solution.py:54
  82.9 15.4 %collective-permute-start.19 = (bf16[2,1024,128]{2,1,0:T(8,128)(2,1)S(1)}, bf16[2,1024,128]{2,1,0:T(8,128)(2,1)S(1)}, u32[]{:S(2)}, u32[]{:S(2)}) collective-permute-start(bf16[2,1024,128]{2,1,0:T(8,128)(2,1)S(1)} %collective-permute-done.17.refs_13_), channel_id=1, source_target_pairs={{0,8},{1,7},{2,4},{3,11},{4,6},{5,3},{6,0},{7,5},{8,14},{9,1},{10,... | collective-permute-start | bytes 1572872 | tf_op jit(solution)/shard_map/ppermute | solution.py:54
  82.9 15.4 %collective-permute-start.26 = (bf16[256,1024]{1,0:T(8,128)(2,1)S(1)}, bf16[256,1024]{1,0:T(8,128)(2,1)}, u32[]{:S(2)}, u32[]{:S(2)}) collective-permute-start(bf16[256,1024]{1,0:T(8,128)(2,1)S(1)} %collective-permute-done.24.refs_28_), channel_id=1, source_target_pairs={{0,16},{1,49},{2,18},{3,51},{4,68},{5,53},{6,70},{7,55},{8,24},{9,... | collective-permute-start | bytes 1572872 | tf_op jit(solution)/shard_map/ppermute | solution.py:54
  85.1 13.2 %collective-permute-start.27 = (bf16[256,1024]{1,0:T(8,128)(2,1)S(1)}, bf16[256,1024]{1,0:T(8,128)(2,1)}, u32[]{:S(2)}, u32[]{:S(2)}) collective-permute-start(bf16[256,1024]{1,0:T(8,128)(2,1)S(1)} %collective-permute-done.25.refs_29_), channel_id=1, source_target_pairs={{0,16},{1,49},{2,18},{3,51},{4,68},{5,53},{6,70},{7,55},{8,24},{9,... | collective-permute-start | bytes 1572872 | tf_op jit(solution)/shard_map/ppermute | solution.py:54
  87.1 11.2 %collective-permute-start.18 = (bf16[2,1024,128]{2,1,0:T(8,128)(2,1)}, bf16[2,1024,128]{2,1,0:T(8,128)(2,1)S(1)}, u32[]{:S(2)}, u32[]{:S(2)}) collective-permute-start(bf16[2,1024,128]{2,1,0:T(8,128)(2,1)} %gate.1.refs_12_), channel_id=1, source_target_pairs={{0,8},{1,7},{2,4},{3,11},{4,6},{5,3},{6,0},{7,5},{8,14},{9,1},{10,... | collective-permute-start | bytes 1572872 | tf_op jit(solution)/shard_map/ppermute | solution.py:54
  105.4 10.0 %collective-permute-start.28 = (f32[512,1024]{1,0:T(8,128)S(1)}, f32[512,1024]{1,0:T(8,128)S(1)}, u32[]{:S(2)}, u32[]{:S(2)}) collective-permute-start(f32[512,1024]{1,0:T(8,128)S(1)} %get-tuple-element.10), channel_id=1, source_target_pairs={{0,1},{1,0},{2,3},{3,2},{4,5},{5,4},{6,7},{7,6},{8,9},{9,8},{10,11... | collective-permute-start | bytes 6291464 | tf_op jit(solution)/shard_map/ppermute | solution.py:54
  (26 other events, 566.5 us)

commit v4 on v3

--- a/solution.py
+++ b/solution.py
@@ -8,7 +8,10 @@
 from jax.sharding import PartitionSpec as P
 
 TILE = 128
-GATE, STAY = 7, 6
+LIM = 20
+EG = ((0, 3), (3, 9))
+LG = ((0, 2), (2, 7))
+WIDTH, STAY = 1024, 6
 AXES = ("pair", "virt", "rep")
 
 
@@ -83,9 +86,9 @@
             yield t, 2 * i + t, self.v[2 * i + t], second, k
 
 
-def start_left(tiles, left, a_all, sems, row_start, rows):
+def start_left(tiles, left, a_all, sems, row_start, rows, some):
     part = pl.ds(row_start, rows)
-    for item in range(len(tiles.items)):
+    for item in some:
         for t, q, _, _, k in tiles.pairs(item):
             for half in range(2):
 
@@ -109,8 +112,8 @@
     return wait
 
 
-def start_right(tiles, right, b_all, sems):
-    for item in range(len(tiles.items)):
+def start_right(tiles, right, b_all, sems, some):
+    for item in some:
         j = tiles.items[item][1]
         for t, _, v, second, _ in tiles.pairs(item):
             for which in range(2):
@@ -137,22 +140,27 @@
     return wait
 
 
-def multiply(tiles, fock_ref, acc_ref, out_ref, a_all, b_all, row_start):
-    rows, width, block = out_ref.shape[0], 256, 512
+def multiply(tiles, some, fock_ref, acc_ref, out_ref, a_all, b_all, row_start):
+    rows, width, block = out_ref.shape[0], WIDTH, 512
+    depth = slice(some[0] * 256, (some[-1] + 1) * 256)
 
     def columns_of(step, carry):
         columns = pl.ds(pl.multiple_of(step * width, width), width)
         for row in range(0, rows, block):
             source = pl.ds(row_start + row, block)
-            total = jnp.dot(a_all[source, :], b_all[:, columns], preferred_element_type=jnp.float32)
-            if acc_ref is not None:
+            total = jnp.dot(
+                a_all[source, depth], b_all[depth, columns], preferred_element_type=jnp.float32
+            )
+            if acc_ref is out_ref:
+                total += out_ref[pl.ds(row, block), columns]
+            elif acc_ref is not None:
                 total += acc_ref[source, columns]
             out_ref[pl.ds(row, block), columns] = total
         return carry
 
     lax.fori_loop(0, 1024 // width, columns_of, 0)
     blank = jnp.zeros((TILE, TILE), jnp.bfloat16)
-    for item in range(len(tiles.items)):
+    for item in some:
         fock, places = [], []
         for t, _, v, _, k in tiles.pairs(item):
             own = fock_ref[pl.ds(pl.multiple_of(v * TILE, TILE), TILE), :]
@@ -167,72 +175,62 @@
                 out_ref[part, places[t]] += total[:, t * TILE : (t + 1) * TILE]
 
 
-def gate_kernel(*refs):
-    pass
-
-
-def gate(passed, after):
-    return pl.pallas_call(
-        gate_kernel,
-        out_shape=[jax.ShapeDtypeStruct(x.shape, x.dtype) for x in passed],
-        in_specs=[ANYWHERE] * (len(passed) + len(after)),
-        out_specs=[ANYWHERE] * len(passed),
-        input_output_aliases={i: i for i in range(len(passed))},
-        name="gate",
-    )(*passed, *after)
-
-
 def paired(refs):
     return [refs[n : n + 2] for n in range(0, len(refs), 2)]
 
 
-def part_kernel(start_from, items, count, where, *refs):
+def early_kernel(items, count, where, *refs):
     left, right = paired(refs[: 2 * count]), paired(refs[2 * count : 4 * count])
-    fock_ref, refs = refs[4 * count], refs[4 * count + 1 :]
-    acc_ref = None
-    if start_from:
-        acc_ref, refs = refs[0], refs[1:]
-    out_ref, a_all, b_all, left_sems, right_sems = refs
+    fock_ref, out_ref, a_all, b_all, left_sems, right_sems = refs[4 * count :]
     tiles = Tiles(where, items)
-    wait_right = start_right(tiles, right, b_all, right_sems)
-    wait_left = start_left(tiles, left, a_all, left_sems, 0, 1024)
-    for item in range(len(items)):
-        wait_right(item)
-        wait_left(item)
-    multiply(tiles, fock_ref, acc_ref, out_ref, a_all, b_all, 0)
+    waits = []
+    for some in EARLY_GROUPS:
+        wait_right = start_right(tiles, right, b_all, right_sems, some)
+        wait_left = start_left(tiles, left, a_all, left_sems, 0, 1024, some)
+        waits.append((wait_right, wait_left))
+    for some, (wait_right, wait_left) in zip(EARLY_GROUPS, waits):
+        for item in some:
+            wait_right(item)
+            wait_left(item)
+        source = out_ref if some[0] else None
+        multiply(tiles, some, fock_ref, source, out_ref, a_all, b_all, 0)
 
 
 def last_kernel(items, count, where, *refs):
     left, right = paired(refs[: 2 * count]), paired(refs[2 * count : 4 * count])
     fock_ref, acc_ref, out_ref, a_all, b_all, left_sems, right_sems = refs[4 * count :]
     tiles = Tiles(where, items)
-    wait_right = start_right(tiles, right, b_all, right_sems)
     row_start = pl.multiple_of((1 - where[2]) * 512, 512)
-    wait_left = start_left(tiles, left, a_all, left_sems.at[0], row_start, 512)
-    kept = pl.multiple_of(where[2] * 512, 512)
-    wait_kept = start_left(tiles, left, a_all, left_sems.at[1], kept, 512)
-    for item in range(len(items)):
-        wait_right(item)
-        wait_left(item)
-    multiply(tiles, fock_ref, acc_ref, out_ref, a_all, b_all, row_start)
-    for item in range(len(items)):
-        wait_kept(item)
+    waits = []
+    for some in LAST_GROUPS:
+        wait_right = start_right(tiles, right, b_all, right_sems, some)
+        wait_left = start_left(tiles, left, a_all, left_sems, 0, 1024, some)
+        waits.append((wait_right, wait_left))
+    for some, (wait_right, wait_left) in zip(LAST_GROUPS, waits):
+        for item in some:
+            wait_right(item)
+            wait_left(item)
+        source = out_ref if some[0] else acc_ref
+        multiply(tiles, some, fock_ref, source, out_ref, a_all, b_all, row_start)
 
 
 def rest_kernel(items, where, a_all, b_all, fock_ref, acc_ref, out_ref):
     tiles = Tiles(where, items)
     row_start = pl.multiple_of(where[2] * 512, 512)
-    multiply(tiles, fock_ref, acc_ref, out_ref, a_all, b_all, row_start)
+    multiply(tiles, range(len(items)), fock_ref, acc_ref, out_ref, a_all, b_all, row_start)
 
 
 ANYWHERE = pl.BlockSpec(memory_space=pl.ANY)
 HBM = pl.BlockSpec(memory_space=pltpu.HBM)
 VMEM = pl.BlockSpec(memory_space=pltpu.VMEM)
 SMEM = pl.BlockSpec(memory_space=pltpu.SMEM)
-LIMIT = pltpu.CompilerParams(vmem_limit_bytes=16 * 2**20)
+LIMIT = pltpu.CompilerParams(vmem_limit_bytes=LIM * 2**20)
 FIRST = ((0, 0), (0, 1), (1, 0), (1, 1))
 SECOND = ((0, 2), (2, 0), (1, 2), (2, 1), (2, 2))
 THIRD = ((0, 3), (3, 0), (1, 3), (3, 1), (2, 3), (3, 2), (3, 3))
+
+EARLY_GROUPS = tuple(range(n, m) for n, m in EG)
+LAST_GROUPS = tuple(range(n, m) for n, m in LG)
 
 
 def cost(rows, items):
@@ -251,12 +249,11 @@
     ]
 
 
-def add_part(acc, where, left, right, fock_columns, items):
-    start_from = acc is not None
+def early_part(where, left, right, fock_columns, items):
     count = len(left)
     return pl.pallas_call(
-        functools.partial(part_kernel, start_from, items, count),
-        in_specs=[SMEM] + [HBM] * 4 * count + [VMEM] * (1 + start_from),
+        functools.partial(early_kernel, items, count),
+        in_specs=[SMEM] + [HBM] * 4 * count + [VMEM],
         out_specs=VMEM,
         scratch_shapes=[
             pltpu.VMEM((1024, 256 * len(items)), jnp.bfloat16),
@@ -265,11 +262,10 @@
             pltpu.SemaphoreType.DMA((len(items), 2)),
         ],
         out_shape=jax.ShapeDtypeStruct((1024, 1024), jnp.float32),
-        input_output_aliases={4 * count + 2: 0} if start_from else {},
         compiler_params=LIMIT,
         cost_estimate=cost(1024, items),
-        name="add_part",
-    )(where, *flat(left), *flat(right), fock_columns, *([acc] * start_from))
+        name="early_part",
+    )(where, *flat(left), *flat(right), fock_columns)
 
 
 def last_part(acc, where, left, right, fock_columns, items):
@@ -279,7 +275,7 @@
         in_specs=[SMEM] + [HBM] * 4 * count + [VMEM] * 2,
         out_specs=[VMEM] * 3,
         scratch_shapes=[
-            pltpu.SemaphoreType.DMA((2, len(items), 2)),
+            pltpu.SemaphoreType.DMA((len(items), 2)),
             pltpu.SemaphoreType.DMA((len(items), 2)),
         ],
         out_shape=[
@@ -370,15 +366,10 @@
     right = [[right_half(0), right_half(1)]]
     where = jnp.stack([p, v, r]).astype(jnp.int32)
     fock_columns = virt_fock.T
-    for step in range(1, 8):
-        passing = left[-1]
-        if step == GATE:
-            acc = add_part(None, where, left[:4], right[:4], fock_columns, FIRST)
-            passing = [gate([passing[0]], [acc])[0], passing[1]]
-            left[-1] = passing
-        left.append([send(half, ALONG_VIRT) for half in passing])
+    for _ in range(7):
+        left.append([send(half, ALONG_VIRT) for half in left[-1]])
         right.append([send(half, ALONG_PAIR) for half in right[-1]])
-    acc = add_part(acc, where, left[:6], right[:6], fock_columns, SECOND)
+    acc = early_part(where, left[:6], right[:6], fock_columns, FIRST + SECOND)
     other_part, a_all, b_all = last_part(acc, where, left, right, fock_columns, THIRD)
     arrived = send(other_part, CORES)
     own_part = rest_of_part(acc, where, a_all, b_all, fock_columns, THIRD)

time: 118 us -> 112 us (0.949); the launches traced: 118 us -> 110 us
  Pallas kernels: 30.3 us -> 23.5 us
  local copies, waits for them, and re-layouts: 8.09 us -> 1.83 us
  waiting for transfers between devices: 13.9 us -> 17.7 us
  starting transfers between devices: 63.3 us -> 64.6 us
    unnamed x67 -> x57, local copies, waits for them, and re-layouts: 6.7 us -> 1.69 us
    pallas_call x3 -> x1, Pallas kernels: 16.2 us -> 11.5 us  [early_part(): pl.pallas_call(functools.partial(early_kernel, items, count), in_specs=[S...]
    ppermute x29, waiting for transfers between devices: 13.9 us -> 17.7 us  [send(): return lax.ppermute(block, AXES, permutation)]
    pallas_call x1, Pallas kernels: 7.12 us -> 5.77 us  [last_part(): pl.pallas_call(functools.partial(last_kernel, items, count), in_specs=[SM...]
    ppermute x29, starting transfers between devices: 63.3 us -> 64.6 us  [send(): return lax.ppermute(block, AXES, permutation)]
    dynamic_slice x1, local copies, waits for them, and re-layouts: 1.32 us -> 0.07 us  [half_of(): lax.dynamic_slice(block, starts, sizes).reshape((2,) + block.shape[3:])]
  transfers between devices with their start and end apart: 29 -> 29, of which waited for: 10 -> 12; matrix products, arithmetic and copies ran while one was open for 1% -> 0% of each run, Pallas kernels for 18% -> 14%
where the time goes in v4:
time: 112 us; the launch traced here: 110 us
  starting transfers between devices  64.6 us (58%)
  Pallas kernels  23.5 us (21%)
  waiting for transfers between devices  17.7 us (16%)
  other arithmetic  1.85 us (2%)
  local copies, waits for them, and re-layouts  1.83 us (2%)
    ppermute x29, starting transfers between devices, send(): return lax.ppermute(block, AXES, permutation)  64.6 us
    ppermute x29, waiting for transfers between devices, send(): return lax.ppermute(block, AXES, permutation)  17.7 us
    pallas_call x1, Pallas kernels, early_part(): pl.pallas_call(functools.partial(early_kernel, items, count), in_specs=[S...  11.5 us
    pallas_call x1, Pallas kernels, last_part(): pl.pallas_call(functools.partial(last_kernel, items, count), in_specs=[SM...  5.77 us
    pallas_call x1, Pallas kernels, rest_of_part(): pl.pallas_call(functools.partial(rest_kernel, items), in_specs=[SMEM] + [...  3.78 us
    pallas_call x1, Pallas kernels, update(): pl.pallas_call(update_kernel, in_specs=[SMEM, SMEM, SMEM, VMEM, VMEM, VME...  2.47 us
  transfers between devices with their start and end apart: 29, of which 12 were waited for; matrix products, arithmetic and copies ran while one was open for 0% of the time, Pallas kernels for 14%

profile of v4, /device:TPU:1, one launch (start us, length us, event | category | flops | bytes accessed | tf_op | source)
XLA Modules:
  0.0 110.0 jit_solution(13824953333338165215)
XLA Ops:
  3.1 4.7 %collective-permute-start.1 = (bf16[2,1024,128]{2,1,0:T(8,128)(2,1)S(1)}, bf16[2,1024,128]{2,1,0:T(8,128)(2,1)}, u32[]{:S(2)}, u32[]{:S(2)}) collective-permute-start(bf16[2,1024,128]{2,1,0:T(8,128)(2,1)S(1)} %get-tuple-element.13.refs_1_), channel_id=1, source_target_pairs={{0,8},{1,7},{2,4},{3,11},{4,6},{5,3},{6,0},{7,5},{8,14},{9,1},{10,... | collective-permute-start | bytes 1572872 | tf_op jit(solution)/shard_map/ppermute | solution.py:57
  8.1 3.7 %collective-permute-start.14 = (bf16[256,1024]{1,0:T(8,128)(2,1)S(1)}, bf16[256,1024]{1,0:T(8,128)(2,1)S(1)}, u32[]{:S(2)}, u32[]{:S(2)}) collective-permute-start(bf16[256,1024]{1,0:T(8,128)(2,1)S(1)} %bitcast.52), channel_id=1, source_target_pairs={{0,16},{1,49},{2,18},{3,51},{4,68},{5,53},{6,70},{7,55},{8,24},{9,... | collective-permute-start | bytes 1572872 | tf_op jit(solution)/shard_map/ppermute | solution.py:57
  12.0 2.7 %collective-permute-start.15 = (bf16[256,1024]{1,0:T(8,128)(2,1)S(1)}, bf16[256,1024]{1,0:T(8,128)(2,1)S(1)}, u32[]{:S(2)}, u32[]{:S(2)}) collective-permute-start(bf16[256,1024]{1,0:T(8,128)(2,1)S(1)} %bitcast.55), channel_id=1, source_target_pairs={{0,16},{1,49},{2,18},{3,51},{4,68},{5,53},{6,70},{7,55},{8,24},{9,... | collective-permute-start | bytes 1572872 | tf_op jit(solution)/shard_map/ppermute | solution.py:57
  14.6 2.7 %collective-permute-start.3 = (bf16[2,1024,128]{2,1,0:T(8,128)(2,1)}, bf16[2,1024,128]{2,1,0:T(8,128)(2,1)S(1)}, u32[]{:S(2)}, u32[]{:S(2)}) collective-permute-start(bf16[2,1024,128]{2,1,0:T(8,128)(2,1)} %collective-permute-done.1.refs_3_), channel_id=1, source_target_pairs={{0,8},{1,7},{2,4},{3,11},{4,6},{5,3},{6,0},{7,5},{8,14},{9,1},{10,... | collective-permute-start | bytes 1572872 | tf_op jit(solution)/shard_map/ppermute | solution.py:57
  17.3 2.2 %collective-permute-done.refs_2_ = bf16[2,1024,128]{2,1,0:T(8,128)(2,1)} collective-permute-done((bf16[2,1024,128]{2,1,0:T(8,128)(2,1)S(1)}, bf16[2,1024,128]{2,1,0:T(8,128)(2,1)}, u32[]{:S(2)}, u32[]{:S(2)}) %collective-permute-start) | collective-permute-done | bytes 524320 | tf_op jit(solution)/shard_map/ppermute | solution.py:57
  19.5 3.4 %collective-permute-start.2 = (bf16[2,1024,128]{2,1,0:T(8,128)(2,1)}, bf16[2,1024,128]{2,1,0:T(8,128)(2,1)S(1)}, u32[]{:S(2)}, u32[]{:S(2)}) collective-permute-start(bf16[2,1024,128]{2,1,0:T(8,128)(2,1)} %collective-permute-done.refs_2_), channel_id=1, source_target_pairs={{0,8},{1,7},{2,4},{3,11},{4,6},{5,3},{6,0},{7,5},{8,14},{9,1},{10,... | collective-permute-start | bytes 1572872 | tf_op jit(solution)/shard_map/ppermute | solution.py:57
  22.9 2.3 %collective-permute-start.16 = (bf16[256,1024]{1,0:T(8,128)(2,1)S(1)}, bf16[256,1024]{1,0:T(8,128)(2,1)S(1)}, u32[]{:S(2)}, u32[]{:S(2)}) collective-permute-start(bf16[256,1024]{1,0:T(8,128)(2,1)S(1)} %collective-permute-done.14.refs_14_.refs_18_), channel_id=1, source_target_pairs={{0,16},{1,49},{2,18},{3,51},{4,68},{5,53},{6,70},{7,55},{8,24},{9,... | collective-permute-start | bytes 1572872 | tf_op jit(solution)/shard_map/ppermute | solution.py:57
  25.2 3.1 %collective-permute-start.17 = (bf16[256,1024]{1,0:T(8,128)(2,1)S(1)}, bf16[256,1024]{1,0:T(8,128)(2,1)S(1)}, u32[]{:S(2)}, u32[]{:S(2)}) collective-permute-start(bf16[256,1024]{1,0:T(8,128)(2,1)S(1)} %collective-permute-done.15.refs_15_.refs_19_), channel_id=1, source_target_pairs={{0,16},{1,49},{2,18},{3,51},{4,68},{5,53},{6,70},{7,55},{8,24},{9,... | collective-permute-start | bytes 1572872 | tf_op jit(solution)/shard_map/ppermute | solution.py:57
  28.4 2.5 %collective-permute-done.2.refs_4_ = bf16[2,1024,128]{2,1,0:T(8,128)(2,1)S(1)} collective-permute-done((bf16[2,1024,128]{2,1,0:T(8,128)(2,1)}, bf16[2,1024,128]{2,1,0:T(8,128)(2,1)S(1)}, u32[]{:S(2)}, u32[]{:S(2)}) %collective-permute-start.2) | collective-permute-done | bytes 524320 | tf_op jit(solution)/shard_map/ppermute | solution.py:57
  30.9 3.3 %collective-permute-start.4 = (bf16[2,1024,128]{2,1,0:T(8,128)(2,1)S(1)}, bf16[2,1024,128]{2,1,0:T(8,128)(2,1)S(1)}, u32[]{:S(2)}, u32[]{:S(2)}) collective-permute-start(bf16[2,1024,128]{2,1,0:T(8,128)(2,1)S(1)} %collective-permute-done.2.refs_4_), channel_id=1, source_target_pairs={{0,8},{1,7},{2,4},{3,11},{4,6},{5,3},{6,0},{7,5},{8,14},{9,1},{10,... | collective-permute-start | bytes 1572872 | tf_op jit(solution)/shard_map/ppermute | solution.py:57
  34.2 2.2 %collective-permute-start.18 = (bf16[256,1024]{1,0:T(8,128)(2,1)S(1)}, bf16[256,1024]{1,0:T(8,128)(2,1)S(1)}, u32[]{:S(2)}, u32[]{:S(2)}) collective-permute-start(bf16[256,1024]{1,0:T(8,128)(2,1)S(1)} %collective-permute-done.16.refs_16_.refs_20_), channel_id=1, source_target_pairs={{0,16},{1,49},{2,18},{3,51},{4,68},{5,53},{6,70},{7,55},{8,24},{9,... | collective-permute-start | bytes 1572872 | tf_op jit(solution)/shard_map/ppermute | solution.py:57
  37.0 3.4 %collective-permute-start.19 = (bf16[256,1024]{1,0:T(8,128)(2,1)S(1)}, bf16[256,1024]{1,0:T(8,128)(2,1)S(1)}, u32[]{:S(2)}, u32[]{:S(2)}) collective-permute-start(bf16[256,1024]{1,0:T(8,128)(2,1)S(1)} %collective-permute-done.17.refs_17_.refs_21_), channel_id=1, source_target_pairs={{0,16},{1,49},{2,18},{3,51},{4,68},{5,53},{6,70},{7,55},{8,24},{9,... | collective-permute-start | bytes 1572872 | tf_op jit(solution)/shard_map/ppermute | solution.py:57
  40.5 1.8 %collective-permute-done.4.refs_6_ = bf16[2,1024,128]{2,1,0:T(8,128)(2,1)S(1)} collective-permute-done((bf16[2,1024,128]{2,1,0:T(8,128)(2,1)S(1)}, bf16[2,1024,128]{2,1,0:T(8,128)(2,1)S(1)}, u32[]{:S(2)}, u32[]{:S(2)}) %collective-permute-start.4) | collective-permute-done | bytes 524320 | tf_op jit(solution)/shard_map/ppermute | solution.py:57
  42.3 3.1 %collective-permute-start.6 = (bf16[2,1024,128]{2,1,0:T(8,128)(2,1)S(1)}, bf16[2,1024,128]{2,1,0:T(8,128)(2,1)S(1)}, u32[]{:S(2)}, u32[]{:S(2)}) collective-permute-start(bf16[2,1024,128]{2,1,0:T(8,128)(2,1)S(1)} %collective-permute-done.4.refs_6_), channel_id=1, source_target_pairs={{0,8},{1,7},{2,4},{3,11},{4,6},{5,3},{6,0},{7,5},{8,14},{9,1},{10,... | collective-permute-start | bytes 1572872 | tf_op jit(solution)/shard_map/ppermute | solution.py:57
  45.4 2.2 %collective-permute-start.20 = (bf16[256,1024]{1,0:T(8,128)(2,1)S(1)}, bf16[256,1024]{1,0:T(8,128)(2,1)S(1)}, u32[]{:S(2)}, u32[]{:S(2)}) collective-permute-start(bf16[256,1024]{1,0:T(8,128)(2,1)S(1)} %collective-permute-done.18.refs_18_.refs_22_), channel_id=1, source_target_pairs={{0,16},{1,49},{2,18},{3,51},{4,68},{5,53},{6,70},{7,55},{8,24},{9,... | collective-permute-start | bytes 1572872 | tf_op jit(solution)/shard_map/ppermute | solution.py:57
  48.2 3.4 %collective-permute-start.21 = (bf16[256,1024]{1,0:T(8,128)(2,1)S(1)}, bf16[256,1024]{1,0:T(8,128)(2,1)S(1)}, u32[]{:S(2)}, u32[]{:S(2)}) collective-permute-start(bf16[256,1024]{1,0:T(8,128)(2,1)S(1)} %collective-permute-done.19.refs_19_.refs_23_), channel_id=1, source_target_pairs={{0,16},{1,49},{2,18},{3,51},{4,68},{5,53},{6,70},{7,55},{8,24},{9,... | collective-permute-start | bytes 1572872 | tf_op jit(solution)/shard_map/ppermute | solution.py:57
  51.7 2.6 %collective-permute-done.6.refs_8_ = bf16[2,1024,128]{2,1,0:T(8,128)(2,1)S(1)} collective-permute-done((bf16[2,1024,128]{2,1,0:T(8,128)(2,1)S(1)}, bf16[2,1024,128]{2,1,0:T(8,128)(2,1)S(1)}, u32[]{:S(2)}, u32[]{:S(2)}) %collective-permute-start.6) | collective-permute-done | bytes 524320 | tf_op jit(solution)/shard_map/ppermute | solution.py:57
  54.3 2.3 %collective-permute-start.8 = (bf16[2,1024,128]{2,1,0:T(8,128)(2,1)S(1)}, bf16[2,1024,128]{2,1,0:T(8,128)(2,1)}, u32[]{:S(2)}, u32[]{:S(2)}) collective-permute-start(bf16[2,1024,128]{2,1,0:T(8,128)(2,1)S(1)} %collective-permute-done.6.refs_8_), channel_id=1, source_target_pairs={{0,8},{1,7},{2,4},{3,11},{4,6},{5,3},{6,0},{7,5},{8,14},{9,1},{10,... | collective-permute-start | bytes 1572872 | tf_op jit(solution)/shard_map/ppermute | solution.py:57
  56.7 2.2 %collective-permute-start.22 = (bf16[256,1024]{1,0:T(8,128)(2,1)S(1)}, bf16[256,1024]{1,0:T(8,128)(2,1)}, u32[]{:S(2)}, u32[]{:S(2)}) collective-permute-start(bf16[256,1024]{1,0:T(8,128)(2,1)S(1)} %collective-permute-done.20.refs_20_.refs_24_), channel_id=1, source_target_pairs={{0,16},{1,49},{2,18},{3,51},{4,68},{5,53},{6,70},{7,55},{8,24},{9,... | collective-permute-start | bytes 1572872 | tf_op jit(solution)/shard_map/ppermute | solution.py:57
  59.5 3.5 %collective-permute-start.23 = (bf16[256,1024]{1,0:T(8,128)(2,1)S(1)}, bf16[256,1024]{1,0:T(8,128)(2,1)}, u32[]{:S(2)}, u32[]{:S(2)}) collective-permute-start(bf16[256,1024]{1,0:T(8,128)(2,1)S(1)} %collective-permute-done.21.refs_21_.refs_25_), channel_id=1, source_target_pairs={{0,16},{1,49},{2,18},{3,51},{4,68},{5,53},{6,70},{7,55},{8,24},{9,... | collective-permute-start | bytes 1572872 | tf_op jit(solution)/shard_map/ppermute | solution.py:57
  63.1 2.6 %collective-permute-done.8.refs_10_ = bf16[2,1024,128]{2,1,0:T(8,128)(2,1)} collective-permute-done((bf16[2,1024,128]{2,1,0:T(8,128)(2,1)S(1)}, bf16[2,1024,128]{2,1,0:T(8,128)(2,1)}, u32[]{:S(2)}, u32[]{:S(2)}) %collective-permute-start.8) | collective-permute-done | bytes 524320 | tf_op jit(solution)/shard_map/ppermute | solution.py:57
  65.7 2.3 %collective-permute-start.10 = (bf16[2,1024,128]{2,1,0:T(8,128)(2,1)}, bf16[2,1024,128]{2,1,0:T(8,128)(2,1)S(1)}, u32[]{:S(2)}, u32[]{:S(2)}) collective-permute-start(bf16[2,1024,128]{2,1,0:T(8,128)(2,1)} %collective-permute-done.8.refs_10_), channel_id=1, source_target_pairs={{0,8},{1,7},{2,4},{3,11},{4,6},{5,3},{6,0},{7,5},{8,14},{9,1},{10,... | collective-permute-start | bytes 1572872 | tf_op jit(solution)/shard_map/ppermute | solution.py:57
  68.0 2.2 %collective-permute-start.24 = (bf16[256,1024]{1,0:T(8,128)(2,1)}, bf16[256,1024]{1,0:T(8,128)(2,1)S(1)}, u32[]{:S(2)}, u32[]{:S(2)}) collective-permute-start(bf16[256,1024]{1,0:T(8,128)(2,1)} %collective-permute-done.22.refs_22_.refs_26_), channel_id=1, source_target_pairs={{0,16},{1,49},{2,18},{3,51},{4,68},{5,53},{6,70},{7,55},{8,24},{9,... | collective-permute-start | bytes 1572872 | tf_op jit(solution)/shard_map/ppermute | solution.py:57
  70.8 3.5 %collective-permute-start.25 = (bf16[256,1024]{1,0:T(8,128)(2,1)}, bf16[256,1024]{1,0:T(8,128)(2,1)S(1)}, u32[]{:S(2)}, u32[]{:S(2)}) collective-permute-start(bf16[256,1024]{1,0:T(8,128)(2,1)} %collective-permute-done.23.refs_23_.refs_27_), channel_id=1, source_target_pairs={{0,16},{1,49},{2,18},{3,51},{4,68},{5,53},{6,70},{7,55},{8,24},{9,... | collective-permute-start | bytes 1572872 | tf_op jit(solution)/shard_map/ppermute | solution.py:57
  74.7 2.5 %collective-permute-done.10.refs_12_ = bf16[2,1024,128]{2,1,0:T(8,128)(2,1)S(1)} collective-permute-done((bf16[2,1024,128]{2,1,0:T(8,128)(2,1)}, bf16[2,1024,128]{2,1,0:T(8,128)(2,1)S(1)}, u32[]{:S(2)}, u32[]{:S(2)}) %collective-permute-start.10) | collective-permute-done | bytes 524320 | tf_op jit(solution)/shard_map/ppermute | solution.py:57
  77.2 1.9 %collective-permute-start.12 = (bf16[2,1024,128]{2,1,0:T(8,128)(2,1)S(1)}, bf16[2,1024,128]{2,1,0:T(8,128)(2,1)S(1)}, u32[]{:S(2)}, u32[]{:S(2)}) collective-permute-start(bf16[2,1024,128]{2,1,0:T(8,128)(2,1)S(1)} %collective-permute-done.10.refs_12_), channel_id=1, source_target_pairs={{0,8},{1,7},{2,4},{3,11},{4,6},{5,3},{6,0},{7,5},{8,14},{9,1},{10,... | collective-permute-start | bytes 1572872 | tf_op jit(solution)/shard_map/ppermute | solution.py:57
  79.1 2.4 %collective-permute-start.26 = (bf16[256,1024]{1,0:T(8,128)(2,1)S(1)}, bf16[256,1024]{1,0:T(8,128)(2,1)S(1)}, u32[]{:S(2)}, u32[]{:S(2)}) collective-permute-start(bf16[256,1024]{1,0:T(8,128)(2,1)S(1)} %collective-permute-done.24.refs_28_), channel_id=1, source_target_pairs={{0,16},{1,49},{2,18},{3,51},{4,68},{5,53},{6,70},{7,55},{8,24},{9,... | collective-permute-start | bytes 1572872 | tf_op jit(solution)/shard_map/ppermute | solution.py:57
  82.2 3.3 %collective-permute-start.27 = (bf16[256,1024]{1,0:T(8,128)(2,1)S(1)}, bf16[256,1024]{1,0:T(8,128)(2,1)S(1)}, u32[]{:S(2)}, u32[]{:S(2)}) collective-permute-start(bf16[256,1024]{1,0:T(8,128)(2,1)S(1)} %collective-permute-done.25.refs_29_), channel_id=1, source_target_pairs={{0,16},{1,49},{2,18},{3,51},{4,68},{5,53},{6,70},{7,55},{8,24},{9,... | collective-permute-start | bytes 1572872 | tf_op jit(solution)/shard_map/ppermute | solution.py:57
  85.5 11.5 %early_part.1.refs_33_.acc_ref = f32[1024,1024]{1,0:T(8,128)S(1)} custom-call(s32[3]{0:T(128)S(1)} %pad_add_fusion.where, bf16[2,1024,128]{2,1,0:T(8,128)(2,1)} %copy-done.7, bf16[2,1024,128]{2,1,0:T(8,128)(2,1)} %copy-done.6, bf16[2,1024,128]{2,1,0:T(8,128)(2,1)} %collective-permute-done.refs_2_, bf16[2,1024,128]{2,1,0:T(8,128)(2,1)} %collective-permute-done.1.refs_3_, ...), custom_call_target="tpu_custom_call" | custom-call | flops 6039797760 | bytes 9437184 | tf_op jit(solution)/shard_map/early_part/pallas_call | solution.py:254
  97.1 5.8 %last_part.1 = (f32[512,1024]{1,0:T(8,128)S(1)}, bf16[1024,1792]{1,0:T(8,128)(2,1)S(1)}, bf16[1792,1024]{1,0:T(8,128)(2,1)S(1)}) custom-call(s32[3]{0:T(128)S(1)} %pad_add_fusion.where, bf16[2,1024,128]{2,1,0:T(8,128)(2,1)} %copy-done.7, bf16[2,1024,128]{2,1,0:T(8,128)(2,1)} %copy-done.6, bf16[2,1024,128]{2,1,0:T(8,128)(2,1)} %collective-permute-done.refs_2_, ...), custom_call_target="tpu_custom_call" | custom-call | flops 2348810240 | bytes 7340032 | tf_op jit(solution)/shard_map/last_part/pallas_call | solution.py:273
  103.2 3.8 %rest_of_part.1.own_ref = f32[512,1024]{1,0:T(8,128)S(1)} custom-call(s32[3]{0:T(128)S(1)} %pad_add_fusion.where, bf16[1024,1792]{1,0:T(8,128)(2,1)S(1)} %get-tuple-element.8.a_all, bf16[1792,1024]{1,0:T(8,128)(2,1)S(1)} %get-tuple-element.9.b_all, bf16[1024,128]{1,0:T(8,128)(2,1)S(1)} %bitcast.48, f32[1024,1024]{1,0:T(8,128)S(1)} %early_part.1.refs_33_.acc_ref), custom_call_target="tpu_custom_call" | custom-call | flops 2348810240 | bytes 7340032 | tf_op jit(solution)/shard_map/rest_of_part/pallas_call | solution.py:293
  107.4 2.5 %update.1 = f32[1,8,512,128]{3,2,1,0:T(8,128)} custom-call(s32[3]{0:T(128)S(1)} %pad_add_fusion.where, s32[8,8]{1,0:T(8,128)S(1)} %bitcast.50, f32[8]{0:T(128)S(1)} %copy-done.3, f32[8,128]{1,0:T(8,128)S(1)} %bitcast.51, f32[512,1024]{1,0:T(8,128)S(1)} %rest_of_part.1.own_ref, f32[512,1024]{1,0:T(8,128)S(1)} %collective-permute-done.28.other_ref, ...), custom_call_target="tpu_custom_call" | custom-call | tf_op jit(solution)/shard_map/update/pallas_call | solution.py:331
  (92 shorter events, 8.0 us)
Async XLA Ops:
  3.1 11.5 %collective-permute-start.1 = (bf16[2,1024,128]{2,1,0:T(8,128)(2,1)S(1)}, bf16[2,1024,128]{2,1,0:T(8,128)(2,1)}, u32[]{:S(2)}, u32[]{:S(2)}) collective-permute-start(bf16[2,1024,128]{2,1,0:T(8,128)(2,1)S(1)} %get-tuple-element.13.refs_1_), channel_id=1, source_target_pairs={{0,8},{1,7},{2,4},{3,11},{4,6},{5,3},{6,0},{7,5},{8,14},{9,1},{10,... | collective-permute-start | bytes 1572872 | tf_op jit(solution)/shard_map/ppermute | solution.py:57
  7.8 11.7 %collective-permute-start = (bf16[2,1024,128]{2,1,0:T(8,128)(2,1)S(1)}, bf16[2,1024,128]{2,1,0:T(8,128)(2,1)}, u32[]{:S(2)}, u32[]{:S(2)}) collective-permute-start(bf16[2,1024,128]{2,1,0:T(8,128)(2,1)S(1)} %get-tuple-element.14.refs_0_), channel_id=1, source_target_pairs={{0,8},{1,7},{2,4},{3,11},{4,6},{5,3},{6,0},{7,5},{8,14},{9,1},{10,... | collective-permute-start | bytes 1572872 | tf_op jit(solution)/shard_map/ppermute | solution.py:57
  8.0 66.3 %copy-start.23 = (bf16[128,1024]{1,0:T(8,128)(2,1)S(1)}, bf16[128,1024]{1,0:T(8,128)(2,1)}, u32[]{:S(2)}) copy-start(bf16[128,1024]{1,0:T(8,128)(2,1)} %param.9) | copy-start | bytes 786436
  8.1 77.4 %copy-start.4 = (bf16[32,8,8,128]{3,1,2,0:T(8,128)(2,1)}, bf16[32,8,8,128]{3,1,2,0:T(8,128)(2,1)S(1)}, u32[]{:S(2)}) copy-start(bf16[32,8,8,128]{3,1,2,0:T(8,128)(2,1)S(1)} %copy.37) | copy-start | bytes 1572868
  8.1 14.8 %collective-permute-start.14 = (bf16[256,1024]{1,0:T(8,128)(2,1)S(1)}, bf16[256,1024]{1,0:T(8,128)(2,1)S(1)}, u32[]{:S(2)}, u32[]{:S(2)}) collective-permute-start(bf16[256,1024]{1,0:T(8,128)(2,1)S(1)} %bitcast.52), channel_id=1, source_target_pairs={{0,16},{1,49},{2,18},{3,51},{4,68},{5,53},{6,70},{7,55},{8,24},{9,... | collective-permute-start | bytes 1572872 | tf_op jit(solution)/shard_map/ppermute | solution.py:57
  11.9 51.0 %copy-start.5 = (bf16[32,8,8,128]{3,1,2,0:T(8,128)(2,1)}, bf16[32,8,8,128]{3,1,2,0:T(8,128)(2,1)S(1)}, u32[]{:S(2)}) copy-start(bf16[32,8,8,128]{3,1,2,0:T(8,128)(2,1)S(1)} %copy.36) | copy-start | bytes 1572868
  12.0 13.3 %collective-permute-start.15 = (bf16[256,1024]{1,0:T(8,128)(2,1)S(1)}, bf16[256,1024]{1,0:T(8,128)(2,1)S(1)}, u32[]{:S(2)}, u32[]{:S(2)}) collective-permute-start(bf16[256,1024]{1,0:T(8,128)(2,1)S(1)} %bitcast.55), channel_id=1, source_target_pairs={{0,16},{1,49},{2,18},{3,51},{4,68},{5,53},{6,70},{7,55},{8,24},{9,... | collective-permute-start | bytes 1572872 | tf_op jit(solution)/shard_map/ppermute | solution.py:57
  14.6 13.7 %collective-permute-start.3 = (bf16[2,1024,128]{2,1,0:T(8,128)(2,1)}, bf16[2,1024,128]{2,1,0:T(8,128)(2,1)S(1)}, u32[]{:S(2)}, u32[]{:S(2)}) collective-permute-start(bf16[2,1024,128]{2,1,0:T(8,128)(2,1)} %collective-permute-done.1.refs_3_), channel_id=1, source_target_pairs={{0,8},{1,7},{2,4},{3,11},{4,6},{5,3},{6,0},{7,5},{8,14},{9,1},{10,... | collective-permute-start | bytes 1572872 | tf_op jit(solution)/shard_map/ppermute | solution.py:57
  19.5 11.3 %collective-permute-start.2 = (bf16[2,1024,128]{2,1,0:T(8,128)(2,1)}, bf16[2,1024,128]{2,1,0:T(8,128)(2,1)S(1)}, u32[]{:S(2)}, u32[]{:S(2)}) collective-permute-start(bf16[2,1024,128]{2,1,0:T(8,128)(2,1)} %collective-permute-done.refs_2_), channel_id=1, source_target_pairs={{0,8},{1,7},{2,4},{3,11},{4,6},{5,3},{6,0},{7,5},{8,14},{9,1},{10,... | collective-permute-start | bytes 1572872 | tf_op jit(solution)/shard_map/ppermute | solution.py:57
  22.9 11.2 %collective-permute-start.16 = (bf16[256,1024]{1,0:T(8,128)(2,1)S(1)}, bf16[256,1024]{1,0:T(8,128)(2,1)S(1)}, u32[]{:S(2)}, u32[]{:S(2)}) collective-permute-start(bf16[256,1024]{1,0:T(8,128)(2,1)S(1)} %collective-permute-done.14.refs_14_.refs_18_), channel_id=1, source_target_pairs={{0,16},{1,49},{2,18},{3,51},{4,68},{5,53},{6,70},{7,55},{8,24},{9,... | collective-permute-start | bytes 1572872 | tf_op jit(solution)/shard_map/ppermute | solution.py:57
  25.2 11.7 %collective-permute-start.17 = (bf16[256,1024]{1,0:T(8,128)(2,1)S(1)}, bf16[256,1024]{1,0:T(8,128)(2,1)S(1)}, u32[]{:S(2)}, u32[]{:S(2)}) collective-permute-start(bf16[256,1024]{1,0:T(8,128)(2,1)S(1)} %collective-permute-done.15.refs_15_.refs_19_), channel_id=1, source_target_pairs={{0,16},{1,49},{2,18},{3,51},{4,68},{5,53},{6,70},{7,55},{8,24},{9,... | collective-permute-start | bytes 1572872 | tf_op jit(solution)/shard_map/ppermute | solution.py:57
  28.3 12.0 %collective-permute-start.5 = (bf16[2,1024,128]{2,1,0:T(8,128)(2,1)S(1)}, bf16[2,1024,128]{2,1,0:T(8,128)(2,1)S(1)}, u32[]{:S(2)}, u32[]{:S(2)}) collective-permute-start(bf16[2,1024,128]{2,1,0:T(8,128)(2,1)S(1)} %collective-permute-done.3.refs_5_), channel_id=1, source_target_pairs={{0,8},{1,7},{2,4},{3,11},{4,6},{5,3},{6,0},{7,5},{8,14},{9,1},{10,... | collective-permute-start | bytes 1572872 | tf_op jit(solution)/shard_map/ppermute | solution.py:57
  30.9 11.4 %collective-permute-start.4 = (bf16[2,1024,128]{2,1,0:T(8,128)(2,1)S(1)}, bf16[2,1024,128]{2,1,0:T(8,128)(2,1)S(1)}, u32[]{:S(2)}, u32[]{:S(2)}) collective-permute-start(bf16[2,1024,128]{2,1,0:T(8,128)(2,1)S(1)} %collective-permute-done.2.refs_4_), channel_id=1, source_target_pairs={{0,8},{1,7},{2,4},{3,11},{4,6},{5,3},{6,0},{7,5},{8,14},{9,1},{10,... | collective-permute-start | bytes 1572872 | tf_op jit(solution)/shard_map/ppermute | solution.py:57
  34.2 11.2 %collective-permute-start.18 = (bf16[256,1024]{1,0:T(8,128)(2,1)S(1)}, bf16[256,1024]{1,0:T(8,128)(2,1)S(1)}, u32[]{:S(2)}, u32[]{:S(2)}) collective-permute-start(bf16[256,1024]{1,0:T(8,128)(2,1)S(1)} %collective-permute-done.16.refs_16_.refs_20_), channel_id=1, source_target_pairs={{0,16},{1,49},{2,18},{3,51},{4,68},{5,53},{6,70},{7,55},{8,24},{9,... | collective-permute-start | bytes 1572872 | tf_op jit(solution)/shard_map/ppermute | solution.py:57
  37.0 11.2 %collective-permute-start.19 = (bf16[256,1024]{1,0:T(8,128)(2,1)S(1)}, bf16[256,1024]{1,0:T(8,128)(2,1)S(1)}, u32[]{:S(2)}, u32[]{:S(2)}) collective-permute-start(bf16[256,1024]{1,0:T(8,128)(2,1)S(1)} %collective-permute-done.17.refs_17_.refs_21_), channel_id=1, source_target_pairs={{0,16},{1,49},{2,18},{3,51},{4,68},{5,53},{6,70},{7,55},{8,24},{9,... | collective-permute-start | bytes 1572872 | tf_op jit(solution)/shard_map/ppermute | solution.py:57
  40.4 11.2 %collective-permute-start.7 = (bf16[2,1024,128]{2,1,0:T(8,128)(2,1)S(1)}, bf16[2,1024,128]{2,1,0:T(8,128)(2,1)S(1)}, u32[]{:S(2)}, u32[]{:S(2)}) collective-permute-start(bf16[2,1024,128]{2,1,0:T(8,128)(2,1)S(1)} %collective-permute-done.5.refs_7_), channel_id=1, source_target_pairs={{0,8},{1,7},{2,4},{3,11},{4,6},{5,3},{6,0},{7,5},{8,14},{9,1},{10,... | collective-permute-start | bytes 1572872 | tf_op jit(solution)/shard_map/ppermute | solution.py:57
  42.3 12.0 %collective-permute-start.6 = (bf16[2,1024,128]{2,1,0:T(8,128)(2,1)S(1)}, bf16[2,1024,128]{2,1,0:T(8,128)(2,1)S(1)}, u32[]{:S(2)}, u32[]{:S(2)}) collective-permute-start(bf16[2,1024,128]{2,1,0:T(8,128)(2,1)S(1)} %collective-permute-done.4.refs_6_), channel_id=1, source_target_pairs={{0,8},{1,7},{2,4},{3,11},{4,6},{5,3},{6,0},{7,5},{8,14},{9,1},{10,... | collective-permute-start | bytes 1572872 | tf_op jit(solution)/shard_map/ppermute | solution.py:57
  45.4 11.2 %collective-permute-start.20 = (bf16[256,1024]{1,0:T(8,128)(2,1)S(1)}, bf16[256,1024]{1,0:T(8,128)(2,1)S(1)}, u32[]{:S(2)}, u32[]{:S(2)}) collective-permute-start(bf16[256,1024]{1,0:T(8,128)(2,1)S(1)} %collective-permute-done.18.refs_18_.refs_22_), channel_id=1, source_target_pairs={{0,16},{1,49},{2,18},{3,51},{4,68},{5,53},{6,70},{7,55},{8,24},{9,... | collective-permute-start | bytes 1572872 | tf_op jit(solution)/shard_map/ppermute | solution.py:57
  48.2 11.3 %collective-permute-start.21 = (bf16[256,1024]{1,0:T(8,128)(2,1)S(1)}, bf16[256,1024]{1,0:T(8,128)(2,1)S(1)}, u32[]{:S(2)}, u32[]{:S(2)}) collective-permute-start(bf16[256,1024]{1,0:T(8,128)(2,1)S(1)} %collective-permute-done.19.refs_19_.refs_23_), channel_id=1, source_target_pairs={{0,16},{1,49},{2,18},{3,51},{4,68},{5,53},{6,70},{7,55},{8,24},{9,... | collective-permute-start | bytes 1572872 | tf_op jit(solution)/shard_map/ppermute | solution.py:57
  51.6 11.3 %collective-permute-start.9 = (bf16[2,1024,128]{2,1,0:T(8,128)(2,1)S(1)}, bf16[2,1024,128]{2,1,0:T(8,128)(2,1)}, u32[]{:S(2)}, u32[]{:S(2)}) collective-permute-start(bf16[2,1024,128]{2,1,0:T(8,128)(2,1)S(1)} %collective-permute-done.7.refs_9_), channel_id=1, source_target_pairs={{0,8},{1,7},{2,4},{3,11},{4,6},{5,3},{6,0},{7,5},{8,14},{9,1},{10,... | collective-permute-start | bytes 1572872 | tf_op jit(solution)/shard_map/ppermute | solution.py:57
  54.3 11.3 %collective-permute-start.8 = (bf16[2,1024,128]{2,1,0:T(8,128)(2,1)S(1)}, bf16[2,1024,128]{2,1,0:T(8,128)(2,1)}, u32[]{:S(2)}, u32[]{:S(2)}) collective-permute-start(bf16[2,1024,128]{2,1,0:T(8,128)(2,1)S(1)} %collective-permute-done.6.refs_8_), channel_id=1, source_target_pairs={{0,8},{1,7},{2,4},{3,11},{4,6},{5,3},{6,0},{7,5},{8,14},{9,1},{10,... | collective-permute-start | bytes 1572872 | tf_op jit(solution)/shard_map/ppermute | solution.py:57
  56.7 11.3 %collective-permute-start.22 = (bf16[256,1024]{1,0:T(8,128)(2,1)S(1)}, bf16[256,1024]{1,0:T(8,128)(2,1)}, u32[]{:S(2)}, u32[]{:S(2)}) collective-permute-start(bf16[256,1024]{1,0:T(8,128)(2,1)S(1)} %collective-permute-done.20.refs_20_.refs_24_), channel_id=1, source_target_pairs={{0,16},{1,49},{2,18},{3,51},{4,68},{5,53},{6,70},{7,55},{8,24},{9,... | collective-permute-start | bytes 1572872 | tf_op jit(solution)/shard_map/ppermute | solution.py:57
  59.5 11.2 %collective-permute-start.23 = (bf16[256,1024]{1,0:T(8,128)(2,1)S(1)}, bf16[256,1024]{1,0:T(8,128)(2,1)}, u32[]{:S(2)}, u32[]{:S(2)}) collective-permute-start(bf16[256,1024]{1,0:T(8,128)(2,1)S(1)} %collective-permute-done.21.refs_21_.refs_25_), channel_id=1, source_target_pairs={{0,16},{1,49},{2,18},{3,51},{4,68},{5,53},{6,70},{7,55},{8,24},{9,... | collective-permute-start | bytes 1572872 | tf_op jit(solution)/shard_map/ppermute | solution.py:57
  63.0 11.5 %collective-permute-start.11 = (bf16[2,1024,128]{2,1,0:T(8,128)(2,1)}, bf16[2,1024,128]{2,1,0:T(8,128)(2,1)S(1)}, u32[]{:S(2)}, u32[]{:S(2)}) collective-permute-start(bf16[2,1024,128]{2,1,0:T(8,128)(2,1)} %collective-permute-done.9.refs_11_), channel_id=1, source_target_pairs={{0,8},{1,7},{2,4},{3,11},{4,6},{5,3},{6,0},{7,5},{8,14},{9,1},{10,... | collective-permute-start | bytes 1572872 | tf_op jit(solution)/shard_map/ppermute | solution.py:57
  65.7 11.5 %collective-permute-start.10 = (bf16[2,1024,128]{2,1,0:T(8,128)(2,1)}, bf16[2,1024,128]{2,1,0:T(8,128)(2,1)S(1)}, u32[]{:S(2)}, u32[]{:S(2)}) collective-permute-start(bf16[2,1024,128]{2,1,0:T(8,128)(2,1)} %collective-permute-done.8.refs_10_), channel_id=1, source_target_pairs={{0,8},{1,7},{2,4},{3,11},{4,6},{5,3},{6,0},{7,5},{8,14},{9,1},{10,... | collective-permute-start | bytes 1572872 | tf_op jit(solution)/shard_map/ppermute | solution.py:57
  68.0 11.1 %collective-permute-start.24 = (bf16[256,1024]{1,0:T(8,128)(2,1)}, bf16[256,1024]{1,0:T(8,128)(2,1)S(1)}, u32[]{:S(2)}, u32[]{:S(2)}) collective-permute-start(bf16[256,1024]{1,0:T(8,128)(2,1)} %collective-permute-done.22.refs_22_.refs_26_), channel_id=1, source_target_pairs={{0,16},{1,49},{2,18},{3,51},{4,68},{5,53},{6,70},{7,55},{8,24},{9,... | collective-permute-start | bytes 1572872 | tf_op jit(solution)/shard_map/ppermute | solution.py:57
  70.8 11.4 %collective-permute-start.25 = (bf16[256,1024]{1,0:T(8,128)(2,1)}, bf16[256,1024]{1,0:T(8,128)(2,1)S(1)}, u32[]{:S(2)}, u32[]{:S(2)}) collective-permute-start(bf16[256,1024]{1,0:T(8,128)(2,1)} %collective-permute-done.23.refs_23_.refs_27_), channel_id=1, source_target_pairs={{0,16},{1,49},{2,18},{3,51},{4,68},{5,53},{6,70},{7,55},{8,24},{9,... | collective-permute-start | bytes 1572872 | tf_op jit(solution)/shard_map/ppermute | solution.py:57
  74.5 22.6 %collective-permute-start.13 = (bf16[2,1024,128]{2,1,0:T(8,128)(2,1)S(1)}, bf16[2,1024,128]{2,1,0:T(8,128)(2,1)S(1)}, u32[]{:S(2)}, u32[]{:S(2)}) collective-permute-start(bf16[2,1024,128]{2,1,0:T(8,128)(2,1)S(1)} %collective-permute-done.11.refs_13_), channel_id=1, source_target_pairs={{0,8},{1,7},{2,4},{3,11},{4,6},{5,3},{6,0},{7,5},{8,14},{9,1},{10,... | collective-permute-start | bytes 1572872 | tf_op jit(solution)/shard_map/ppermute | solution.py:57
  77.2 19.9 %collective-permute-start.12 = (bf16[2,1024,128]{2,1,0:T(8,128)(2,1)S(1)}, bf16[2,1024,128]{2,1,0:T(8,128)(2,1)S(1)}, u32[]{:S(2)}, u32[]{:S(2)}) collective-permute-start(bf16[2,1024,128]{2,1,0:T(8,128)(2,1)S(1)} %collective-permute-done.10.refs_12_), channel_id=1, source_target_pairs={{0,8},{1,7},{2,4},{3,11},{4,6},{5,3},{6,0},{7,5},{8,14},{9,1},{10,... | collective-permute-start | bytes 1572872 | tf_op jit(solution)/shard_map/ppermute | solution.py:57
  79.1 18.0 %collective-permute-start.26 = (bf16[256,1024]{1,0:T(8,128)(2,1)S(1)}, bf16[256,1024]{1,0:T(8,128)(2,1)S(1)}, u32[]{:S(2)}, u32[]{:S(2)}) collective-permute-start(bf16[256,1024]{1,0:T(8,128)(2,1)S(1)} %collective-permute-done.24.refs_28_), channel_id=1, source_target_pairs={{0,16},{1,49},{2,18},{3,51},{4,68},{5,53},{6,70},{7,55},{8,24},{9,... | collective-permute-start | bytes 1572872 | tf_op jit(solution)/shard_map/ppermute | solution.py:57
  82.2 14.9 %collective-permute-start.27 = (bf16[256,1024]{1,0:T(8,128)(2,1)S(1)}, bf16[256,1024]{1,0:T(8,128)(2,1)S(1)}, u32[]{:S(2)}, u32[]{:S(2)}) collective-permute-start(bf16[256,1024]{1,0:T(8,128)(2,1)S(1)} %collective-permute-done.25.refs_29_), channel_id=1, source_target_pairs={{0,16},{1,49},{2,18},{3,51},{4,68},{5,53},{6,70},{7,55},{8,24},{9,... | collective-permute-start | bytes 1572872 | tf_op jit(solution)/shard_map/ppermute | solution.py:57
  102.9 4.5 %collective-permute-start.28 = (f32[512,1024]{1,0:T(8,128)S(1)}, f32[512,1024]{1,0:T(8,128)S(1)}, u32[]{:S(2)}, u32[]{:S(2)}) collective-permute-start(f32[512,1024]{1,0:T(8,128)S(1)} %get-tuple-element.10), channel_id=1, source_target_pairs={{0,1},{1,0},{2,3},{3,2},{4,5},{5,4},{6,7},{7,6},{8,9},{9,8},{10,11... | collective-permute-start | bytes 6291464 | tf_op jit(solution)/shard_map/ppermute | solution.py:57
  (21 other events, 434.1 us)

commit v5 on v4

--- a/solution.py
+++ b/solution.py
@@ -141,7 +141,7 @@
 
 
 def multiply(tiles, some, fock_ref, acc_ref, out_ref, a_all, b_all, row_start):
-    rows, width, block = out_ref.shape[0], WIDTH, 512
+    rows, width, block = out_ref.shape[0], WIDTH, 256
     depth = slice(some[0] * 256, (some[-1] + 1) * 256)
 
     def columns_of(step, carry):

time: 112 us -> 112 us (level)
  no operation moved by 1% of the time
where the time goes in v5:
time: 112 us; the launch traced here: 110 us
  starting transfers between devices  64.6 us (58%)
  Pallas kernels  23.1 us (21%)
  waiting for transfers between devices  17.8 us (16%)
  other arithmetic  1.85 us (2%)
  local copies, waits for them, and re-layouts  1.83 us (2%)
    ppermute x29, starting transfers between devices, send(): return lax.ppermute(block, AXES, permutation)  64.6 us
    ppermute x29, waiting for transfers between devices, send(): return lax.ppermute(block, AXES, permutation)  17.8 us
    pallas_call x1, Pallas kernels, early_part(): pl.pallas_call(functools.partial(early_kernel, items, count), in_specs=[S...  11.3 us
    pallas_call x1, Pallas kernels, last_part(): pl.pallas_call(functools.partial(last_kernel, items, count), in_specs=[SM...  5.66 us
    pallas_call x1, Pallas kernels, rest_of_part(): pl.pallas_call(functools.partial(rest_kernel, items), in_specs=[SMEM] + [...  3.66 us
    pallas_call x1, Pallas kernels, update(): pl.pallas_call(update_kernel, in_specs=[SMEM, SMEM, SMEM, VMEM, VMEM, VME...  2.47 us
  transfers between devices with their start and end apart: 29, of which 12 were waited for; matrix products, arithmetic and copies ran while one was open for 0% of the time, Pallas kernels for 14%

profile of v5, /device:TPU:1, one launch (start us, length us, event | category | flops | bytes accessed | tf_op | source)
XLA Modules:
  0.0 109.7 jit_solution(5923926895188664783)
XLA Ops:
  3.1 4.7 %collective-permute-start.1 = (bf16[2,1024,128]{2,1,0:T(8,128)(2,1)S(1)}, bf16[2,1024,128]{2,1,0:T(8,128)(2,1)}, u32[]{:S(2)}, u32[]{:S(2)}) collective-permute-start(bf16[2,1024,128]{2,1,0:T(8,128)(2,1)S(1)} %get-tuple-element.13.refs_1_), channel_id=1, source_target_pairs={{0,8},{1,7},{2,4},{3,11},{4,6},{5,3},{6,0},{7,5},{8,14},{9,1},{10,... | collective-permute-start | bytes 1572872 | tf_op jit(solution)/shard_map/ppermute | solution.py:57
  8.1 3.7 %collective-permute-start.14 = (bf16[256,1024]{1,0:T(8,128)(2,1)S(1)}, bf16[256,1024]{1,0:T(8,128)(2,1)S(1)}, u32[]{:S(2)}, u32[]{:S(2)}) collective-permute-start(bf16[256,1024]{1,0:T(8,128)(2,1)S(1)} %bitcast.52), channel_id=1, source_target_pairs={{0,16},{1,49},{2,18},{3,51},{4,68},{5,53},{6,70},{7,55},{8,24},{9,... | collective-permute-start | bytes 1572872 | tf_op jit(solution)/shard_map/ppermute | solution.py:57
  12.0 2.7 %collective-permute-start.15 = (bf16[256,1024]{1,0:T(8,128)(2,1)S(1)}, bf16[256,1024]{1,0:T(8,128)(2,1)S(1)}, u32[]{:S(2)}, u32[]{:S(2)}) collective-permute-start(bf16[256,1024]{1,0:T(8,128)(2,1)S(1)} %bitcast.55), channel_id=1, source_target_pairs={{0,16},{1,49},{2,18},{3,51},{4,68},{5,53},{6,70},{7,55},{8,24},{9,... | collective-permute-start | bytes 1572872 | tf_op jit(solution)/shard_map/ppermute | solution.py:57
  14.6 2.7 %collective-permute-start.3 = (bf16[2,1024,128]{2,1,0:T(8,128)(2,1)}, bf16[2,1024,128]{2,1,0:T(8,128)(2,1)S(1)}, u32[]{:S(2)}, u32[]{:S(2)}) collective-permute-start(bf16[2,1024,128]{2,1,0:T(8,128)(2,1)} %collective-permute-done.1.refs_3_), channel_id=1, source_target_pairs={{0,8},{1,7},{2,4},{3,11},{4,6},{5,3},{6,0},{7,5},{8,14},{9,1},{10,... | collective-permute-start | bytes 1572872 | tf_op jit(solution)/shard_map/ppermute | solution.py:57
  17.3 2.2 %collective-permute-done.refs_2_ = bf16[2,1024,128]{2,1,0:T(8,128)(2,1)} collective-permute-done((bf16[2,1024,128]{2,1,0:T(8,128)(2,1)S(1)}, bf16[2,1024,128]{2,1,0:T(8,128)(2,1)}, u32[]{:S(2)}, u32[]{:S(2)}) %collective-permute-start) | collective-permute-done | bytes 524320 | tf_op jit(solution)/shard_map/ppermute | solution.py:57
  19.5 3.4 %collective-permute-start.2 = (bf16[2,1024,128]{2,1,0:T(8,128)(2,1)}, bf16[2,1024,128]{2,1,0:T(8,128)(2,1)S(1)}, u32[]{:S(2)}, u32[]{:S(2)}) collective-permute-start(bf16[2,1024,128]{2,1,0:T(8,128)(2,1)} %collective-permute-done.refs_2_), channel_id=1, source_target_pairs={{0,8},{1,7},{2,4},{3,11},{4,6},{5,3},{6,0},{7,5},{8,14},{9,1},{10,... | collective-permute-start | bytes 1572872 | tf_op jit(solution)/shard_map/ppermute | solution.py:57
  22.9 2.3 %collective-permute-start.16 = (bf16[256,1024]{1,0:T(8,128)(2,1)S(1)}, bf16[256,1024]{1,0:T(8,128)(2,1)S(1)}, u32[]{:S(2)}, u32[]{:S(2)}) collective-permute-start(bf16[256,1024]{1,0:T(8,128)(2,1)S(1)} %collective-permute-done.14.refs_14_.refs_18_), channel_id=1, source_target_pairs={{0,16},{1,49},{2,18},{3,51},{4,68},{5,53},{6,70},{7,55},{8,24},{9,... | collective-permute-start | bytes 1572872 | tf_op jit(solution)/shard_map/ppermute | solution.py:57
  25.2 3.1 %collective-permute-start.17 = (bf16[256,1024]{1,0:T(8,128)(2,1)S(1)}, bf16[256,1024]{1,0:T(8,128)(2,1)S(1)}, u32[]{:S(2)}, u32[]{:S(2)}) collective-permute-start(bf16[256,1024]{1,0:T(8,128)(2,1)S(1)} %collective-permute-done.15.refs_15_.refs_19_), channel_id=1, source_target_pairs={{0,16},{1,49},{2,18},{3,51},{4,68},{5,53},{6,70},{7,55},{8,24},{9,... | collective-permute-start | bytes 1572872 | tf_op jit(solution)/shard_map/ppermute | solution.py:57
  28.4 2.5 %collective-permute-done.2.refs_4_ = bf16[2,1024,128]{2,1,0:T(8,128)(2,1)S(1)} collective-permute-done((bf16[2,1024,128]{2,1,0:T(8,128)(2,1)}, bf16[2,1024,128]{2,1,0:T(8,128)(2,1)S(1)}, u32[]{:S(2)}, u32[]{:S(2)}) %collective-permute-start.2) | collective-permute-done | bytes 524320 | tf_op jit(solution)/shard_map/ppermute | solution.py:57
  30.9 3.3 %collective-permute-start.4 = (bf16[2,1024,128]{2,1,0:T(8,128)(2,1)S(1)}, bf16[2,1024,128]{2,1,0:T(8,128)(2,1)S(1)}, u32[]{:S(2)}, u32[]{:S(2)}) collective-permute-start(bf16[2,1024,128]{2,1,0:T(8,128)(2,1)S(1)} %collective-permute-done.2.refs_4_), channel_id=1, source_target_pairs={{0,8},{1,7},{2,4},{3,11},{4,6},{5,3},{6,0},{7,5},{8,14},{9,1},{10,... | collective-permute-start | bytes 1572872 | tf_op jit(solution)/shard_map/ppermute | solution.py:57
  34.2 2.2 %collective-permute-start.18 = (bf16[256,1024]{1,0:T(8,128)(2,1)S(1)}, bf16[256,1024]{1,0:T(8,128)(2,1)S(1)}, u32[]{:S(2)}, u32[]{:S(2)}) collective-permute-start(bf16[256,1024]{1,0:T(8,128)(2,1)S(1)} %collective-permute-done.16.refs_16_.refs_20_), channel_id=1, source_target_pairs={{0,16},{1,49},{2,18},{3,51},{4,68},{5,53},{6,70},{7,55},{8,24},{9,... | collective-permute-start | bytes 1572872 | tf_op jit(solution)/shard_map/ppermute | solution.py:57
  37.0 3.4 %collective-permute-start.19 = (bf16[256,1024]{1,0:T(8,128)(2,1)S(1)}, bf16[256,1024]{1,0:T(8,128)(2,1)S(1)}, u32[]{:S(2)}, u32[]{:S(2)}) collective-permute-start(bf16[256,1024]{1,0:T(8,128)(2,1)S(1)} %collective-permute-done.17.refs_17_.refs_21_), channel_id=1, source_target_pairs={{0,16},{1,49},{2,18},{3,51},{4,68},{5,53},{6,70},{7,55},{8,24},{9,... | collective-permute-start | bytes 1572872 | tf_op jit(solution)/shard_map/ppermute | solution.py:57
  40.5 1.8 %collective-permute-done.4.refs_6_ = bf16[2,1024,128]{2,1,0:T(8,128)(2,1)S(1)} collective-permute-done((bf16[2,1024,128]{2,1,0:T(8,128)(2,1)S(1)}, bf16[2,1024,128]{2,1,0:T(8,128)(2,1)S(1)}, u32[]{:S(2)}, u32[]{:S(2)}) %collective-permute-start.4) | collective-permute-done | bytes 524320 | tf_op jit(solution)/shard_map/ppermute | solution.py:57
  42.3 3.1 %collective-permute-start.6 = (bf16[2,1024,128]{2,1,0:T(8,128)(2,1)S(1)}, bf16[2,1024,128]{2,1,0:T(8,128)(2,1)S(1)}, u32[]{:S(2)}, u32[]{:S(2)}) collective-permute-start(bf16[2,1024,128]{2,1,0:T(8,128)(2,1)S(1)} %collective-permute-done.4.refs_6_), channel_id=1, source_target_pairs={{0,8},{1,7},{2,4},{3,11},{4,6},{5,3},{6,0},{7,5},{8,14},{9,1},{10,... | collective-permute-start | bytes 1572872 | tf_op jit(solution)/shard_map/ppermute | solution.py:57
  45.4 2.2 %collective-permute-start.20 = (bf16[256,1024]{1,0:T(8,128)(2,1)S(1)}, bf16[256,1024]{1,0:T(8,128)(2,1)S(1)}, u32[]{:S(2)}, u32[]{:S(2)}) collective-permute-start(bf16[256,1024]{1,0:T(8,128)(2,1)S(1)} %collective-permute-done.18.refs_18_.refs_22_), channel_id=1, source_target_pairs={{0,16},{1,49},{2,18},{3,51},{4,68},{5,53},{6,70},{7,55},{8,24},{9,... | collective-permute-start | bytes 1572872 | tf_op jit(solution)/shard_map/ppermute | solution.py:57
  48.2 3.4 %collective-permute-start.21 = (bf16[256,1024]{1,0:T(8,128)(2,1)S(1)}, bf16[256,1024]{1,0:T(8,128)(2,1)S(1)}, u32[]{:S(2)}, u32[]{:S(2)}) collective-permute-start(bf16[256,1024]{1,0:T(8,128)(2,1)S(1)} %collective-permute-done.19.refs_19_.refs_23_), channel_id=1, source_target_pairs={{0,16},{1,49},{2,18},{3,51},{4,68},{5,53},{6,70},{7,55},{8,24},{9,... | collective-permute-start | bytes 1572872 | tf_op jit(solution)/shard_map/ppermute | solution.py:57
  51.7 2.6 %collective-permute-done.6.refs_8_ = bf16[2,1024,128]{2,1,0:T(8,128)(2,1)S(1)} collective-permute-done((bf16[2,1024,128]{2,1,0:T(8,128)(2,1)S(1)}, bf16[2,1024,128]{2,1,0:T(8,128)(2,1)S(1)}, u32[]{:S(2)}, u32[]{:S(2)}) %collective-permute-start.6) | collective-permute-done | bytes 524320 | tf_op jit(solution)/shard_map/ppermute | solution.py:57
  54.3 2.3 %collective-permute-start.8 = (bf16[2,1024,128]{2,1,0:T(8,128)(2,1)S(1)}, bf16[2,1024,128]{2,1,0:T(8,128)(2,1)}, u32[]{:S(2)}, u32[]{:S(2)}) collective-permute-start(bf16[2,1024,128]{2,1,0:T(8,128)(2,1)S(1)} %collective-permute-done.6.refs_8_), channel_id=1, source_target_pairs={{0,8},{1,7},{2,4},{3,11},{4,6},{5,3},{6,0},{7,5},{8,14},{9,1},{10,... | collective-permute-start | bytes 1572872 | tf_op jit(solution)/shard_map/ppermute | solution.py:57
  56.7 2.2 %collective-permute-start.22 = (bf16[256,1024]{1,0:T(8,128)(2,1)S(1)}, bf16[256,1024]{1,0:T(8,128)(2,1)}, u32[]{:S(2)}, u32[]{:S(2)}) collective-permute-start(bf16[256,1024]{1,0:T(8,128)(2,1)S(1)} %collective-permute-done.20.refs_20_.refs_24_), channel_id=1, source_target_pairs={{0,16},{1,49},{2,18},{3,51},{4,68},{5,53},{6,70},{7,55},{8,24},{9,... | collective-permute-start | bytes 1572872 | tf_op jit(solution)/shard_map/ppermute | solution.py:57
  59.5 3.5 %collective-permute-start.23 = (bf16[256,1024]{1,0:T(8,128)(2,1)S(1)}, bf16[256,1024]{1,0:T(8,128)(2,1)}, u32[]{:S(2)}, u32[]{:S(2)}) collective-permute-start(bf16[256,1024]{1,0:T(8,128)(2,1)S(1)} %collective-permute-done.21.refs_21_.refs_25_), channel_id=1, source_target_pairs={{0,16},{1,49},{2,18},{3,51},{4,68},{5,53},{6,70},{7,55},{8,24},{9,... | collective-permute-start | bytes 1572872 | tf_op jit(solution)/shard_map/ppermute | solution.py:57
  63.1 2.6 %collective-permute-done.8.refs_10_ = bf16[2,1024,128]{2,1,0:T(8,128)(2,1)} collective-permute-done((bf16[2,1024,128]{2,1,0:T(8,128)(2,1)S(1)}, bf16[2,1024,128]{2,1,0:T(8,128)(2,1)}, u32[]{:S(2)}, u32[]{:S(2)}) %collective-permute-start.8) | collective-permute-done | bytes 524320 | tf_op jit(solution)/shard_map/ppermute | solution.py:57
  65.7 2.3 %collective-permute-start.10 = (bf16[2,1024,128]{2,1,0:T(8,128)(2,1)}, bf16[2,1024,128]{2,1,0:T(8,128)(2,1)S(1)}, u32[]{:S(2)}, u32[]{:S(2)}) collective-permute-start(bf16[2,1024,128]{2,1,0:T(8,128)(2,1)} %collective-permute-done.8.refs_10_), channel_id=1, source_target_pairs={{0,8},{1,7},{2,4},{3,11},{4,6},{5,3},{6,0},{7,5},{8,14},{9,1},{10,... | collective-permute-start | bytes 1572872 | tf_op jit(solution)/shard_map/ppermute | solution.py:57
  68.0 2.2 %collective-permute-start.24 = (bf16[256,1024]{1,0:T(8,128)(2,1)}, bf16[256,1024]{1,0:T(8,128)(2,1)S(1)}, u32[]{:S(2)}, u32[]{:S(2)}) collective-permute-start(bf16[256,1024]{1,0:T(8,128)(2,1)} %collective-permute-done.22.refs_22_.refs_26_), channel_id=1, source_target_pairs={{0,16},{1,49},{2,18},{3,51},{4,68},{5,53},{6,70},{7,55},{8,24},{9,... | collective-permute-start | bytes 1572872 | tf_op jit(solution)/shard_map/ppermute | solution.py:57
  70.8 3.5 %collective-permute-start.25 = (bf16[256,1024]{1,0:T(8,128)(2,1)}, bf16[256,1024]{1,0:T(8,128)(2,1)S(1)}, u32[]{:S(2)}, u32[]{:S(2)}) collective-permute-start(bf16[256,1024]{1,0:T(8,128)(2,1)} %collective-permute-done.23.refs_23_.refs_27_), channel_id=1, source_target_pairs={{0,16},{1,49},{2,18},{3,51},{4,68},{5,53},{6,70},{7,55},{8,24},{9,... | collective-permute-start | bytes 1572872 | tf_op jit(solution)/shard_map/ppermute | solution.py:57
  74.7 2.5 %collective-permute-done.10.refs_12_ = bf16[2,1024,128]{2,1,0:T(8,128)(2,1)S(1)} collective-permute-done((bf16[2,1024,128]{2,1,0:T(8,128)(2,1)}, bf16[2,1024,128]{2,1,0:T(8,128)(2,1)S(1)}, u32[]{:S(2)}, u32[]{:S(2)}) %collective-permute-start.10) | collective-permute-done | bytes 524320 | tf_op jit(solution)/shard_map/ppermute | solution.py:57
  77.2 1.9 %collective-permute-start.12 = (bf16[2,1024,128]{2,1,0:T(8,128)(2,1)S(1)}, bf16[2,1024,128]{2,1,0:T(8,128)(2,1)S(1)}, u32[]{:S(2)}, u32[]{:S(2)}) collective-permute-start(bf16[2,1024,128]{2,1,0:T(8,128)(2,1)S(1)} %collective-permute-done.10.refs_12_), channel_id=1, source_target_pairs={{0,8},{1,7},{2,4},{3,11},{4,6},{5,3},{6,0},{7,5},{8,14},{9,1},{10,... | collective-permute-start | bytes 1572872 | tf_op jit(solution)/shard_map/ppermute | solution.py:57
  79.1 2.4 %collective-permute-start.26 = (bf16[256,1024]{1,0:T(8,128)(2,1)S(1)}, bf16[256,1024]{1,0:T(8,128)(2,1)S(1)}, u32[]{:S(2)}, u32[]{:S(2)}) collective-permute-start(bf16[256,1024]{1,0:T(8,128)(2,1)S(1)} %collective-permute-done.24.refs_28_), channel_id=1, source_target_pairs={{0,16},{1,49},{2,18},{3,51},{4,68},{5,53},{6,70},{7,55},{8,24},{9,... | collective-permute-start | bytes 1572872 | tf_op jit(solution)/shard_map/ppermute | solution.py:57
  82.2 3.3 %collective-permute-start.27 = (bf16[256,1024]{1,0:T(8,128)(2,1)S(1)}, bf16[256,1024]{1,0:T(8,128)(2,1)S(1)}, u32[]{:S(2)}, u32[]{:S(2)}) collective-permute-start(bf16[256,1024]{1,0:T(8,128)(2,1)S(1)} %collective-permute-done.25.refs_29_), channel_id=1, source_target_pairs={{0,16},{1,49},{2,18},{3,51},{4,68},{5,53},{6,70},{7,55},{8,24},{9,... | collective-permute-start | bytes 1572872 | tf_op jit(solution)/shard_map/ppermute | solution.py:57
  85.5 11.3 %early_part.1.refs_33_.acc_ref = f32[1024,1024]{1,0:T(8,128)S(1)} custom-call(s32[3]{0:T(128)S(1)} %pad_add_fusion.where, bf16[2,1024,128]{2,1,0:T(8,128)(2,1)} %copy-done.7, bf16[2,1024,128]{2,1,0:T(8,128)(2,1)} %copy-done.6, bf16[2,1024,128]{2,1,0:T(8,128)(2,1)} %collective-permute-done.refs_2_, bf16[2,1024,128]{2,1,0:T(8,128)(2,1)} %collective-permute-done.1.refs_3_, ...), custom_call_target="tpu_custom_call" | custom-call | flops 6039797760 | bytes 9437184 | tf_op jit(solution)/shard_map/early_part/pallas_call | solution.py:254
  96.9 5.7 %last_part.1 = (f32[512,1024]{1,0:T(8,128)S(1)}, bf16[1024,1792]{1,0:T(8,128)(2,1)S(1)}, bf16[1792,1024]{1,0:T(8,128)(2,1)S(1)}) custom-call(s32[3]{0:T(128)S(1)} %pad_add_fusion.where, bf16[2,1024,128]{2,1,0:T(8,128)(2,1)} %copy-done.7, bf16[2,1024,128]{2,1,0:T(8,128)(2,1)} %copy-done.6, bf16[2,1024,128]{2,1,0:T(8,128)(2,1)} %collective-permute-done.refs_2_, ...), custom_call_target="tpu_custom_call" | custom-call | flops 2348810240 | bytes 7340032 | tf_op jit(solution)/shard_map/last_part/pallas_call | solution.py:273
  102.9 3.7 %rest_of_part.1.own_ref = f32[512,1024]{1,0:T(8,128)S(1)} custom-call(s32[3]{0:T(128)S(1)} %pad_add_fusion.where, bf16[1024,1792]{1,0:T(8,128)(2,1)S(1)} %get-tuple-element.8.a_all, bf16[1792,1024]{1,0:T(8,128)(2,1)S(1)} %get-tuple-element.9.b_all, bf16[1024,128]{1,0:T(8,128)(2,1)S(1)} %bitcast.48, f32[1024,1024]{1,0:T(8,128)S(1)} %early_part.1.refs_33_.acc_ref), custom_call_target="tpu_custom_call" | custom-call | flops 2348810240 | bytes 7340032 | tf_op jit(solution)/shard_map/rest_of_part/pallas_call | solution.py:293
  107.0 2.5 %update.1 = f32[1,8,512,128]{3,2,1,0:T(8,128)} custom-call(s32[3]{0:T(128)S(1)} %pad_add_fusion.where, s32[8,8]{1,0:T(8,128)S(1)} %bitcast.50, f32[8]{0:T(128)S(1)} %copy-done.3, f32[8,128]{1,0:T(8,128)S(1)} %bitcast.51, f32[512,1024]{1,0:T(8,128)S(1)} %rest_of_part.1.own_ref, f32[512,1024]{1,0:T(8,128)S(1)} %collective-permute-done.28.other_ref, ...), custom_call_target="tpu_custom_call" | custom-call | tf_op jit(solution)/shard_map/update/pallas_call | solution.py:331
  (92 shorter events, 8.1 us)
Async XLA Ops:
  3.1 11.5 %collective-permute-start.1 = (bf16[2,1024,128]{2,1,0:T(8,128)(2,1)S(1)}, bf16[2,1024,128]{2,1,0:T(8,128)(2,1)}, u32[]{:S(2)}, u32[]{:S(2)}) collective-permute-start(bf16[2,1024,128]{2,1,0:T(8,128)(2,1)S(1)} %get-tuple-element.13.refs_1_), channel_id=1, source_target_pairs={{0,8},{1,7},{2,4},{3,11},{4,6},{5,3},{6,0},{7,5},{8,14},{9,1},{10,... | collective-permute-start | bytes 1572872 | tf_op jit(solution)/shard_map/ppermute | solution.py:57
  7.8 11.7 %collective-permute-start = (bf16[2,1024,128]{2,1,0:T(8,128)(2,1)S(1)}, bf16[2,1024,128]{2,1,0:T(8,128)(2,1)}, u32[]{:S(2)}, u32[]{:S(2)}) collective-permute-start(bf16[2,1024,128]{2,1,0:T(8,128)(2,1)S(1)} %get-tuple-element.14.refs_0_), channel_id=1, source_target_pairs={{0,8},{1,7},{2,4},{3,11},{4,6},{5,3},{6,0},{7,5},{8,14},{9,1},{10,... | collective-permute-start | bytes 1572872 | tf_op jit(solution)/shard_map/ppermute | solution.py:57
  8.0 66.3 %copy-start.23 = (bf16[128,1024]{1,0:T(8,128)(2,1)S(1)}, bf16[128,1024]{1,0:T(8,128)(2,1)}, u32[]{:S(2)}) copy-start(bf16[128,1024]{1,0:T(8,128)(2,1)} %param.9) | copy-start | bytes 786436
  8.1 77.4 %copy-start.4 = (bf16[32,8,8,128]{3,1,2,0:T(8,128)(2,1)}, bf16[32,8,8,128]{3,1,2,0:T(8,128)(2,1)S(1)}, u32[]{:S(2)}) copy-start(bf16[32,8,8,128]{3,1,2,0:T(8,128)(2,1)S(1)} %copy.37) | copy-start | bytes 1572868
  8.1 14.8 %collective-permute-start.14 = (bf16[256,1024]{1,0:T(8,128)(2,1)S(1)}, bf16[256,1024]{1,0:T(8,128)(2,1)S(1)}, u32[]{:S(2)}, u32[]{:S(2)}) collective-permute-start(bf16[256,1024]{1,0:T(8,128)(2,1)S(1)} %bitcast.52), channel_id=1, source_target_pairs={{0,16},{1,49},{2,18},{3,51},{4,68},{5,53},{6,70},{7,55},{8,24},{9,... | collective-permute-start | bytes 1572872 | tf_op jit(solution)/shard_map/ppermute | solution.py:57
  11.9 51.0 %copy-start.5 = (bf16[32,8,8,128]{3,1,2,0:T(8,128)(2,1)}, bf16[32,8,8,128]{3,1,2,0:T(8,128)(2,1)S(1)}, u32[]{:S(2)}) copy-start(bf16[32,8,8,128]{3,1,2,0:T(8,128)(2,1)S(1)} %copy.36) | copy-start | bytes 1572868
  12.0 13.3 %collective-permute-start.15 = (bf16[256,1024]{1,0:T(8,128)(2,1)S(1)}, bf16[256,1024]{1,0:T(8,128)(2,1)S(1)}, u32[]{:S(2)}, u32[]{:S(2)}) collective-permute-start(bf16[256,1024]{1,0:T(8,128)(2,1)S(1)} %bitcast.55), channel_id=1, source_target_pairs={{0,16},{1,49},{2,18},{3,51},{4,68},{5,53},{6,70},{7,55},{8,24},{9,... | collective-permute-start | bytes 1572872 | tf_op jit(solution)/shard_map/ppermute | solution.py:57
  14.6 13.7 %collective-permute-start.3 = (bf16[2,1024,128]{2,1,0:T(8,128)(2,1)}, bf16[2,1024,128]{2,1,0:T(8,128)(2,1)S(1)}, u32[]{:S(2)}, u32[]{:S(2)}) collective-permute-start(bf16[2,1024,128]{2,1,0:T(8,128)(2,1)} %collective-permute-done.1.refs_3_), channel_id=1, source_target_pairs={{0,8},{1,7},{2,4},{3,11},{4,6},{5,3},{6,0},{7,5},{8,14},{9,1},{10,... | collective-permute-start | bytes 1572872 | tf_op jit(solution)/shard_map/ppermute | solution.py:57
  19.5 11.3 %collective-permute-start.2 = (bf16[2,1024,128]{2,1,0:T(8,128)(2,1)}, bf16[2,1024,128]{2,1,0:T(8,128)(2,1)S(1)}, u32[]{:S(2)}, u32[]{:S(2)}) collective-permute-start(bf16[2,1024,128]{2,1,0:T(8,128)(2,1)} %collective-permute-done.refs_2_), channel_id=1, source_target_pairs={{0,8},{1,7},{2,4},{3,11},{4,6},{5,3},{6,0},{7,5},{8,14},{9,1},{10,... | collective-permute-start | bytes 1572872 | tf_op jit(solution)/shard_map/ppermute | solution.py:57
  22.9 11.2 %collective-permute-start.16 = (bf16[256,1024]{1,0:T(8,128)(2,1)S(1)}, bf16[256,1024]{1,0:T(8,128)(2,1)S(1)}, u32[]{:S(2)}, u32[]{:S(2)}) collective-permute-start(bf16[256,1024]{1,0:T(8,128)(2,1)S(1)} %collective-permute-done.14.refs_14_.refs_18_), channel_id=1, source_target_pairs={{0,16},{1,49},{2,18},{3,51},{4,68},{5,53},{6,70},{7,55},{8,24},{9,... | collective-permute-start | bytes 1572872 | tf_op jit(solution)/shard_map/ppermute | solution.py:57
  25.2 11.7 %collective-permute-start.17 = (bf16[256,1024]{1,0:T(8,128)(2,1)S(1)}, bf16[256,1024]{1,0:T(8,128)(2,1)S(1)}, u32[]{:S(2)}, u32[]{:S(2)}) collective-permute-start(bf16[256,1024]{1,0:T(8,128)(2,1)S(1)} %collective-permute-done.15.refs_15_.refs_19_), channel_id=1, source_target_pairs={{0,16},{1,49},{2,18},{3,51},{4,68},{5,53},{6,70},{7,55},{8,24},{9,... | collective-permute-start | bytes 1572872 | tf_op jit(solution)/shard_map/ppermute | solution.py:57
  28.3 12.0 %collective-permute-start.5 = (bf16[2,1024,128]{2,1,0:T(8,128)(2,1)S(1)}, bf16[2,1024,128]{2,1,0:T(8,128)(2,1)S(1)}, u32[]{:S(2)}, u32[]{:S(2)}) collective-permute-start(bf16[2,1024,128]{2,1,0:T(8,128)(2,1)S(1)} %collective-permute-done.3.refs_5_), channel_id=1, source_target_pairs={{0,8},{1,7},{2,4},{3,11},{4,6},{5,3},{6,0},{7,5},{8,14},{9,1},{10,... | collective-permute-start | bytes 1572872 | tf_op jit(solution)/shard_map/ppermute | solution.py:57
  30.9 11.4 %collective-permute-start.4 = (bf16[2,1024,128]{2,1,0:T(8,128)(2,1)S(1)}, bf16[2,1024,128]{2,1,0:T(8,128)(2,1)S(1)}, u32[]{:S(2)}, u32[]{:S(2)}) collective-permute-start(bf16[2,1024,128]{2,1,0:T(8,128)(2,1)S(1)} %collective-permute-done.2.refs_4_), channel_id=1, source_target_pairs={{0,8},{1,7},{2,4},{3,11},{4,6},{5,3},{6,0},{7,5},{8,14},{9,1},{10,... | collective-permute-start | bytes 1572872 | tf_op jit(solution)/shard_map/ppermute | solution.py:57
  34.2 11.2 %collective-permute-start.18 = (bf16[256,1024]{1,0:T(8,128)(2,1)S(1)}, bf16[256,1024]{1,0:T(8,128)(2,1)S(1)}, u32[]{:S(2)}, u32[]{:S(2)}) collective-permute-start(bf16[256,1024]{1,0:T(8,128)(2,1)S(1)} %collective-permute-done.16.refs_16_.refs_20_), channel_id=1, source_target_pairs={{0,16},{1,49},{2,18},{3,51},{4,68},{5,53},{6,70},{7,55},{8,24},{9,... | collective-permute-start | bytes 1572872 | tf_op jit(solution)/shard_map/ppermute | solution.py:57
  37.0 11.2 %collective-permute-start.19 = (bf16[256,1024]{1,0:T(8,128)(2,1)S(1)}, bf16[256,1024]{1,0:T(8,128)(2,1)S(1)}, u32[]{:S(2)}, u32[]{:S(2)}) collective-permute-start(bf16[256,1024]{1,0:T(8,128)(2,1)S(1)} %collective-permute-done.17.refs_17_.refs_21_), channel_id=1, source_target_pairs={{0,16},{1,49},{2,18},{3,51},{4,68},{5,53},{6,70},{7,55},{8,24},{9,... | collective-permute-start | bytes 1572872 | tf_op jit(solution)/shard_map/ppermute | solution.py:57
  40.4 11.2 %collective-permute-start.7 = (bf16[2,1024,128]{2,1,0:T(8,128)(2,1)S(1)}, bf16[2,1024,128]{2,1,0:T(8,128)(2,1)S(1)}, u32[]{:S(2)}, u32[]{:S(2)}) collective-permute-start(bf16[2,1024,128]{2,1,0:T(8,128)(2,1)S(1)} %collective-permute-done.5.refs_7_), channel_id=1, source_target_pairs={{0,8},{1,7},{2,4},{3,11},{4,6},{5,3},{6,0},{7,5},{8,14},{9,1},{10,... | collective-permute-start | bytes 1572872 | tf_op jit(solution)/shard_map/ppermute | solution.py:57
  42.3 12.0 %collective-permute-start.6 = (bf16[2,1024,128]{2,1,0:T(8,128)(2,1)S(1)}, bf16[2,1024,128]{2,1,0:T(8,128)(2,1)S(1)}, u32[]{:S(2)}, u32[]{:S(2)}) collective-permute-start(bf16[2,1024,128]{2,1,0:T(8,128)(2,1)S(1)} %collective-permute-done.4.refs_6_), channel_id=1, source_target_pairs={{0,8},{1,7},{2,4},{3,11},{4,6},{5,3},{6,0},{7,5},{8,14},{9,1},{10,... | collective-permute-start | bytes 1572872 | tf_op jit(solution)/shard_map/ppermute | solution.py:57
  45.4 11.2 %collective-permute-start.20 = (bf16[256,1024]{1,0:T(8,128)(2,1)S(1)}, bf16[256,1024]{1,0:T(8,128)(2,1)S(1)}, u32[]{:S(2)}, u32[]{:S(2)}) collective-permute-start(bf16[256,1024]{1,0:T(8,128)(2,1)S(1)} %collective-permute-done.18.refs_18_.refs_22_), channel_id=1, source_target_pairs={{0,16},{1,49},{2,18},{3,51},{4,68},{5,53},{6,70},{7,55},{8,24},{9,... | collective-permute-start | bytes 1572872 | tf_op jit(solution)/shard_map/ppermute | solution.py:57
  48.2 11.3 %collective-permute-start.21 = (bf16[256,1024]{1,0:T(8,128)(2,1)S(1)}, bf16[256,1024]{1,0:T(8,128)(2,1)S(1)}, u32[]{:S(2)}, u32[]{:S(2)}) collective-permute-start(bf16[256,1024]{1,0:T(8,128)(2,1)S(1)} %collective-permute-done.19.refs_19_.refs_23_), channel_id=1, source_target_pairs={{0,16},{1,49},{2,18},{3,51},{4,68},{5,53},{6,70},{7,55},{8,24},{9,... | collective-permute-start | bytes 1572872 | tf_op jit(solution)/shard_map/ppermute | solution.py:57
  51.6 11.3 %collective-permute-start.9 = (bf16[2,1024,128]{2,1,0:T(8,128)(2,1)S(1)}, bf16[2,1024,128]{2,1,0:T(8,128)(2,1)}, u32[]{:S(2)}, u32[]{:S(2)}) collective-permute-start(bf16[2,1024,128]{2,1,0:T(8,128)(2,1)S(1)} %collective-permute-done.7.refs_9_), channel_id=1, source_target_pairs={{0,8},{1,7},{2,4},{3,11},{4,6},{5,3},{6,0},{7,5},{8,14},{9,1},{10,... | collective-permute-start | bytes 1572872 | tf_op jit(solution)/shard_map/ppermute | solution.py:57
  54.3 11.3 %collective-permute-start.8 = (bf16[2,1024,128]{2,1,0:T(8,128)(2,1)S(1)}, bf16[2,1024,128]{2,1,0:T(8,128)(2,1)}, u32[]{:S(2)}, u32[]{:S(2)}) collective-permute-start(bf16[2,1024,128]{2,1,0:T(8,128)(2,1)S(1)} %collective-permute-done.6.refs_8_), channel_id=1, source_target_pairs={{0,8},{1,7},{2,4},{3,11},{4,6},{5,3},{6,0},{7,5},{8,14},{9,1},{10,... | collective-permute-start | bytes 1572872 | tf_op jit(solution)/shard_map/ppermute | solution.py:57
  56.7 11.3 %collective-permute-start.22 = (bf16[256,1024]{1,0:T(8,128)(2,1)S(1)}, bf16[256,1024]{1,0:T(8,128)(2,1)}, u32[]{:S(2)}, u32[]{:S(2)}) collective-permute-start(bf16[256,1024]{1,0:T(8,128)(2,1)S(1)} %collective-permute-done.20.refs_20_.refs_24_), channel_id=1, source_target_pairs={{0,16},{1,49},{2,18},{3,51},{4,68},{5,53},{6,70},{7,55},{8,24},{9,... | collective-permute-start | bytes 1572872 | tf_op jit(solution)/shard_map/ppermute | solution.py:57
  59.5 11.2 %collective-permute-start.23 = (bf16[256,1024]{1,0:T(8,128)(2,1)S(1)}, bf16[256,1024]{1,0:T(8,128)(2,1)}, u32[]{:S(2)}, u32[]{:S(2)}) collective-permute-start(bf16[256,1024]{1,0:T(8,128)(2,1)S(1)} %collective-permute-done.21.refs_21_.refs_25_), channel_id=1, source_target_pairs={{0,16},{1,49},{2,18},{3,51},{4,68},{5,53},{6,70},{7,55},{8,24},{9,... | collective-permute-start | bytes 1572872 | tf_op jit(solution)/shard_map/ppermute | solution.py:57
  63.0 11.5 %collective-permute-start.11 = (bf16[2,1024,128]{2,1,0:T(8,128)(2,1)}, bf16[2,1024,128]{2,1,0:T(8,128)(2,1)S(1)}, u32[]{:S(2)}, u32[]{:S(2)}) collective-permute-start(bf16[2,1024,128]{2,1,0:T(8,128)(2,1)} %collective-permute-done.9.refs_11_), channel_id=1, source_target_pairs={{0,8},{1,7},{2,4},{3,11},{4,6},{5,3},{6,0},{7,5},{8,14},{9,1},{10,... | collective-permute-start | bytes 1572872 | tf_op jit(solution)/shard_map/ppermute | solution.py:57
  65.7 11.5 %collective-permute-start.10 = (bf16[2,1024,128]{2,1,0:T(8,128)(2,1)}, bf16[2,1024,128]{2,1,0:T(8,128)(2,1)S(1)}, u32[]{:S(2)}, u32[]{:S(2)}) collective-permute-start(bf16[2,1024,128]{2,1,0:T(8,128)(2,1)} %collective-permute-done.8.refs_10_), channel_id=1, source_target_pairs={{0,8},{1,7},{2,4},{3,11},{4,6},{5,3},{6,0},{7,5},{8,14},{9,1},{10,... | collective-permute-start | bytes 1572872 | tf_op jit(solution)/shard_map/ppermute | solution.py:57
  68.0 11.1 %collective-permute-start.24 = (bf16[256,1024]{1,0:T(8,128)(2,1)}, bf16[256,1024]{1,0:T(8,128)(2,1)S(1)}, u32[]{:S(2)}, u32[]{:S(2)}) collective-permute-start(bf16[256,1024]{1,0:T(8,128)(2,1)} %collective-permute-done.22.refs_22_.refs_26_), channel_id=1, source_target_pairs={{0,16},{1,49},{2,18},{3,51},{4,68},{5,53},{6,70},{7,55},{8,24},{9,... | collective-permute-start | bytes 1572872 | tf_op jit(solution)/shard_map/ppermute | solution.py:57
  70.8 11.4 %collective-permute-start.25 = (bf16[256,1024]{1,0:T(8,128)(2,1)}, bf16[256,1024]{1,0:T(8,128)(2,1)S(1)}, u32[]{:S(2)}, u32[]{:S(2)}) collective-permute-start(bf16[256,1024]{1,0:T(8,128)(2,1)} %collective-permute-done.23.refs_23_.refs_27_), channel_id=1, source_target_pairs={{0,16},{1,49},{2,18},{3,51},{4,68},{5,53},{6,70},{7,55},{8,24},{9,... | collective-permute-start | bytes 1572872 | tf_op jit(solution)/shard_map/ppermute | solution.py:57
  74.5 22.3 %collective-permute-start.13 = (bf16[2,1024,128]{2,1,0:T(8,128)(2,1)S(1)}, bf16[2,1024,128]{2,1,0:T(8,128)(2,1)S(1)}, u32[]{:S(2)}, u32[]{:S(2)}) collective-permute-start(bf16[2,1024,128]{2,1,0:T(8,128)(2,1)S(1)} %collective-permute-done.11.refs_13_), channel_id=1, source_target_pairs={{0,8},{1,7},{2,4},{3,11},{4,6},{5,3},{6,0},{7,5},{8,14},{9,1},{10,... | collective-permute-start | bytes 1572872 | tf_op jit(solution)/shard_map/ppermute | solution.py:57
  77.2 19.6 %collective-permute-start.12 = (bf16[2,1024,128]{2,1,0:T(8,128)(2,1)S(1)}, bf16[2,1024,128]{2,1,0:T(8,128)(2,1)S(1)}, u32[]{:S(2)}, u32[]{:S(2)}) collective-permute-start(bf16[2,1024,128]{2,1,0:T(8,128)(2,1)S(1)} %collective-permute-done.10.refs_12_), channel_id=1, source_target_pairs={{0,8},{1,7},{2,4},{3,11},{4,6},{5,3},{6,0},{7,5},{8,14},{9,1},{10,... | collective-permute-start | bytes 1572872 | tf_op jit(solution)/shard_map/ppermute | solution.py:57
  79.1 17.7 %collective-permute-start.26 = (bf16[256,1024]{1,0:T(8,128)(2,1)S(1)}, bf16[256,1024]{1,0:T(8,128)(2,1)S(1)}, u32[]{:S(2)}, u32[]{:S(2)}) collective-permute-start(bf16[256,1024]{1,0:T(8,128)(2,1)S(1)} %collective-permute-done.24.refs_28_), channel_id=1, source_target_pairs={{0,16},{1,49},{2,18},{3,51},{4,68},{5,53},{6,70},{7,55},{8,24},{9,... | collective-permute-start | bytes 1572872 | tf_op jit(solution)/shard_map/ppermute | solution.py:57
  82.2 14.6 %collective-permute-start.27 = (bf16[256,1024]{1,0:T(8,128)(2,1)S(1)}, bf16[256,1024]{1,0:T(8,128)(2,1)S(1)}, u32[]{:S(2)}, u32[]{:S(2)}) collective-permute-start(bf16[256,1024]{1,0:T(8,128)(2,1)S(1)} %collective-permute-done.25.refs_29_), channel_id=1, source_target_pairs={{0,16},{1,49},{2,18},{3,51},{4,68},{5,53},{6,70},{7,55},{8,24},{9,... | collective-permute-start | bytes 1572872 | tf_op jit(solution)/shard_map/ppermute | solution.py:57
  102.5 4.5 %collective-permute-start.28 = (f32[512,1024]{1,0:T(8,128)S(1)}, f32[512,1024]{1,0:T(8,128)S(1)}, u32[]{:S(2)}, u32[]{:S(2)}) collective-permute-start(f32[512,1024]{1,0:T(8,128)S(1)} %get-tuple-element.10), channel_id=1, source_target_pairs={{0,1},{1,0},{2,3},{3,2},{4,5},{5,4},{6,7},{7,6},{8,9},{9,8},{10,11... | collective-permute-start | bytes 6291464 | tf_op jit(solution)/shard_map/ppermute | solution.py:57
  (21 other events, 434.1 us)
